TPU v7x, 32 devices: a whole 2x2x4 slice. The times are simulated.
32 devices in a mesh: rows: 8 (over y, x, core), batch: 4 (over z).
Axes of the slice: x: 2, y: 2, z: 4, core: 2. Of those that a mesh axis runs over, the one named last changes fastest.
Arguments:
- bases: bfloat16 [24576, 1024], P('rows', 'batch'), may hold values from -30 to 30
- start: float32 [1024, 512], P('batch'), may hold values from -6 to 6
Outputs:
- modes: bfloat16 [24576, 512], P(('rows', 'batch'))
All inputs are finite; a program needn't handle non-finite values.
Results may differ from a plain program's by a relative error of at most 0.0041.
Values may be sent and summed in bfloat16 or wider, within the bound.
No kernel may reach another device: no remote copies, remote signals or barrier semaphores. Data moves between devices by JAX's collectives and lax.ppermute only.
A program may use at most 128 MiB of HBM per device.

v0:
```python
import jax
import jax.numpy as jnp
from jax import lax
from jax.sharding import PartitionSpec as P

ITERS = 2


def inner_cols(left, right):
    return lax.dot_general(
        left, right, (((0,), (0,)), ((), ())), preferred_element_type=jnp.float32
    )


def on_device(bases, start):
    basis_width = bases.shape[1]
    local_rows = bases.shape[0]
    group_count = lax.axis_size("batch")
    all_columns = basis_width * group_count
    sub_rows = local_rows // group_count
    energy = lax.psum(jnp.sum(jnp.square(bases.astype(jnp.float32))), ("rows", "batch"))
    diag_mean = energy / all_columns
    partial_value = inner_cols(bases, lax.all_gather(bases, "batch", axis=1, tiled=True))
    gram_rows = lax.psum(partial_value, "rows")
    q_own = start
    for iteration in range(ITERS):
        q_full = lax.all_gather(q_own, "batch", axis=0, tiled=True)
        lifted = jnp.dot(gram_rows, q_full, precision=lax.Precision.HIGHEST) / diag_mean + q_own
        local_correlation = lax.dot_general(
            lifted, lifted, (((0,), (0,)), ((), ())), precision=lax.Precision.HIGHEST
        )
        correlation = lax.psum(local_correlation, "batch")
        factor = jnp.linalg.cholesky(correlation)
        q_own = jax.scipy.linalg.solve_triangular(factor, lifted.T, lower=True).T
    q_low = q_own.astype(jnp.bfloat16)
    q_every = lax.all_gather(q_low, "batch", axis=0, tiled=True)
    stacked_rows = bases.reshape(group_count, sub_rows, basis_width)
    modes = jnp.dot(
        lax.all_to_all(stacked_rows, "batch", split_axis=0, concat_axis=2, tiled=True)[0],
        q_every,
        preferred_element_type=jnp.float32,
    )
    return modes.astype(jnp.bfloat16)


def solution(mesh):
    in_specs = (P("rows", "batch"), P("batch", None))
    out_specs = P(("rows", "batch"), None)
    return jax.shard_map(
        on_device, mesh=mesh, in_specs=in_specs, out_specs=out_specs, check_vma=False
    )
```

profile of v0, /device:TPU:0, one launch (start us, length us, event | category | flops | bytes accessed | tf_op | source)
XLA Modules:
  0.0 751.5 jit_solution(14153086746771359615)
XLA Ops:
  8.1 118.4 %all-gather.5.cloned.1.call-done = bf16[3072,1024]{1,0:T(8,128)(2,1)} async-done(((bf16[3072,256]{1,0:T(8,128)(2,1)}), bf16[3072,1024]{1,0:T(8,128)(2,1)}) %all-gather.5.cloned.1.call-update) | async-done | bytes 6291472 | tf_op jit(solution)/shard_map/all_gather | solution.py:23
  126.5 6.2 fusion.77
  132.7 3.0 multiply_reduce_fusion
  135.7 41.2 %psum.29 = f32[]{:T(128)} all-reduce(f32[]{:T(128)} %multiply_reduce_fusion), channel_id=1, replica_groups=mesh['rows'=8,'batch'=4] {'rows','batch'}, use_global_device_ids=true, to_apply=%region_2.0 | all-reduce | flops 1 | bytes 8 | tf_op jit(solution)/shard_map/psum | solution.py:21
  177.6 54.5 %all-reduce.5.cloned.1.call-done = f32[256,1024]{1,0:T(8,128)} async-done(((f32[256,1024]{1,0:T(8,128)}), f32[256,1024]{1,0:T(8,128)}) %all-reduce.5.cloned.1.call-update) | async-done | bytes 1048592 | tf_op jit(solution)/shard_map/psum | solution.py:24
  232.1 3.9 fusion.1
  235.9 2.1 fusion.78
  238.3 50.8 %all-reduce.7.cloned.1.call-done = f32[512,512]{0,1:T(8,128)} async-done(((f32[512,512]{0,1:T(8,128)}), f32[512,512]{0,1:T(8,128)}) %all-reduce.7.cloned.1.call-update) | async-done | bytes 1048592 | tf_op jit(solution)/shard_map/psum | solution.py:32
  289.1 1.6 copy.22
  291.0 1.0 copy-done.4
  292.0 11.7 %cholesky.286 = f32[128,128]{1,0:T(8,128)S(1)} custom-call(f32[128,128]{1,0:T(8,128)S(1)} %cholesky.426), custom_call_target="Cholesky" | custom-call | tf_op jit(solution)/shard_map/jit(cholesky)/cholesky | solution.py:33
  303.7 9.8 %custom-call.27 = f32[1,128,128]{1,2,0:T(8,128)S(1)} custom-call(f32[1,128,128]{2,1,0:T(8,128)S(1)} %get-tuple-element.62), custom_call_target="InvertDiagBlocksLowerTriangular" | custom-call | tf_op jit(solution)/shard_map/jit(cholesky)/cholesky | solution.py:33
  313.7 1.2 constant_dynamic-update-slice_fusion.5
  314.9 1.3 convolution_subtract_fusion.1
  316.2 11.7 %cholesky.305 = f32[128,128]{1,0:T(8,128)S(1)} custom-call(f32[128,128]{1,0:T(8,128)S(1)} %cholesky.430), custom_call_target="Cholesky" | custom-call | tf_op jit(solution)/shard_map/jit(cholesky)/cholesky | solution.py:33
  327.9 10.0 %custom-call.28 = f32[1,128,128]{1,2,0:T(8,128)S(1)} custom-call(f32[1,128,128]{2,1,0:T(8,128)S(1)} %get-tuple-element.59), custom_call_target="InvertDiagBlocksLowerTriangular" | custom-call | tf_op jit(solution)/shard_map/jit(cholesky)/cholesky | solution.py:33
  338.2 1.3 convolution_subtract_fusion.7
  339.5 11.7 %cholesky.326 = f32[128,128]{1,0:T(8,128)S(1)} custom-call(f32[128,128]{1,0:T(8,128)S(1)} %cholesky.435), custom_call_target="Cholesky" | custom-call | tf_op jit(solution)/shard_map/jit(cholesky)/cholesky | solution.py:33
  351.3 0.7 compare_reduce_fusion.5
  352.0 9.8 %custom-call.29 = f32[1,128,128]{1,2,0:T(8,128)S(1)} custom-call(f32[1,128,128]{2,1,0:T(8,128)S(1)} %get-tuple-element.56), custom_call_target="InvertDiagBlocksLowerTriangular" | custom-call | tf_op jit(solution)/shard_map/jit(cholesky)/cholesky | solution.py:33
  362.0 1.2 convolution_subtract_fusion.11
  363.2 11.7 %cholesky.343 = f32[128,128]{1,0:T(8,128)S(1)} custom-call(f32[128,128]{1,0:T(8,128)S(1)} %convolution_subtract_fusion.11), custom_call_target="Cholesky" | custom-call | tf_op jit(solution)/shard_map/jit(cholesky)/cholesky | solution.py:33
  379.4 8.1 %while.4 = (s32[]{:T(128)}, f32[512,512]{1,0:T(8,128)S(1)}, s32[4,2]{0,1:T(2,128)S(1)}, f32[4,128,128]{2,1,0:T(8,128)S(1)}, s32[]{:T(128)}) while((s32[]{:T(128)}, f32[512,512]{1,0:T(8,128)S(1)}, s32[4,2]{0,1:T(2,128)S(1)}, f32[4,128,128]{2,1,0:T(8,128)S(1)}, s32[]{:T(128)}) %tuple.52), condition=%wide.while_cond, body=%wide.while_body.sunk | while | flops 2 | bytes 131181 | solution.py:34
  380.1 1.3 bitcast_dynamic-update-slice_fusion.4
  382.1 1.3 bitcast_dynamic-update-slice_fusion.4
  384.2 1.3 bitcast_dynamic-update-slice_fusion.4
  386.2 1.3 bitcast_dynamic-update-slice_fusion.4
  387.6 39.3 %custom-call.30 = f32[4,128,128]{1,2,0:T(8,128)S(1)} custom-call(f32[4,128,128]{2,1,0:T(8,128)S(1)} %get-tuple-element.21), custom_call_target="InvertDiagBlocksLowerTriangular" | custom-call | tf_op jit(solution)/shard_map/jit(_solve_triangular)/triangular_solve | solution.py:34
  428.8 0.8 convolution_subtract_fusion.5
  430.2 0.8 fusion.16
  431.1 45.4 %all-gather.9.cloned.1.call-done = f32[1024,512]{1,0:T(8,128)} async-done(((f32[256,512]{1,0:T(8,128)}), f32[1024,512]{1,0:T(8,128)}) %all-gather.9.cloned.1.call-update) | async-done | bytes 2097168 | tf_op jit(solution)/shard_map/all_gather | solution.py:27
  476.6 3.5 bitcast_add_fusion.2
  480.1 2.1 fusion.4
  482.3 3.6 all-to-all-start
  486.1 73.1 %all-reduce.9.cloned.1.call-done = f32[512,512]{0,1:T(8,128)} async-done(((f32[512,512]{0,1:T(8,128)}), f32[512,512]{0,1:T(8,128)}) %all-reduce.9.cloned.1.call-update) | async-done | bytes 1048592 | tf_op jit(solution)/shard_map/psum | solution.py:32
  559.1 2.7 copy.31
  561.8 1.4 fusion.2
  563.3 1.0 copy-done.3
  564.3 11.7 %cholesky.358 = f32[128,128]{1,0:T(8,128)S(1)} custom-call(f32[128,128]{1,0:T(8,128)S(1)} %cholesky.439), custom_call_target="Cholesky" | custom-call | tf_op jit(solution)/shard_map/jit(cholesky)/cholesky | solution.py:33
  576.2 9.8 %custom-call.31 = f32[1,128,128]{1,2,0:T(8,128)S(1)} custom-call(f32[1,128,128]{2,1,0:T(8,128)S(1)} %get-tuple-element.52), custom_call_target="InvertDiagBlocksLowerTriangular" | custom-call | tf_op jit(solution)/shard_map/jit(cholesky)/cholesky | solution.py:33
  586.0 1.2 constant_dynamic-update-slice_fusion.3
  587.2 1.3 convolution_subtract_fusion
  588.5 11.7 %cholesky.377 = f32[128,128]{1,0:T(8,128)S(1)} custom-call(f32[128,128]{1,0:T(8,128)S(1)} %cholesky.443), custom_call_target="Cholesky" | custom-call | tf_op jit(solution)/shard_map/jit(cholesky)/cholesky | solution.py:33
  601.6 10.0 %custom-call.32 = f32[1,128,128]{1,2,0:T(8,128)S(1)} custom-call(f32[1,128,128]{2,1,0:T(8,128)S(1)} %get-tuple-element.49), custom_call_target="InvertDiagBlocksLowerTriangular" | custom-call | tf_op jit(solution)/shard_map/jit(cholesky)/cholesky | solution.py:33
  611.9 1.3 convolution_subtract_fusion.4
  613.2 11.7 %cholesky.398 = f32[128,128]{1,0:T(8,128)S(1)} custom-call(f32[128,128]{1,0:T(8,128)S(1)} %cholesky.448), custom_call_target="Cholesky" | custom-call | tf_op jit(solution)/shard_map/jit(cholesky)/cholesky | solution.py:33
  625.5 9.8 %custom-call.33 = f32[1,128,128]{1,2,0:T(8,128)S(1)} custom-call(f32[1,128,128]{2,1,0:T(8,128)S(1)} %get-tuple-element.46), custom_call_target="InvertDiagBlocksLowerTriangular" | custom-call | tf_op jit(solution)/shard_map/jit(cholesky)/cholesky | solution.py:33
  635.6 1.2 convolution_subtract_fusion.10
  636.8 11.7 %cholesky.415 = f32[128,128]{1,0:T(8,128)S(1)} custom-call(f32[128,128]{1,0:T(8,128)S(1)} %convolution_subtract_fusion.10), custom_call_target="Cholesky" | custom-call | tf_op jit(solution)/shard_map/jit(cholesky)/cholesky | solution.py:33
  648.5 0.7 compare_reduce_fusion
  651.9 1.4 select_select_fusion
  653.2 12.0 %while.5 = (s32[]{:T(128)}, f32[512,512]{1,0:T(8,128)}, s32[4,2]{0,1:T(2,128)S(1)}, f32[4,128,128]{2,1,0:T(8,128)S(1)}, s32[]{:T(128)}) while((s32[]{:T(128)}, f32[512,512]{1,0:T(8,128)}, s32[4,2]{0,1:T(2,128)S(1)}, f32[4,128,128]{2,1,0:T(8,128)S(1)}, s32[]{:T(128)}) %tuple.72), condition=%wide.while_cond.clone, body=%wide.while_body.clone.sunk | while | flops 2 | bytes 131181 | solution.py:34
  653.9 2.3 bitcast_dynamic-update-slice_fusion.5
  656.9 2.3 bitcast_dynamic-update-slice_fusion.5
  660.0 2.3 bitcast_dynamic-update-slice_fusion.5
  663.0 2.3 bitcast_dynamic-update-slice_fusion.5
  665.3 39.3 %custom-call.34 = f32[4,128,128]{1,2,0:T(8,128)S(1)} custom-call(f32[4,128,128]{2,1,0:T(8,128)S(1)} %get-tuple-element.22), custom_call_target="InvertDiagBlocksLowerTriangular" | custom-call | tf_op jit(solution)/shard_map/jit(_solve_triangular)/triangular_solve | solution.py:34
  704.9 1.2 convolution_subtract_fusion.8
  706.5 1.5 convolution_subtract_fusion.3
  708.3 1.7 convolution_subtract_fusion.2
  710.4 0.7 fusion.17
  711.9 29.0 %all-gather.11.cloned.1.call-done = bf16[1024,512]{0,1:T(8,128)(2,1)} async-done(((bf16[256,512]{0,1:T(8,128)(2,1)}), bf16[1024,512]{0,1:T(8,128)(2,1)}) %all-gather.11.cloned.1.call-update) | async-done | bytes 1048592 | tf_op jit(solution)/shard_map/all_gather | solution.py:36
  740.9 2.2 fusion
  743.1 1.2 copy.36
  (87 shorter events, 17.5 us)
Async XLA Ops:
  6.5 120.0 %all-gather.5.cloned.1.call-start = ((), (), s32[]{:S(2)}) async-start(), calls=%async_computation.1 | async-start | bytes 7864320 | tf_op jit(solution)/shard_map/all_gather | solution.py:23
  7.3 170.3 %all-gather.7.cloned.1.call-start = ((), (), s32[]{:S(2)}) async-start(), calls=%async_computation.3 | async-start | bytes 2621440 | tf_op jit(solution)/shard_map/all_gather | solution.py:27
  8.0 224.1 %all-reduce.5.cloned.1.call-start = ((), (), s32[]{:S(2)}) async-start(), calls=%async_computation.2 | async-start | bytes 2097152 | tf_op jit(solution)/shard_map/psum | solution.py:24
  132.7 99.4 %copy-start.5 = (f32[256,512]{1,0:T(8,128)S(1)}, f32[256,512]{1,0:T(8,128)}, u32[]{:S(2)}) copy-start(f32[256,512]{1,0:T(8,128)} %param.6) | copy-start | bytes 1572868
  132.7 156.4 %all-reduce.7.cloned.1.call-start = ((), (), s32[]{:S(2)}) async-start(), calls=%async_computation.4 | async-start | bytes 2097152 | tf_op jit(solution)/shard_map/psum | solution.py:32
  238.0 238.5 %all-gather.9.cloned.1.call-start = ((), (), s32[]{:S(2)}) async-start(), calls=%async_computation.5 | async-start | bytes 2621440 | tf_op jit(solution)/shard_map/all_gather | solution.py:27
  289.1 1.7 copy-start.2
  291.0 1.0 copy-start.4
  428.5 48.1 %copy-start = (f32[256,1024]{1,0:T(8,128)S(1)}, f32[256,1024]{1,0:T(8,128)}, u32[]{:S(2)}) copy-start(f32[256,1024]{1,0:T(8,128)} %all-reduce.5.cloned.1.call-done) | copy-start | bytes 3145732
  431.1 128.1 %all-reduce.9.cloned.1.call-start = ((), (), s32[]{:S(2)}) async-start(), calls=%async_computation.6 | async-start | bytes 2097152 | tf_op jit(solution)/shard_map/psum | solution.py:32
  482.3 228.9 %all-to-all-start = ((bf16[4,768,256]{2,1,0:T(8,128)(2,1)}), bf16[4,768,256]{2,1,0:T(8,128)(2,1)S(1)}, u32[]{:S(2)}, u32[]{:S(2)}) async-start(bf16[4,768,256]{2,1,0:T(8,128)(2,1)} %bitcast.26), calls=%async_computation | async-start | bytes 3145728 | tf_op jit(solution)/shard_map/all_to_all | solution.py:39
  485.8 255.0 %all-gather.11.cloned.1.call-start = ((), (), s32[]{:S(2)}) async-start(), calls=%async_computation.7 | async-start | bytes 1310720 | tf_op jit(solution)/shard_map/all_gather | solution.py:36
  559.1 2.7 copy-start.1
  563.3 1.0 copy-start.3
Sparse Core Ops, SparseCore 0:
  8.9 117.5 all-gather.4
  128.1 45.1 all-gather.6
  176.4 55.6 all-reduce.4
  238.2 50.8 all-reduce.6
  431.2 45.3 all-gather.8
  482.4 76.7 all-reduce.8
  711.2 29.5 all-gather.10
where the time goes:
time: 757 us; the launch traced here: 752 us
  waiting for transfers between devices  373 us (49%)
  other arithmetic  245 us (32%)
  blocking collectives  41.2 us (5%)
  matrix products  39.6 us (5%)
  local copies, waits for them, and re-layouts  28.8 us (4%)
  between operations  20.2 us (3%)
    another operation x29, other arithmetic, on_device(): factor = jnp.linalg.cholesky(correlation)  158 us
    psum x2, waiting for transfers between devices, on_device(): correlation = lax.psum(local_correlation, 'batch')  124 us
    all_gather x1, waiting for transfers between devices, on_device(): lax.all_gather(bases, 'batch', axis=1, tiled=True)  118 us
    another operation x5, other arithmetic, on_device(): q_own = jax.scipy.linalg.solve_triangular(factor, lifted.T, lower=True).T  80.5 us
    psum x1, waiting for transfers between devices, on_device(): gram_rows = lax.psum(partial_value, 'rows')  54.5 us
    all_gather x2, waiting for transfers between devices, on_device(): q_full = lax.all_gather(q_own, 'batch', axis=0, tiled=True)  45.5 us
    psum x1, blocking collectives, on_device(): lax.psum(jnp.sum(jnp.square(bases.astype(jnp.float32))), ('rows', 'batch'))  41.2 us
    all_gather x1, waiting for transfers between devices, on_device(): q_every = lax.all_gather(q_low, 'batch', axis=0, tiled=True)  29 us
  transfers between devices with their start and end apart: 8, of which 6 were waited for; matrix products, arithmetic and copies ran while one was open for 21% of the time, Pallas kernels for 0%

commit v1 on v0

v1 whole, which is shorter than its diff:
```python
import functools

import jax
import jax.numpy as jnp
from jax import lax
from jax.experimental import pallas as pl
from jax.experimental.pallas import tpu as pltpu
from jax.sharding import PartitionSpec as P

ITERS = 2
LANES = 128
SUB = 8
PANEL = 32
REPEAT = 4
SHIFT = 2.0**-15
WIDE = 256
ORTHO_TOL = 2.0**-8
NN = ((1,), (0,))
TN = ((0,), (0,))
NT = ((1,), (1,))
f32 = jnp.float32
bf16 = jnp.bfloat16
VMEM = pl.BlockSpec(memory_space=pltpu.VMEM)
SMEM = pl.BlockSpec(memory_space=pltpu.SMEM)


def dot(left, right, dims):
    return lax.dot_general(left, right, (dims, ((), ())), preferred_element_type=f32)


def split(value):
    high = value.astype(bf16)
    return high, (value - high.astype(f32)).astype(bf16)


def dot_split(left, right, dims):
    return dot(left[0], right[0], dims) + dot(left[0], right[1], dims) + dot(left[1], right[0], dims)


def swap(value, axis, offset):
    size = lax.axis_size(axis)
    return lax.ppermute(value, axis, [(i, i ^ offset) for i in range(size)])


def spans(count, size):
    return [slice(i * size, (i + 1) * size) for i in range(count)]


def tile_table(n_batch, per_basis, n_rows):
    tiles = [
        (first * per_basis + i, second * per_basis + j)
        for first in range(n_batch)
        for second in range(first + 1, n_batch)
        for i in range(per_basis)
        for j in range(per_basis)
    ]
    share = -(-len(tiles) // n_rows)
    return tiles + tiles[-1:] * (share * n_rows - len(tiles)), share


def own_tiles(per_basis):
    return [(i, j) for i in range(per_basis) for j in range(i, per_basis)]


def spread_copy(value, axis, offsets):
    return jnp.stack([value] + [swap(value, axis, offset) for offset in offsets])


def diagonal_kernel(bases, out):
    per_basis = bases.shape[1] // LANES
    columns = spans(per_basis, LANES)
    for at, (i, j) in zip(spans(len(own_tiles(per_basis)), LANES), own_tiles(per_basis)):
        out[at] = dot(bases[:, columns[i]], bases[:, columns[j]], TN)


def cross_kernel(at_ref, table, *refs):
    chips = lax.axis_size("rows") // 2
    n_batch = lax.axis_size("batch")
    pieces, (rows, *outs, both) = refs[: 2 * n_batch], refs[2 * n_batch :]
    chip, core, batch = at_ref[0], at_ref[1], at_ref[2]
    sub_rows, basis = pieces[0].shape
    for half in range(2):
        for offset in range(n_batch):
            first = pl.multiple_of(lax.bitwise_xor(batch, offset) * basis, basis)
            both[half * sub_rows : (half + 1) * sub_rows, pl.ds(first, basis)] = pieces[half * n_batch + offset][...]
    rows[...] = both[:sub_rows]
    for offset, out in enumerate(outs):
        share = out.shape[0] // LANES
        owner = 2 * lax.bitwise_xor(chip, offset) + core
        for j, at in enumerate(spans(share, LANES)):
            place = 2 * (owner * share + j)
            left = pl.multiple_of(table[place] * LANES, LANES)
            right = pl.multiple_of(table[place + 1] * LANES, LANES)
            out[at] = dot(both[:, pl.ds(left, LANES)], both[:, pl.ds(right, LANES)], TN)


def share_kernel(at_ref, *refs):
    n_batch = lax.axis_size("batch")
    blocks, outs = refs[:-n_batch], refs[-n_batch:]
    batch = at_ref[2]
    height = LANES // n_batch
    for offset, out in enumerate(outs):
        first = pl.multiple_of(lax.bitwise_xor(batch, offset) * height, height)
        for j, at in enumerate(spans(out.shape[0] // height, height)):
            rows = pl.ds(j * LANES + first, height)
            total = blocks[0][rows, :]
            for block in blocks[1:]:
                total = total + block[rows, :]
            out[at] = total


def spread(value, index):
    return jnp.broadcast_to(value[index : index + 1, :], value.shape)


def factor_block(work):
    groups = PANEL // SUB
    sub = lax.broadcasted_iota(jnp.int32, (SUB, LANES), 0)
    for r0 in range(0, LANES, PANEL):
        m = [
            [work[r0 + SUB * g : r0 + SUB * (g + 1), LANES * t : LANES * (t + 1)] for t in range(2)]
            for g in range(groups)
        ]
        col = {}
        for j in range(PANEL):
            for g in range(j // SUB, groups):
                col[j, g] = jnp.broadcast_to(m[g][0][:, r0 + j : r0 + j + 1], (SUB, LANES))
        scale = [None] * groups
        for j in range(PANEL):
            gj, sj = divmod(j, SUB)
            pivot = spread(col[j, gj], sj)
            inverse = 1.0 / pivot
            root = lax.rsqrt(pivot)
            scale[gj] = root if scale[gj] is None else jnp.where(sub == sj, root, scale[gj])
            source = [spread(m[gj][t], sj) for t in range(2)]
            scaled = {g: col[j, g] * inverse for g in range(gj, groups)}
            for k in range(j + 1, PANEL):
                entry = spread(col[j, k // SUB], k % SUB)
                for g in range(k // SUB, groups):
                    col[k, g] = col[k, g] - scaled[g] * entry
            for g in range(gj, groups):
                factor = jnp.where(sub > sj, scaled[g], 0.0) if g == gj else scaled[g]
                for t in range(2):
                    m[g][t] = m[g][t] - factor * source[t]
        rows = jnp.concatenate(
            [jnp.concatenate([m[g][t] * scale[g] for t in range(2)], axis=1) for g in range(groups)], axis=0
        )
        work[r0 : r0 + PANEL, :] = rows
        below = r0 + PANEL
        if below < LANES:
            high, low = split(rows)
            left = jnp.concatenate([high[:, :LANES], high[:, :LANES], low[:, :LANES]], axis=0)
            right = jnp.concatenate([high, low, high], axis=0)
            work[below:, :] = work[below:, :] - dot(left, right, TN)[below:, :]


def identity(size):
    return lax.broadcasted_iota(jnp.int32, (size, size), 0) == lax.broadcasted_iota(jnp.int32, (size, size), 1)


def inverse_factor(a, e, x, work):
    size = a.shape[0]
    e[...] = identity(size).astype(f32)
    lanes = lax.broadcasted_iota(jnp.int32, (LANES, size), 1)

    def block(k, carry):
        at = pl.ds(pl.multiple_of(k * LANES, LANES), LANES)
        work[:, :LANES] = a[at, at]
        work[:, LANES:] = identity(LANES).astype(f32)
        factor_block(work)
        own = split(work[:, LANES:])
        x_rows = dot_split(own, split(e[at, :]), NN)
        x[at, :] = x_rows
        upper = dot_split(own, split(a[at, :]), NN)
        upper = split(jnp.where(lanes >= (k + 1) * LANES, upper, 0.0))
        a[...] = a[...] - dot_split(upper, upper, TN)
        e[...] = e[...] - dot_split(upper, split(x_rows), TN)
        return carry

    lax.fori_loop(0, size // LANES, block, 0)


def prepare_kernel(at_ref, own, sibling, high, low, diagonal, whole):
    chip, core, batch = at_ref[0], at_ref[1], at_ref[2]
    chips, n_batch, height, _ = own.shape
    columns, size = whole.shape
    basis = columns // n_batch
    share = basis // (2 * chips)
    part = diagonal.shape[1] // (2 * chips)

    def place(offset, carry):
        for other, block in enumerate((own, sibling)):
            row = 2 * lax.bitwise_xor(chip, offset) + lax.bitwise_xor(core, other)
            for z in range(n_batch):
                group = lax.bitwise_xor(batch, z)
                diagonal[group, pl.ds(pl.multiple_of(row * part, SUB), part), :] = block[offset, z, :part, :]
                first = pl.multiple_of(group * basis + row * share, SUB)
                for k, lanes in enumerate(spans(size // LANES, LANES)):
                    lower = part + k * share
                    whole[pl.ds(first, share), lanes] = block[offset, z, lower : lower + share, :]
        return carry

    lax.fori_loop(0, chips, place, 0)
    for rows in spans(columns // LANES, LANES):
        high[:, rows], low[:, rows] = split(whole[rows, :].T)


def trace_of(diagonal, per_basis):
    total = jnp.zeros((LANES, LANES), f32)
    eye = identity(LANES)
    for group in range(diagonal.shape[0]):
        for at, (i, j) in zip(spans(len(own_tiles(per_basis)), LANES), own_tiles(per_basis)):
            if i == j:
                total = total + jnp.where(eye, diagonal[group, at, :], 0.0)
    return jnp.sum(total)


def place_gram(at_ref, table, own, sibling, diagonal, factor, pair):
    chip, core, batch = at_ref[0], at_ref[1], at_ref[2]
    chips, n_batch, share_rows, _ = own.shape
    height = LANES // n_batch
    share = share_rows // height
    per_basis = pair[0].shape[0] // LANES // n_batch

    def place(offset, carry):
        for other, block in enumerate((own, sibling)):
            owner = 2 * lax.bitwise_xor(chip, offset) + lax.bitwise_xor(core, other)
            for j, inner in enumerate(spans(share, height)):
                at = 2 * (owner * share + j)
                row = pl.multiple_of(table[at] * LANES, LANES)
                column = pl.multiple_of(table[at + 1] * LANES, LANES)
                for z in range(n_batch):
                    first = pl.multiple_of(row + lax.bitwise_xor(batch, z) * height, height)
                    for ref, value in zip(pair, split(block[offset, z, inner, :] * factor)):
                        ref[pl.ds(first, height), pl.ds(column, LANES)] = value
                for ref in pair:
                    ref[pl.ds(column, LANES), pl.ds(row, LANES)] = ref[pl.ds(row, LANES), pl.ds(column, LANES)].T
        return carry

    lax.fori_loop(0, chips, place, 0)
    for group in range(n_batch):
        for at, (i, j) in zip(spans(len(own_tiles(per_basis)), LANES), own_tiles(per_basis)):
            rows, columns = (slice((group * per_basis + k) * LANES, (group * per_basis + k + 1) * LANES) for k in (i, j))
            for ref, value in zip(pair, split(diagonal[group, at, :] * factor)):
                ref[rows, columns] = value
                if i != j:
                    ref[columns, rows] = value.T


def solve_kernel(at_ref, table, own, sibling, diagonal, sh, sl, rows, modes, ah, al, ph, plo, qh, ql, a, e, x, work):
    size, columns = sh.shape
    per_basis = columns // LANES // own.shape[1]
    gram, p, q = (ah, al), (ph, plo), (qh, ql)
    factor = 1.0 / (trace_of(diagonal, per_basis) / columns)
    place_gram(at_ref, table, own, sibling, diagonal, factor, gram)

    def lift(source, target):
        def chunk(n, carry):
            at = pl.ds(pl.multiple_of(n * WIDE, WIDE), WIDE)
            before = source[0][:, at].astype(f32) + source[1][:, at].astype(f32)
            after = before + dot_split((source[0][...], source[1][...]), (gram[0][:, at], gram[1][:, at]), NN)
            target[0][:, at], target[1][:, at] = split(after)
            return carry

        lax.fori_loop(0, columns // WIDE, chunk, 0)

    def correlate():
        for at in spans(size // LANES, LANES):
            a[at, at.start :] = dot_split((ph[at], plo[at]), (ph[at.start :], plo[at.start :]), NT)

    def rotate():
        for at in spans(size // LANES, LANES):
            turned = dot_split(split(x[at, : at.stop]), (ph[: at.stop], plo[: at.stop]), NN)
            qh[at], ql[at] = split(turned)

    lift((sh, sl), q)
    lift(q, p)
    correlate()
    inverse_factor(a, e, x, work)
    rotate()

    worst = jnp.zeros((), f32)
    for at in spans(size // LANES, LANES):
        gap = dot(qh[at], qh[...], NT)
        here = lax.broadcasted_iota(jnp.int32, gap.shape, 0) + at.start == lax.broadcasted_iota(jnp.int32, gap.shape, 1)
        gap = gap - here.astype(f32)
        worst = jnp.maximum(worst, jnp.max(jnp.sum(gap * gap, axis=1, keepdims=True)))

    @pl.when(jnp.logical_not(worst < ORTHO_TOL**2))
    def _():
        qh[...], ql[...] = sh[...], sl[...]

        def again(k, carry):
            turn = lax.rem(k, REPEAT)

            @pl.when(turn == 0)
            def _():
                lift(q, p)

            @pl.when(turn != 0)
            def _():
                ph[...], plo[...] = qh[...], ql[...]

            correlate()

            @pl.when(turn < 2)
            def _():
                eye = identity(LANES)
                tiles = [a[at, at] for at in spans(size // LANES, LANES)]
                shift = SHIFT * jnp.sum(sum(jnp.where(eye, tile, 0.0) for tile in tiles))
                for at, tile in zip(spans(size // LANES, LANES), tiles):
                    a[at, at] = tile + jnp.where(eye, shift, 0.0)

            inverse_factor(a, e, x, work)
            rotate()
            return carry

        lax.fori_loop(0, ITERS * REPEAT, again, 0)

    for lo in range(0, size, WIDE):
        modes[:, lo : lo + WIDE] = dot(rows[...], qh[lo : lo + WIDE], NT).astype(bf16)


def on_device(bases, start):
    local_rows, basis = bases.shape
    size = start.shape[1]
    n_batch, n_rows = lax.axis_size("batch"), lax.axis_size("rows")
    chips = n_rows // 2
    columns = basis * n_batch
    sub_rows = local_rows // n_batch
    per_basis = basis // LANES
    batch, row = lax.axis_index("batch"), lax.axis_index("rows")
    at = jnp.stack([row // 2, row % 2, batch]).astype(jnp.int32)
    tiles, share = tile_table(n_batch, per_basis, n_rows)
    table = jnp.asarray([k for tile in tiles for k in tile], jnp.int32)
    other_batches, other_chips = range(1, n_batch), range(2, n_rows, 2)

    def call(kernel, outs, scratch, *args, n_smem=0, flops=0, moved=1 << 20):
        return pl.pallas_call(
            kernel,
            out_shape=[jax.ShapeDtypeStruct(shape, dtype) for shape, dtype in outs],
            in_specs=[SMEM] * n_smem + [VMEM] * (len(args) - n_smem),
            out_specs=[VMEM] * len(outs),
            scratch_shapes=[pltpu.VMEM(shape, dtype) for shape, dtype in scratch],
            compiler_params=pltpu.CompilerParams(vmem_limit_bytes=60 << 20),
            cost_estimate=pl.CostEstimate(flops=flops, bytes_accessed=moved, transcendentals=0),
        )(*args)

    pieces = []
    for offset in range(n_batch):
        piece = lax.dynamic_slice_in_dim(bases, (batch ^ offset) * sub_rows, sub_rows, 0)
        pieces.append(swap(piece, "batch", offset) if offset else piece)
    other_pieces = [swap(piece, "rows", 1) for piece in pieces]

    own_count = len(own_tiles(per_basis))
    (diagonal,) = call(
        diagonal_kernel, [((own_count * LANES, LANES), f32)], [], bases,
        flops=2 * local_rows * own_count * LANES * LANES, moved=bases.size * 2,
    )
    for offset in (1 << k for k in range(n_rows.bit_length() - 1)):
        diagonal = diagonal + swap(diagonal, "rows", offset)
    part = own_count * LANES // n_rows
    start_share = start.shape[0] // n_rows
    mine = lax.dynamic_slice_in_dim(start, row * start_share, start_share, 0)
    mine = [lax.dynamic_slice_in_dim(diagonal, row * part, part, 0)] + jnp.split(mine, size // LANES, axis=1)
    mine = spread_copy(jnp.concatenate(mine), "batch", other_batches)
    mine = spread_copy(mine, "rows", other_chips)
    high, low, diagonal = call(
        prepare_kernel,
        [((size, columns), bf16)] * 2 + [((n_batch, own_count * LANES, LANES), f32)],
        [((columns, size), f32)],
        at, mine, swap(mine, "rows", 1), n_smem=1, moved=8 << 20,
    )

    rows, *blocks = call(
        cross_kernel,
        [((sub_rows, columns), bf16)] + [((share * LANES, LANES), f32)] * chips,
        [((2 * sub_rows, columns), bf16)],
        at, table, *pieces, *other_pieces, n_smem=2,
        flops=4 * sub_rows * chips * share * LANES * LANES, moved=6 << 20,
    )
    blocks = [blocks[0]] + [swap(block, "rows", offset) for block, offset in zip(blocks[1:], other_chips)]
    height = LANES // n_batch
    parts = call(share_kernel, [((share * height, LANES), f32)] * n_batch, [], at, *blocks, n_smem=1)
    total = sum((swap(parts[offset], "batch", offset) for offset in other_batches), parts[0])

    own = spread_copy(spread_copy(total, "batch", other_batches), "rows", other_chips)
    (modes,) = call(
        solve_kernel,
        [((sub_rows, size), bf16)],
        [((columns, columns), bf16)] * 2
        + [((size, columns), bf16)] * 4
        + [((size, size), f32)] * 3
        + [((LANES, 2 * LANES), f32)],
        at, table, own, swap(own, "rows", 1), diagonal, high, low, rows, n_smem=2, flops=10**10, moved=10 << 20,
    )
    return modes


def solution(mesh):
    in_specs = (P("rows", "batch"), P("batch", None))
    out_specs = P(("rows", "batch"), None)
    return jax.shard_map(
        on_device, mesh=mesh, in_specs=in_specs, out_specs=out_specs, check_vma=False
    )
```

time: 757 us -> 158 us (0.21)
  waiting for transfers between devices: 373 us -> 61.1 us
  other arithmetic: 245 us -> 0.89 us
  Pallas kernels: 0 us -> 53.7 us
  blocking collectives: 41.2 us -> 0 us
  matrix products: 39.6 us -> 0 us
  starting transfers between devices: 4.16 us -> 35.5 us
  local copies, waits for them, and re-layouts: 28.8 us -> 6.49 us
  between operations: 20.2 us -> 0.25 us
    another operation x34 -> x5, other arithmetic: 238 us -> 0.82 us  [the longest x1 0.59 us: on_device(): at = jnp.stack([row // 2, row % 2, batch]).astype(jnp.int32)]
    all_gather x4 -> x0, waiting for transfers between devices: 193 us -> none  [the longest x1 118 us: on_device(): lax.all_gather(bases, 'batch', axis=1, tiled=True)]
    psum x3 -> x0, waiting for transfers between devices: 178 us -> none  [the longest x2 124 us: on_device(): correlation = lax.psum(local_correlation, 'batch')]
    ppermute x0 -> x30, waiting for transfers between devices: none -> 61.1 us  [swap(): return lax.ppermute(value, axis, [(i, i ^ offset) for i in range(size)])]
    pallas_call x0 -> x5, Pallas kernels: none -> 53.7 us  [call(): pl.pallas_call(kernel, out_shape=[jax.ShapeDtypeStruct(shape, dtype) for...]
    psum x1 -> x0, blocking collectives: 41.2 us -> none  [on_device(): lax.psum(jnp.sum(jnp.square(bases.astype(jnp.float32))), ('rows', 'batch'))]
    ppermute x0 -> x30, starting transfers between devices: none -> 35.5 us  [swap(): return lax.ppermute(value, axis, [(i, i ^ offset) for i in range(size)])]
    another operation x38 -> x0, local copies, waits for them, and re-layouts: 20.6 us -> none  [the longest x30 20.3 us: on_device(): q_own = jax.scipy.linalg.solve_triangular(factor, lifted.T, lower=True).T]
  transfers between devices with their start and end apart: 8 -> 30, of which waited for: 6 -> 12; matrix products, arithmetic and copies ran while one was open for 21% -> 2% of each run, Pallas kernels for 0% -> 8%
where the time goes in v1:
time: 158 us
  waiting for transfers between devices  61.1 us (39%)
  Pallas kernels  53.7 us (34%)
  starting transfers between devices  35.5 us (22%)
  local copies, waits for them, and re-layouts  6.49 us (4%)
    ppermute x30, waiting for transfers between devices, swap(): return lax.ppermute(value, axis, [(i, i ^ offset) for i in range(size)])  61.1 us
    pallas_call x5, Pallas kernels, call(): pl.pallas_call(kernel, out_shape=[jax.ShapeDtypeStruct(shape, dtype) for...  53.7 us
    ppermute x30, starting transfers between devices, swap(): return lax.ppermute(value, axis, [(i, i ^ offset) for i in range(size)])  35.5 us
    unnamed x37, local copies, waits for them, and re-layouts  5.67 us
  transfers between devices with their start and end apart: 30, of which 12 were waited for; matrix products, arithmetic and copies ran while one was open for 2% of the time, Pallas kernels for 8%

profile of v1, /device:TPU:0, one launch (start us, length us, event | category | flops | bytes accessed | tf_op | source)
XLA Modules:
  0.0 157.9 jit_solution(9000955528545124855)
XLA Ops:
  0.0 3.0 %shard_map.39 = f32[384,128]{1,0:T(8,128)} custom-call(bf16[3072,256]{1,0:T(8,128)(2,1)} %bases.1), custom_call_target="tpu_custom_call" | custom-call | flops 301989888 | bytes 1572864 | tf_op jit(solution)/shard_map/pallas_call | solution.py:339
  3.0 0.5 collective-permute-start.20
  3.5 0.1 constant_dynamic-slice_fusion
  3.6 0.0 copy-start.2
  3.6 4.7 %collective-permute-start.2 = (bf16[768,256]{1,0:T(8,128)(2,1)S(1)}, bf16[768,256]{1,0:T(8,128)(2,1)S(1)}, u32[]{:S(2)}, u32[]{:S(2)}) collective-permute-start(bf16[768,256]{1,0:T(8,128)(2,1)S(1)} %get-tuple-element.29), channel_id=1, source_target_pairs={{0,3},{1,2},{2,1},{3,0},{4,7},{5,6},{6,5},{7,4},{8,11},{9,10},{10,... | collective-permute-start | bytes 1179656 | tf_op jit(solution)/shard_map/ppermute | solution.py:42
  8.3 0.6 collective-permute-start
  9.0 1.7 %collective-permute-start.21 = (f32[384,128]{1,0:T(8,128)S(1)}, f32[384,128]{1,0:T(8,128)S(1)}, u32[]{:S(2)}, u32[]{:S(2)}) collective-permute-start(f32[384,128]{1,0:T(8,128)S(1)} %add.49), channel_id=1, source_target_pairs={{0,8},{4,12},{8,0},{12,4},{16,24},{20,28},{24,16},{28,20},{1,9},{5... | collective-permute-start | bytes 589832 | tf_op jit(solution)/shard_map/ppermute | solution.py:42
  10.7 5.1 %collective-permute-done.21 = f32[384,128]{1,0:T(8,128)S(1)} collective-permute-done((f32[384,128]{1,0:T(8,128)S(1)}, f32[384,128]{1,0:T(8,128)S(1)}, u32[]{:S(2)}, u32[]{:S(2)}) %collective-permute-start.21) | collective-permute-done | bytes 196640 | tf_op jit(solution)/shard_map/ppermute | solution.py:42
  15.8 1.6 %collective-permute-start.22 = (f32[384,128]{1,0:T(8,128)S(1)}, f32[384,128]{1,0:T(8,128)S(1)}, u32[]{:S(2)}, u32[]{:S(2)}) collective-permute-start(f32[384,128]{1,0:T(8,128)S(1)} %add.50), channel_id=1, source_target_pairs={{0,16},{4,20},{8,24},{12,28},{16,0},{20,4},{24,8},{28,12},{1,17},{... | collective-permute-start | bytes 589832 | tf_op jit(solution)/shard_map/ppermute | solution.py:42
  17.4 0.0 collective-permute-start.3
  17.4 1.0 collective-permute-done.2.refs_3_
  18.4 24.1 %collective-permute-done.1.refs_2_ = bf16[768,256]{1,0:T(8,128)(2,1)S(1)} collective-permute-done((bf16[768,256]{1,0:T(8,128)(2,1)S(1)}, bf16[768,256]{1,0:T(8,128)(2,1)S(1)}, u32[]{:S(2)}, u32[]{:S(2)}) %collective-permute-start.1) | collective-permute-done | bytes 393248 | tf_op jit(solution)/shard_map/ppermute | solution.py:42
  42.5 0.0 collective-permute-start.5
  42.5 0.5 collective-permute-start.4
  43.0 0.0 collective-permute-done.22
  43.0 0.7 dynamic-slice_dynamic-update-slice_fusion.3
  43.7 0.7 dynamic-slice_dynamic-update-slice_fusion.2
  44.5 0.7 dynamic-slice_dynamic-update-slice_fusion.1
  45.2 0.7 dynamic-slice_dynamic-update-slice_fusion
  45.9 2.5 %collective-permute-start.25 = (f32[176,128]{1,0:T(8,128)S(1)}, f32[176,128]{1,0:T(8,128)S(1)}, u32[]{:S(2)}, u32[]{:S(2)}) collective-permute-start(f32[176,128]{1,0:T(8,128)S(1)} %dynamic-slice_dynamic-update-slice_fusion), channel_id=1, source_target_pairs={{0,3},{1,2},{2,1},{3,0},{4,7},{5,6},{6,5},{7,4},{8,11},{9,10},{10,... | collective-permute-start | bytes 270344 | tf_op jit(solution)/shard_map/ppermute | solution.py:42
  48.4 0.0 collective-permute-done.3.refs_4_
  48.4 0.0 collective-permute-done.6.refs_7_
  48.4 1.9 %collective-permute-start.23 = (f32[176,128]{1,0:T(8,128)S(1)}, f32[176,128]{1,0:T(8,128)S(1)}, u32[]{:S(2)}, u32[]{:S(2)}) collective-permute-start(f32[176,128]{1,0:T(8,128)S(1)} %dynamic-slice_dynamic-update-slice_fusion), channel_id=1, source_target_pairs={{0,1},{1,0},{2,3},{3,2},{4,5},{5,4},{6,7},{7,6},{8,9},{9,8},{10,11... | collective-permute-start | bytes 270344 | tf_op jit(solution)/shard_map/ppermute | solution.py:42
  50.3 0.6 pad_add_fusion.at_ref
  50.9 0.0 collective-permute-done.4.refs_5_
  51.0 0.7 copy-done.11
  51.7 0.8 copy-done.12
  52.4 6.1 %shard_map.37 = (bf16[768,1024]{1,0:T(8,128)(2,1)}, f32[384,128]{1,0:T(8,128)}, f32[384,128]{1,0:T(8,128)}, f32[384,128]{1,0:T(8,128)}, f32[384,128]{1,0:T(8,128)}) custom-call(s32[3]{0:T(128)} %pad_add_fusion.at_ref, s32[48]{0:T(128)} %constant.51.clone.table, bf16[768,256]{1,0:T(8,128)(2,1)} %copy-done.2, bf16[768,256]{1,0:T(8,128)(2,1)} %copy-done.8, ...), custom_call_target="tpu_custom_call" | custom-call | flops 603979776 | bytes 6291456 | tf_op jit(solution)/shard_map/pallas_call | solution.py:339
  58.5 1.5 collective-permute-start.7
  60.0 0.0 collective-permute-done.24
  60.0 0.0 collective-permute-done.23
  60.1 1.6 %collective-permute-start.27 = (f32[4,176,128]{2,1,0:T(8,128)S(1)}, f32[4,176,128]{2,1,0:T(8,128)S(1)}, u32[]{:S(2)}, u32[]{:S(2)}) collective-permute-start(f32[4,176,128]{2,1,0:T(8,128)S(1)} %get-tuple-element.34), channel_id=1, source_target_pairs={{0,16},{4,20},{8,24},{12,28},{16,0},{20,4},{24,8},{28,12},{1,17},{... | collective-permute-start | bytes 1081352 | tf_op jit(solution)/shard_map/ppermute | solution.py:42
  61.7 0.5 collective-permute-start.26
  62.2 1.4 collective-permute-start.28
  63.7 1.5 collective-permute-start.8
  65.2 1.4 collective-permute-done.7.refs_1_
  66.6 2.5 %collective-permute-start.9 = (f32[384,128]{1,0:T(8,128)}, f32[384,128]{1,0:T(8,128)S(1)}, u32[]{:S(2)}, u32[]{:S(2)}) collective-permute-start(f32[384,128]{1,0:T(8,128)} %get-tuple-element.20), channel_id=1, source_target_pairs={{0,24},{4,28},{8,16},{12,20},{16,8},{20,12},{24,0},{28,4},{1,25},{... | collective-permute-start | bytes 589832 | tf_op jit(solution)/shard_map/ppermute | solution.py:42
  69.0 16.6 %collective-permute-done.8.refs_2_ = f32[384,128]{1,0:T(8,128)S(1)} collective-permute-done((f32[384,128]{1,0:T(8,128)}, f32[384,128]{1,0:T(8,128)S(1)}, u32[]{:S(2)}, u32[]{:S(2)}) %collective-permute-start.8) | collective-permute-done | bytes 196640 | tf_op jit(solution)/shard_map/ppermute | solution.py:42
  85.6 0.7 copy-done.14
  86.3 0.1 copy-done.15
  86.4 1.9 %shard_map.38 = (f32[96,128]{1,0:T(8,128)}, f32[96,128]{1,0:T(8,128)}, f32[96,128]{1,0:T(8,128)}, f32[96,128]{1,0:T(8,128)}) custom-call(s32[3]{0:T(128)} %pad_add_fusion.at_ref, f32[384,128]{1,0:T(8,128)} %get-tuple-element.17.refs_0_, f32[384,128]{1,0:T(8,128)} %copy-done.13, f32[384,128]{1,0:T(8,128)} %copy-done.14, f32[384,128]{1,0:T(8,128)} %copy-done.15), custom_call_target="tpu_custom_call" | custom-call | bytes 1048576 | tf_op jit(solution)/shard_map/pallas_call | solution.py:339
  88.3 0.5 collective-permute-start.10
  88.8 2.6 %collective-permute-start.11 = (f32[96,128]{1,0:T(8,128)}, f32[96,128]{1,0:T(8,128)S(1)}, u32[]{:S(2)}, u32[]{:S(2)}) collective-permute-start(f32[96,128]{1,0:T(8,128)} %get-tuple-element.23), channel_id=1, source_target_pairs={{0,2},{1,3},{2,0},{3,1},{4,6},{5,7},{6,4},{7,5},{8,10},{9,11},{10,... | collective-permute-start | bytes 147464 | tf_op jit(solution)/shard_map/ppermute | solution.py:42
  91.4 1.3 collective-permute-start.12
  92.7 0.0 collective-permute-done.26
  92.7 0.1 pad_maximum_fusion.own
  92.8 0.1 collective-permute-start.29
  92.9 2.1 %collective-permute-done.11 = f32[96,128]{1,0:T(8,128)S(1)} collective-permute-done((f32[96,128]{1,0:T(8,128)}, f32[96,128]{1,0:T(8,128)S(1)}, u32[]{:S(2)}, u32[]{:S(2)}) %collective-permute-start.11) | collective-permute-done | bytes 49184 | tf_op jit(solution)/shard_map/ppermute | solution.py:42
  95.1 2.4 %collective-permute-done.12 = f32[96,128]{1,0:T(8,128)S(1)} collective-permute-done((f32[96,128]{1,0:T(8,128)}, f32[96,128]{1,0:T(8,128)S(1)}, u32[]{:S(2)}, u32[]{:S(2)}) %collective-permute-start.12) | collective-permute-done | bytes 49184 | tf_op jit(solution)/shard_map/ppermute | solution.py:42
  97.5 1.4 collective-permute-start.15
  98.9 3.0 %collective-permute-start.13 = (f32[96,128]{1,0:T(8,128)S(1)}, f32[96,128]{1,0:T(8,128)S(1)}, u32[]{:S(2)}, u32[]{:S(2)}) collective-permute-start(f32[96,128]{1,0:T(8,128)S(1)} %add_add_fusion), channel_id=1, source_target_pairs={{0,1},{1,0},{2,3},{3,2},{4,5},{5,4},{6,7},{7,6},{8,9},{9,8},{10,11... | collective-permute-start | bytes 147464 | tf_op jit(solution)/shard_map/ppermute | solution.py:42
  101.9 1.5 collective-permute-done.15
  103.4 1.1 collective-permute-done.14
  104.6 1.6 %collective-permute-start.17 = (f32[4,96,128]{2,1,0:T(8,128)S(1)}, f32[4,96,128]{2,1,0:T(8,128)S(1)}, u32[]{:S(2)}, u32[]{:S(2)}) collective-permute-start(f32[4,96,128]{2,1,0:T(8,128)S(1)} %get-tuple-element.36), channel_id=1, source_target_pairs={{0,16},{4,20},{8,24},{12,28},{16,0},{20,4},{24,8},{28,12},{1,17},{... | collective-permute-start | bytes 589832 | tf_op jit(solution)/shard_map/ppermute | solution.py:42
  106.1 0.5 collective-permute-start.16
  106.7 1.4 collective-permute-start.18
  108.1 2.4 %collective-permute-done.17 = f32[4,96,128]{2,1,0:T(8,128)S(1)} collective-permute-done((f32[4,96,128]{2,1,0:T(8,128)S(1)}, f32[4,96,128]{2,1,0:T(8,128)S(1)}, u32[]{:S(2)}, u32[]{:S(2)}) %collective-permute-start.17) | collective-permute-done | bytes 196640 | tf_op jit(solution)/shard_map/ppermute | solution.py:42
  110.6 1.3 collective-permute-done.16
  111.8 2.0 %collective-permute-done.18 = f32[4,96,128]{2,1,0:T(8,128)S(1)} collective-permute-done((f32[4,96,128]{2,1,0:T(8,128)S(1)}, f32[4,96,128]{2,1,0:T(8,128)S(1)}, u32[]{:S(2)}, u32[]{:S(2)}) %collective-permute-start.18) | collective-permute-done | bytes 196640 | tf_op jit(solution)/shard_map/ppermute | solution.py:42
  113.9 0.1 pad_maximum_fusion.1.own
  113.9 0.1 collective-permute-start.19
  114.0 1.2 copy-done.3
  115.3 4.5 %shard_map.40 = (bf16[512,1024]{1,0:T(8,128)(2,1)}, bf16[512,1024]{1,0:T(8,128)(2,1)}, f32[4,384,128]{2,1,0:T(8,128)}) custom-call(s32[3]{0:T(128)} %pad_add_fusion.at_ref, f32[4,4,176,128]{3,2,1,0:T(8,128)} %copy-done.1, f32[4,4,176,128]{3,2,1,0:T(8,128)} %copy-done.3), custom_call_target="tpu_custom_call" | custom-call | bytes 8388608 | tf_op jit(solution)/shard_map/pallas_call | solution.py:339
  119.8 38.1 %shard_map.41 = bf16[768,512]{1,0:T(8,128)(2,1)} custom-call(s32[3]{0:T(128)} %pad_add_fusion.at_ref, s32[48]{0:T(128)} %constant.51.clone.table, f32[4,4,96,128]{3,2,1,0:T(8,128)} %copy-done.4, f32[4,4,96,128]{3,2,1,0:T(8,128)} %collective-permute-done.19.sibling, f32[4,384,128]{2,1,0:T(8,128)} %get-tuple-element.25.diagonal, ...), custom_call_target="tpu_custom_call" | custom-call | flops 10000000000 | bytes 10485760 | tf_op jit(solution)/shard_map/pallas_call | solution.py:339
  (49 shorter events, 0.2 us)
Async XLA Ops:
  0.0 3.5 %copy-start = (bf16[3072,256]{1,0:T(8,128)(2,1)S(1)}, bf16[3072,256]{1,0:T(8,128)(2,1)}, u32[]{:S(2)}) copy-start(bf16[3072,256]{1,0:T(8,128)(2,1)} %bases.1) | copy-start | bytes 4718596
  3.0 5.9 %collective-permute-start.20 = (f32[384,128]{1,0:T(8,128)}, f32[384,128]{1,0:T(8,128)S(1)}, u32[]{:S(2)}, u32[]{:S(2)}) collective-permute-start(f32[384,128]{1,0:T(8,128)} %shard_map.39), channel_id=1, source_target_pairs={{0,4},{4,0},{8,12},{12,8},{16,20},{20,16},{24,28},{28,24},{1,5},{5... | collective-permute-start | bytes 589832 | tf_op jit(solution)/shard_map/ppermute | solution.py:42
  3.5 5.4 %copy-start.5 = (f32[384,128]{1,0:T(8,128)S(1)}, f32[384,128]{1,0:T(8,128)}, u32[]{:S(2)}) copy-start(f32[384,128]{1,0:T(8,128)} %shard_map.39) | copy-start | bytes 589828
  3.6 47.3 %copy-start.2 = (bf16[768,256]{1,0:T(8,128)(2,1)}, bf16[768,256]{1,0:T(8,128)(2,1)S(1)}, u32[]{:S(2)}) copy-start(bf16[768,256]{1,0:T(8,128)(2,1)S(1)} %get-tuple-element.32.refs_0_) | copy-start | bytes 1179652
  3.6 14.8 %collective-permute-start.2 = (bf16[768,256]{1,0:T(8,128)(2,1)S(1)}, bf16[768,256]{1,0:T(8,128)(2,1)S(1)}, u32[]{:S(2)}, u32[]{:S(2)}) collective-permute-start(bf16[768,256]{1,0:T(8,128)(2,1)S(1)} %get-tuple-element.29), channel_id=1, source_target_pairs={{0,3},{1,2},{2,1},{3,0},{4,7},{5,6},{6,5},{7,4},{8,11},{9,10},{10,... | collective-permute-start | bytes 1179656 | tf_op jit(solution)/shard_map/ppermute | solution.py:42
  8.3 34.2 %collective-permute-start.1 = (bf16[768,256]{1,0:T(8,128)(2,1)S(1)}, bf16[768,256]{1,0:T(8,128)(2,1)S(1)}, u32[]{:S(2)}, u32[]{:S(2)}) collective-permute-start(bf16[768,256]{1,0:T(8,128)(2,1)S(1)} %get-tuple-element.30), channel_id=1, source_target_pairs={{0,2},{1,3},{2,0},{3,1},{4,6},{5,7},{6,4},{7,5},{8,10},{9,11},{10,... | collective-permute-start | bytes 1179656 | tf_op jit(solution)/shard_map/ppermute | solution.py:42
  8.3 34.2 %collective-permute-start = (bf16[768,256]{1,0:T(8,128)(2,1)S(1)}, bf16[768,256]{1,0:T(8,128)(2,1)S(1)}, u32[]{:S(2)}, u32[]{:S(2)}) collective-permute-start(bf16[768,256]{1,0:T(8,128)(2,1)S(1)} %get-tuple-element.31), channel_id=1, source_target_pairs={{0,1},{1,0},{2,3},{3,2},{4,5},{5,4},{6,7},{7,6},{8,9},{9,8},{10,11... | collective-permute-start | bytes 1179656 | tf_op jit(solution)/shard_map/ppermute | solution.py:42
  9.0 6.8 %collective-permute-start.21 = (f32[384,128]{1,0:T(8,128)S(1)}, f32[384,128]{1,0:T(8,128)S(1)}, u32[]{:S(2)}, u32[]{:S(2)}) collective-permute-start(f32[384,128]{1,0:T(8,128)S(1)} %add.49), channel_id=1, source_target_pairs={{0,8},{4,12},{8,0},{12,4},{16,24},{20,28},{24,16},{28,20},{1,9},{5... | collective-permute-start | bytes 589832 | tf_op jit(solution)/shard_map/ppermute | solution.py:42
  15.8 27.2 %collective-permute-start.22 = (f32[384,128]{1,0:T(8,128)S(1)}, f32[384,128]{1,0:T(8,128)S(1)}, u32[]{:S(2)}, u32[]{:S(2)}) collective-permute-start(f32[384,128]{1,0:T(8,128)S(1)} %add.50), channel_id=1, source_target_pairs={{0,16},{4,20},{8,24},{12,28},{16,0},{20,4},{24,8},{28,12},{1,17},{... | collective-permute-start | bytes 589832 | tf_op jit(solution)/shard_map/ppermute | solution.py:42
  17.4 31.0 %collective-permute-start.3 = (bf16[768,256]{1,0:T(8,128)(2,1)S(1)}, bf16[768,256]{1,0:T(8,128)(2,1)S(1)}, u32[]{:S(2)}, u32[]{:S(2)}) collective-permute-start(bf16[768,256]{1,0:T(8,128)(2,1)S(1)} %get-tuple-element.32.refs_0_), channel_id=1, source_target_pairs={{0,4},{4,0},{8,12},{12,8},{16,20},{20,16},{24,28},{28,24},{1,5},{5... | collective-permute-start | bytes 1179656 | tf_op jit(solution)/shard_map/ppermute | solution.py:42
  18.4 32.5 %copy-start.6 = (bf16[768,256]{1,0:T(8,128)(2,1)}, bf16[768,256]{1,0:T(8,128)(2,1)S(1)}, u32[]{:S(2)}) copy-start(bf16[768,256]{1,0:T(8,128)(2,1)S(1)} %collective-permute-done.2.refs_3_) | copy-start | bytes 1179652
  18.4 30.0 %collective-permute-start.6 = (bf16[768,256]{1,0:T(8,128)(2,1)S(1)}, bf16[768,256]{1,0:T(8,128)(2,1)S(1)}, u32[]{:S(2)}, u32[]{:S(2)}) collective-permute-start(bf16[768,256]{1,0:T(8,128)(2,1)S(1)} %collective-permute-done.2.refs_3_), channel_id=1, source_target_pairs={{0,4},{4,0},{8,12},{12,8},{16,20},{20,16},{24,28},{28,24},{1,5},{5... | collective-permute-start | bytes 1179656 | tf_op jit(solution)/shard_map/ppermute | solution.py:42
  42.5 8.4 %copy-start.7 = (bf16[768,256]{1,0:T(8,128)(2,1)}, bf16[768,256]{1,0:T(8,128)(2,1)S(1)}, u32[]{:S(2)}) copy-start(bf16[768,256]{1,0:T(8,128)(2,1)S(1)} %collective-permute-done.1.refs_2_) | copy-start | bytes 1179652
  42.5 8.4 %collective-permute-start.5 = (bf16[768,256]{1,0:T(8,128)(2,1)S(1)}, bf16[768,256]{1,0:T(8,128)(2,1)S(1)}, u32[]{:S(2)}, u32[]{:S(2)}) collective-permute-start(bf16[768,256]{1,0:T(8,128)(2,1)S(1)} %collective-permute-done.1.refs_2_), channel_id=1, source_target_pairs={{0,4},{4,0},{8,12},{12,8},{16,20},{20,16},{24,28},{28,24},{1,5},{5... | collective-permute-start | bytes 1179656 | tf_op jit(solution)/shard_map/ppermute | solution.py:42
  42.5 8.4 %copy-start.8 = (bf16[768,256]{1,0:T(8,128)(2,1)}, bf16[768,256]{1,0:T(8,128)(2,1)S(1)}, u32[]{:S(2)}) copy-start(bf16[768,256]{1,0:T(8,128)(2,1)S(1)} %collective-permute-done.refs_1_) | copy-start | bytes 1179652
  42.5 8.4 %collective-permute-start.4 = (bf16[768,256]{1,0:T(8,128)(2,1)S(1)}, bf16[768,256]{1,0:T(8,128)(2,1)S(1)}, u32[]{:S(2)}, u32[]{:S(2)}) collective-permute-start(bf16[768,256]{1,0:T(8,128)(2,1)S(1)} %collective-permute-done.refs_1_), channel_id=1, source_target_pairs={{0,4},{4,0},{8,12},{12,8},{16,20},{20,16},{24,28},{28,24},{1,5},{5... | collective-permute-start | bytes 1179656 | tf_op jit(solution)/shard_map/ppermute | solution.py:42
  45.9 14.1 %collective-permute-start.25 = (f32[176,128]{1,0:T(8,128)S(1)}, f32[176,128]{1,0:T(8,128)S(1)}, u32[]{:S(2)}, u32[]{:S(2)}) collective-permute-start(f32[176,128]{1,0:T(8,128)S(1)} %dynamic-slice_dynamic-update-slice_fusion), channel_id=1, source_target_pairs={{0,3},{1,2},{2,1},{3,0},{4,7},{5,6},{6,5},{7,4},{8,11},{9,10},{10,... | collective-permute-start | bytes 270344 | tf_op jit(solution)/shard_map/ppermute | solution.py:42
  48.4 2.6 %copy-start.9 = (bf16[768,256]{1,0:T(8,128)(2,1)}, bf16[768,256]{1,0:T(8,128)(2,1)S(1)}, u32[]{:S(2)}) copy-start(bf16[768,256]{1,0:T(8,128)(2,1)S(1)} %collective-permute-done.3.refs_4_) | copy-start | bytes 1179652
  48.4 11.7 %collective-permute-start.24 = (f32[176,128]{1,0:T(8,128)S(1)}, f32[176,128]{1,0:T(8,128)S(1)}, u32[]{:S(2)}, u32[]{:S(2)}) collective-permute-start(f32[176,128]{1,0:T(8,128)S(1)} %dynamic-slice_dynamic-update-slice_fusion), channel_id=1, source_target_pairs={{0,2},{1,3},{2,0},{3,1},{4,6},{5,7},{6,4},{7,5},{8,10},{9,11},{10,... | collective-permute-start | bytes 270344 | tf_op jit(solution)/shard_map/ppermute | solution.py:42
  48.4 2.6 %copy-start.10 = (bf16[768,256]{1,0:T(8,128)(2,1)}, bf16[768,256]{1,0:T(8,128)(2,1)S(1)}, u32[]{:S(2)}) copy-start(bf16[768,256]{1,0:T(8,128)(2,1)S(1)} %collective-permute-done.6.refs_7_) | copy-start | bytes 1179652
  48.4 11.6 %collective-permute-start.23 = (f32[176,128]{1,0:T(8,128)S(1)}, f32[176,128]{1,0:T(8,128)S(1)}, u32[]{:S(2)}, u32[]{:S(2)}) collective-permute-start(f32[176,128]{1,0:T(8,128)S(1)} %dynamic-slice_dynamic-update-slice_fusion), channel_id=1, source_target_pairs={{0,1},{1,0},{2,3},{3,2},{4,5},{5,4},{6,7},{7,6},{8,9},{9,8},{10,11... | collective-permute-start | bytes 270344 | tf_op jit(solution)/shard_map/ppermute | solution.py:42
  50.9 0.8 copy-start.11
  51.7 0.8 copy-start.12
  58.5 8.1 %collective-permute-start.7 = (f32[384,128]{1,0:T(8,128)}, f32[384,128]{1,0:T(8,128)S(1)}, u32[]{:S(2)}, u32[]{:S(2)}) collective-permute-start(f32[384,128]{1,0:T(8,128)} %get-tuple-element.18), channel_id=1, source_target_pairs={{0,8},{4,12},{8,0},{12,4},{16,24},{20,28},{24,16},{28,20},{1,9},{5... | collective-permute-start | bytes 589832 | tf_op jit(solution)/shard_map/ppermute | solution.py:42
  60.1 31.3 %collective-permute-start.27 = (f32[4,176,128]{2,1,0:T(8,128)S(1)}, f32[4,176,128]{2,1,0:T(8,128)S(1)}, u32[]{:S(2)}, u32[]{:S(2)}) collective-permute-start(f32[4,176,128]{2,1,0:T(8,128)S(1)} %get-tuple-element.34), channel_id=1, source_target_pairs={{0,16},{4,20},{8,24},{12,28},{16,0},{20,4},{24,8},{28,12},{1,17},{... | collective-permute-start | bytes 1081352 | tf_op jit(solution)/shard_map/ppermute | solution.py:42
  61.7 31.0 %collective-permute-start.26 = (f32[4,176,128]{2,1,0:T(8,128)S(1)}, f32[4,176,128]{2,1,0:T(8,128)S(1)}, u32[]{:S(2)}, u32[]{:S(2)}) collective-permute-start(f32[4,176,128]{2,1,0:T(8,128)S(1)} %get-tuple-element.34), channel_id=1, source_target_pairs={{0,8},{4,12},{8,0},{12,4},{16,24},{20,28},{24,16},{28,20},{1,9},{5... | collective-permute-start | bytes 1081352 | tf_op jit(solution)/shard_map/ppermute | solution.py:42
  62.2 30.5 %collective-permute-start.28 = (f32[4,176,128]{2,1,0:T(8,128)S(1)}, f32[4,176,128]{2,1,0:T(8,128)S(1)}, u32[]{:S(2)}, u32[]{:S(2)}) collective-permute-start(f32[4,176,128]{2,1,0:T(8,128)S(1)} %get-tuple-element.34), channel_id=1, source_target_pairs={{0,24},{4,28},{8,16},{12,20},{16,8},{20,12},{24,0},{28,4},{1,25},{... | collective-permute-start | bytes 1081352 | tf_op jit(solution)/shard_map/ppermute | solution.py:42
  63.7 22.0 %collective-permute-start.8 = (f32[384,128]{1,0:T(8,128)}, f32[384,128]{1,0:T(8,128)S(1)}, u32[]{:S(2)}, u32[]{:S(2)}) collective-permute-start(f32[384,128]{1,0:T(8,128)} %get-tuple-element.19), channel_id=1, source_target_pairs={{0,16},{4,20},{8,24},{12,28},{16,0},{20,4},{24,8},{28,12},{1,17},{... | collective-permute-start | bytes 589832 | tf_op jit(solution)/shard_map/ppermute | solution.py:42
  66.6 19.0 %copy-start.13 = (f32[384,128]{1,0:T(8,128)}, f32[384,128]{1,0:T(8,128)S(1)}, u32[]{:S(2)}) copy-start(f32[384,128]{1,0:T(8,128)S(1)} %collective-permute-done.7.refs_1_) | copy-start | bytes 589828
  66.6 19.0 %collective-permute-start.9 = (f32[384,128]{1,0:T(8,128)}, f32[384,128]{1,0:T(8,128)S(1)}, u32[]{:S(2)}, u32[]{:S(2)}) collective-permute-start(f32[384,128]{1,0:T(8,128)} %get-tuple-element.20), channel_id=1, source_target_pairs={{0,24},{4,28},{8,16},{12,20},{16,8},{20,12},{24,0},{28,4},{1,25},{... | collective-permute-start | bytes 589832 | tf_op jit(solution)/shard_map/ppermute | solution.py:42
  85.6 0.7 copy-start.14
  85.6 0.8 copy-start.15
  88.3 4.6 %collective-permute-start.10 = (f32[96,128]{1,0:T(8,128)}, f32[96,128]{1,0:T(8,128)S(1)}, u32[]{:S(2)}, u32[]{:S(2)}) collective-permute-start(f32[96,128]{1,0:T(8,128)} %get-tuple-element.22), channel_id=1, source_target_pairs={{0,1},{1,0},{2,3},{3,2},{4,5},{5,4},{6,7},{7,6},{8,9},{9,8},{10,11... | collective-permute-start | bytes 147464 | tf_op jit(solution)/shard_map/ppermute | solution.py:42
  88.8 6.3 %collective-permute-start.11 = (f32[96,128]{1,0:T(8,128)}, f32[96,128]{1,0:T(8,128)S(1)}, u32[]{:S(2)}, u32[]{:S(2)}) collective-permute-start(f32[96,128]{1,0:T(8,128)} %get-tuple-element.23), channel_id=1, source_target_pairs={{0,2},{1,3},{2,0},{3,1},{4,6},{5,7},{6,4},{7,5},{8,10},{9,11},{10,... | collective-permute-start | bytes 147464 | tf_op jit(solution)/shard_map/ppermute | solution.py:42
  91.4 6.1 %collective-permute-start.12 = (f32[96,128]{1,0:T(8,128)}, f32[96,128]{1,0:T(8,128)S(1)}, u32[]{:S(2)}, u32[]{:S(2)}) collective-permute-start(f32[96,128]{1,0:T(8,128)} %get-tuple-element.24), channel_id=1, source_target_pairs={{0,3},{1,2},{2,1},{3,0},{4,7},{5,6},{6,5},{7,4},{8,11},{9,10},{10,... | collective-permute-start | bytes 147464 | tf_op jit(solution)/shard_map/ppermute | solution.py:42
  92.7 4.7 %copy-start.16 = (f32[96,128]{1,0:T(8,128)S(1)}, f32[96,128]{1,0:T(8,128)}, u32[]{:S(2)}) copy-start(f32[96,128]{1,0:T(8,128)} %get-tuple-element.21) | copy-start | bytes 147460
  92.8 21.2 %copy-start.1 = (f32[4,4,176,128]{3,2,1,0:T(8,128)}, f32[4,4,176,128]{3,2,1,0:T(8,128)S(1)}, u32[]{:S(2)}) copy-start(f32[4,4,176,128]{3,2,1,0:T(8,128)S(1)} %pad_maximum_fusion.own) | copy-start | bytes 4325380
  92.8 21.2 %collective-permute-start.29 = (f32[4,4,176,128]{3,2,1,0:T(8,128)S(1)}, f32[4,4,176,128]{3,2,1,0:T(8,128)S(1)}, u32[]{:S(2)}, u32[]{:S(2)}) collective-permute-start(f32[4,4,176,128]{3,2,1,0:T(8,128)S(1)} %pad_maximum_fusion.own), channel_id=1, source_target_pairs={{0,4},{4,0},{8,12},{12,8},{16,20},{20,16},{24,28},{28,24},{1,5},{5... | collective-permute-start | bytes 4325384 | tf_op jit(solution)/shard_map/ppermute | solution.py:42
  97.5 6.0 %collective-permute-start.15 = (f32[96,128]{1,0:T(8,128)S(1)}, f32[96,128]{1,0:T(8,128)S(1)}, u32[]{:S(2)}, u32[]{:S(2)}) collective-permute-start(f32[96,128]{1,0:T(8,128)S(1)} %add_add_fusion), channel_id=1, source_target_pairs={{0,3},{1,2},{2,1},{3,0},{4,7},{5,6},{6,5},{7,4},{8,11},{9,10},{10,... | collective-permute-start | bytes 147464 | tf_op jit(solution)/shard_map/ppermute | solution.py:42
  98.9 5.6 %collective-permute-start.14 = (f32[96,128]{1,0:T(8,128)S(1)}, f32[96,128]{1,0:T(8,128)S(1)}, u32[]{:S(2)}, u32[]{:S(2)}) collective-permute-start(f32[96,128]{1,0:T(8,128)S(1)} %add_add_fusion), channel_id=1, source_target_pairs={{0,2},{1,3},{2,0},{3,1},{4,6},{5,7},{6,4},{7,5},{8,10},{9,11},{10,... | collective-permute-start | bytes 147464 | tf_op jit(solution)/shard_map/ppermute | solution.py:42
  98.9 5.6 %collective-permute-start.13 = (f32[96,128]{1,0:T(8,128)S(1)}, f32[96,128]{1,0:T(8,128)S(1)}, u32[]{:S(2)}, u32[]{:S(2)}) collective-permute-start(f32[96,128]{1,0:T(8,128)S(1)} %add_add_fusion), channel_id=1, source_target_pairs={{0,1},{1,0},{2,3},{3,2},{4,5},{5,4},{6,7},{7,6},{8,9},{9,8},{10,11... | collective-permute-start | bytes 147464 | tf_op jit(solution)/shard_map/ppermute | solution.py:42
  104.6 6.0 %collective-permute-start.17 = (f32[4,96,128]{2,1,0:T(8,128)S(1)}, f32[4,96,128]{2,1,0:T(8,128)S(1)}, u32[]{:S(2)}, u32[]{:S(2)}) collective-permute-start(f32[4,96,128]{2,1,0:T(8,128)S(1)} %get-tuple-element.36), channel_id=1, source_target_pairs={{0,16},{4,20},{8,24},{12,28},{16,0},{20,4},{24,8},{28,12},{1,17},{... | collective-permute-start | bytes 589832 | tf_op jit(solution)/shard_map/ppermute | solution.py:42
  106.1 5.7 %collective-permute-start.16 = (f32[4,96,128]{2,1,0:T(8,128)S(1)}, f32[4,96,128]{2,1,0:T(8,128)S(1)}, u32[]{:S(2)}, u32[]{:S(2)}) collective-permute-start(f32[4,96,128]{2,1,0:T(8,128)S(1)} %get-tuple-element.36), channel_id=1, source_target_pairs={{0,8},{4,12},{8,0},{12,4},{16,24},{20,28},{24,16},{28,20},{1,9},{5... | collective-permute-start | bytes 589832 | tf_op jit(solution)/shard_map/ppermute | solution.py:42
  106.7 7.2 %collective-permute-start.18 = (f32[4,96,128]{2,1,0:T(8,128)S(1)}, f32[4,96,128]{2,1,0:T(8,128)S(1)}, u32[]{:S(2)}, u32[]{:S(2)}) collective-permute-start(f32[4,96,128]{2,1,0:T(8,128)S(1)} %get-tuple-element.36), channel_id=1, source_target_pairs={{0,24},{4,28},{8,16},{12,20},{16,8},{20,12},{24,0},{28,4},{1,25},{... | collective-permute-start | bytes 589832 | tf_op jit(solution)/shard_map/ppermute | solution.py:42
  113.9 5.9 %copy-start.4 = (f32[4,4,96,128]{3,2,1,0:T(8,128)}, f32[4,4,96,128]{3,2,1,0:T(8,128)S(1)}, u32[]{:S(2)}) copy-start(f32[4,4,96,128]{3,2,1,0:T(8,128)S(1)} %pad_maximum_fusion.1.own) | copy-start | bytes 2359300
  113.9 5.9 %collective-permute-start.19 = (f32[4,4,96,128]{3,2,1,0:T(8,128)S(1)}, f32[4,4,96,128]{3,2,1,0:T(8,128)}, u32[]{:S(2)}, u32[]{:S(2)}) collective-permute-start(f32[4,4,96,128]{3,2,1,0:T(8,128)S(1)} %pad_maximum_fusion.1.own), channel_id=1, source_target_pairs={{0,4},{4,0},{8,12},{12,8},{16,20},{20,16},{24,28},{28,24},{1,5},{5... | collective-permute-start | bytes 2359304 | tf_op jit(solution)/shard_map/ppermute | solution.py:42
  114.0 1.2 copy-start.3

commit v2 on v1

--- a/solution.py
+++ b/solution.py
@@ -20,7 +20,10 @@
 NT = ((1,), (1,))
 f32 = jnp.float32
 bf16 = jnp.bfloat16
+f16 = jnp.float16
+SCALE = 32.0
 VMEM = pl.BlockSpec(memory_space=pltpu.VMEM)
+ANY = pl.BlockSpec(memory_space=pl.ANY)
 SMEM = pl.BlockSpec(memory_space=pltpu.SMEM)
 
 
@@ -69,14 +72,19 @@
 def diagonal_kernel(bases, out):
     per_basis = bases.shape[1] // LANES
     columns = spans(per_basis, LANES)
+    energy = jnp.zeros((SUB, LANES), f32)
     for at, (i, j) in zip(spans(len(own_tiles(per_basis)), LANES), own_tiles(per_basis)):
-        out[at] = dot(bases[:, columns[i]], bases[:, columns[j]], TN)
-
-
-def cross_kernel(at_ref, table, *refs):
-    chips = lax.axis_size("rows") // 2
+        tile = dot(bases[:, columns[i]], bases[:, columns[j]], TN)
+        out[at] = tile
+        if i == j:
+            tile = jnp.where(identity(LANES), tile, 0.0)
+            energy = energy + sum(tile[rows] for rows in spans(LANES // SUB, SUB))
+    out[at.stop :] = energy
+
+
+def cross_kernel(at_ref, table, scale, start, diagonal, *refs):
     n_batch = lax.axis_size("batch")
-    pieces, (rows, *outs, both) = refs[: 2 * n_batch], refs[2 * n_batch :]
+    pieces, (rows, message, *outs, both) = refs[: 2 * n_batch], refs[2 * n_batch :]
     chip, core, batch = at_ref[0], at_ref[1], at_ref[2]
     sub_rows, basis = pieces[0].shape
     for half in range(2):
@@ -84,6 +92,13 @@
             first = pl.multiple_of(lax.bitwise_xor(batch, offset) * basis, basis)
             both[half * sub_rows : (half + 1) * sub_rows, pl.ds(first, basis)] = pieces[half * n_batch + offset][...]
     rows[...] = both[:sub_rows]
+    index = 2 * chip + core
+    share, size = start.shape[0] // lax.axis_size("rows"), start.shape[1]
+    part = message.shape[0] - share * size // LANES
+    message[:part] = diagonal[pl.ds(pl.multiple_of(index * part, SUB), part), :]
+    for k, lanes in enumerate(spans(size // LANES, LANES)):
+        first = pl.multiple_of(index * share, SUB)
+        message[part + k * share : part + (k + 1) * share] = start[pl.ds(first, share), lanes]
     for offset, out in enumerate(outs):
         share = out.shape[0] // LANES
         owner = 2 * lax.bitwise_xor(chip, offset) + core
@@ -91,22 +106,7 @@
             place = 2 * (owner * share + j)
             left = pl.multiple_of(table[place] * LANES, LANES)
             right = pl.multiple_of(table[place + 1] * LANES, LANES)
-            out[at] = dot(both[:, pl.ds(left, LANES)], both[:, pl.ds(right, LANES)], TN)
-
-
-def share_kernel(at_ref, *refs):
-    n_batch = lax.axis_size("batch")
-    blocks, outs = refs[:-n_batch], refs[-n_batch:]
-    batch = at_ref[2]
-    height = LANES // n_batch
-    for offset, out in enumerate(outs):
-        first = pl.multiple_of(lax.bitwise_xor(batch, offset) * height, height)
-        for j, at in enumerate(spans(out.shape[0] // height, height)):
-            rows = pl.ds(j * LANES + first, height)
-            total = blocks[0][rows, :]
-            for block in blocks[1:]:
-                total = total + block[rows, :]
-            out[at] = total
+            out[at] = dot(both[:, pl.ds(left, LANES)], both[:, pl.ds(right, LANES)], TN) * scale[0]
 
 
 def spread(value, index):
@@ -180,27 +180,24 @@
     lax.fori_loop(0, size // LANES, block, 0)
 
 
-def prepare_kernel(at_ref, own, sibling, high, low, diagonal, whole):
+def prepare_kernel(at_ref, *refs):
+    *blocks, high, low, diagonal, whole = refs
     chip, core, batch = at_ref[0], at_ref[1], at_ref[2]
-    chips, n_batch, height, _ = own.shape
+    n_batch = blocks[0].shape[0]
     columns, size = whole.shape
     basis = columns // n_batch
-    share = basis // (2 * chips)
-    part = diagonal.shape[1] // (2 * chips)
-
-    def place(offset, carry):
-        for other, block in enumerate((own, sibling)):
-            row = 2 * lax.bitwise_xor(chip, offset) + lax.bitwise_xor(core, other)
-            for z in range(n_batch):
-                group = lax.bitwise_xor(batch, z)
-                diagonal[group, pl.ds(pl.multiple_of(row * part, SUB), part), :] = block[offset, z, :part, :]
-                first = pl.multiple_of(group * basis + row * share, SUB)
-                for k, lanes in enumerate(spans(size // LANES, LANES)):
-                    lower = part + k * share
-                    whole[pl.ds(first, share), lanes] = block[offset, z, lower : lower + share, :]
-        return carry
-
-    lax.fori_loop(0, chips, place, 0)
+    share = basis // len(blocks)
+    part = diagonal.shape[1] // len(blocks)
+    for k, block in enumerate(blocks):
+        other, offset = divmod(k, len(blocks) // 2)
+        row = 2 * lax.bitwise_xor(chip, offset) + lax.bitwise_xor(core, other)
+        for z in range(n_batch):
+            group = lax.bitwise_xor(batch, z)
+            diagonal[group, pl.ds(pl.multiple_of(row * part, SUB), part), :] = block[z, :part, :]
+            first = pl.multiple_of(group * basis + row * share, SUB)
+            for k, lanes in enumerate(spans(size // LANES, LANES)):
+                lower = part + k * share
+                whole[pl.ds(first, share), lanes] = block[z, lower : lower + share, :]
     for rows in spans(columns // LANES, LANES):
         high[:, rows], low[:, rows] = split(whole[rows, :].T)
 
@@ -215,29 +212,26 @@
     return jnp.sum(total)
 
 
-def place_gram(at_ref, table, own, sibling, diagonal, factor, pair):
-    chip, core, batch = at_ref[0], at_ref[1], at_ref[2]
-    chips, n_batch, share_rows, _ = own.shape
-    height = LANES // n_batch
-    share = share_rows // height
+def place_gram(at_ref, table, cross, diagonal, factor, pair):
+    chip, core = at_ref[0], at_ref[1]
+    devices, share_rows, _ = cross.shape
+    share = share_rows // LANES
+    n_batch = diagonal.shape[0]
     per_basis = pair[0].shape[0] // LANES // n_batch
 
-    def place(offset, carry):
-        for other, block in enumerate((own, sibling)):
-            owner = 2 * lax.bitwise_xor(chip, offset) + lax.bitwise_xor(core, other)
-            for j, inner in enumerate(spans(share, height)):
-                at = 2 * (owner * share + j)
-                row = pl.multiple_of(table[at] * LANES, LANES)
-                column = pl.multiple_of(table[at + 1] * LANES, LANES)
-                for z in range(n_batch):
-                    first = pl.multiple_of(row + lax.bitwise_xor(batch, z) * height, height)
-                    for ref, value in zip(pair, split(block[offset, z, inner, :] * factor)):
-                        ref[pl.ds(first, height), pl.ds(column, LANES)] = value
-                for ref in pair:
-                    ref[pl.ds(column, LANES), pl.ds(row, LANES)] = ref[pl.ds(row, LANES), pl.ds(column, LANES)].T
+    def place(k, carry):
+        other, offset = k // (devices // 2), lax.rem(k, devices // 2)
+        owner = 2 * lax.bitwise_xor(chip, offset) + lax.bitwise_xor(core, other)
+        for j, inner in enumerate(spans(share, LANES)):
+            at = 2 * (owner * share + j)
+            row = pl.ds(pl.multiple_of(table[at] * LANES, LANES), LANES)
+            column = pl.ds(pl.multiple_of(table[at + 1] * LANES, LANES), LANES)
+            for ref, value in zip(pair, split(cross[k, inner, :] * (1.0 / SCALE))):
+                ref[row, column] = value
+                ref[column, row] = value.T
         return carry
 
-    lax.fori_loop(0, chips, place, 0)
+    lax.fori_loop(0, devices, place, 0)
     for group in range(n_batch):
         for at, (i, j) in zip(spans(len(own_tiles(per_basis)), LANES), own_tiles(per_basis)):
             rows, columns = (slice((group * per_basis + k) * LANES, (group * per_basis + k + 1) * LANES) for k in (i, j))
@@ -247,12 +241,12 @@
                     ref[columns, rows] = value.T
 
 
-def solve_kernel(at_ref, table, own, sibling, diagonal, sh, sl, rows, modes, ah, al, ph, plo, qh, ql, a, e, x, work):
+def solve_kernel(at_ref, table, cross, diagonal, sh, sl, rows, modes, ah, al, ph, plo, qh, ql, a, e, x, work):
     size, columns = sh.shape
-    per_basis = columns // LANES // own.shape[1]
+    per_basis = columns // LANES // diagonal.shape[0]
     gram, p, q = (ah, al), (ph, plo), (qh, ql)
     factor = 1.0 / (trace_of(diagonal, per_basis) / columns)
-    place_gram(at_ref, table, own, sibling, diagonal, factor, gram)
+    place_gram(at_ref, table, cross, diagonal, factor, gram)
 
     def lift(source, target):
         def chunk(n, carry):
@@ -335,16 +329,19 @@
     table = jnp.asarray([k for tile in tiles for k in tile], jnp.int32)
     other_batches, other_chips = range(1, n_batch), range(2, n_rows, 2)
 
-    def call(kernel, outs, scratch, *args, n_smem=0, flops=0, moved=1 << 20):
+    def call(kernel, outs, scratch, *args, n_smem=0, flops=0, moved=1 << 20, after=()):
+        def body(*refs):
+            kernel(*refs[: len(args)], *refs[len(args) + len(after) :])
+
         return pl.pallas_call(
-            kernel,
+            body,
             out_shape=[jax.ShapeDtypeStruct(shape, dtype) for shape, dtype in outs],
-            in_specs=[SMEM] * n_smem + [VMEM] * (len(args) - n_smem),
+            in_specs=[SMEM] * n_smem + [VMEM] * (len(args) - n_smem) + [ANY] * len(after),
             out_specs=[VMEM] * len(outs),
             scratch_shapes=[pltpu.VMEM(shape, dtype) for shape, dtype in scratch],
             compiler_params=pltpu.CompilerParams(vmem_limit_bytes=60 << 20),
             cost_estimate=pl.CostEstimate(flops=flops, bytes_accessed=moved, transcendentals=0),
-        )(*args)
+        )(*args, *after)
 
     pieces = []
     for offset in range(n_batch):
@@ -354,37 +351,45 @@
 
     own_count = len(own_tiles(per_basis))
     (diagonal,) = call(
-        diagonal_kernel, [((own_count * LANES, LANES), f32)], [], bases,
-        flops=2 * local_rows * own_count * LANES * LANES, moved=bases.size * 2,
+        diagonal_kernel, [((own_count * LANES + SUB, LANES), f32)], [], bases,
+        flops=2 * local_rows * own_count * LANES * LANES, moved=bases.size * 2, after=other_pieces[:1],
     )
     for offset in (1 << k for k in range(n_rows.bit_length() - 1)):
         diagonal = diagonal + swap(diagonal, "rows", offset)
+    energy = diagonal[own_count * LANES :]
+    for offset in (1 << k for k in range(n_batch.bit_length() - 1)):
+        energy = energy + swap(energy, "batch", offset)
+    scale = (SCALE * columns / jnp.sum(energy)).reshape(1)
+
     part = own_count * LANES // n_rows
-    start_share = start.shape[0] // n_rows
-    mine = lax.dynamic_slice_in_dim(start, row * start_share, start_share, 0)
-    mine = [lax.dynamic_slice_in_dim(diagonal, row * part, part, 0)] + jnp.split(mine, size // LANES, axis=1)
-    mine = spread_copy(jnp.concatenate(mine), "batch", other_batches)
-    mine = spread_copy(mine, "rows", other_chips)
+    message_rows = part + start.size // n_rows // LANES
+    rows, mine, *blocks = call(
+        cross_kernel,
+        [((sub_rows, columns), bf16), ((message_rows, LANES), f32)] + [((share * LANES, LANES), f32)] * chips,
+        [((2 * sub_rows, columns), bf16)],
+        at, table, scale, start, diagonal, *pieces, *other_pieces, n_smem=3,
+        flops=4 * sub_rows * chips * share * LANES * LANES, moved=6 << 20,
+    )
+    plane = blocks[0]
+    for block, offset in zip(blocks[1:], other_chips):
+        plane = plane + swap(block.astype(f16), "rows", offset).astype(f32)
+    plane = plane.astype(f16)
+    total = plane.astype(f32)
+    for offset in other_batches:
+        total = total + swap(plane, "batch", offset).astype(f32)
+    total = total.astype(f16)
+
+    mine = spread_copy(mine, "batch", other_batches)
+    mine = [mine] + [swap(mine, "rows", offset) for offset in other_chips]
     high, low, diagonal = call(
         prepare_kernel,
         [((size, columns), bf16)] * 2 + [((n_batch, own_count * LANES, LANES), f32)],
         [((columns, size), f32)],
-        at, mine, swap(mine, "rows", 1), n_smem=1, moved=8 << 20,
+        at, *mine, *(swap(block, "rows", 1) for block in mine), n_smem=1, moved=8 << 20,
     )
 
-    rows, *blocks = call(
-        cross_kernel,
-        [((sub_rows, columns), bf16)] + [((share * LANES, LANES), f32)] * chips,
-        [((2 * sub_rows, columns), bf16)],
-        at, table, *pieces, *other_pieces, n_smem=2,
-        flops=4 * sub_rows * chips * share * LANES * LANES, moved=6 << 20,
-    )
-    blocks = [blocks[0]] + [swap(block, "rows", offset) for block, offset in zip(blocks[1:], other_chips)]
-    height = LANES // n_batch
-    parts = call(share_kernel, [((share * height, LANES), f32)] * n_batch, [], at, *blocks, n_smem=1)
-    total = sum((swap(parts[offset], "batch", offset) for offset in other_batches), parts[0])
-
-    own = spread_copy(spread_copy(total, "batch", other_batches), "rows", other_chips)
+    cross = [total] + [swap(total, "rows", offset) for offset in other_chips]
+    cross = jnp.stack(cross + [swap(block, "rows", 1) for block in cross]).astype(f32)
     (modes,) = call(
         solve_kernel,
         [((sub_rows, size), bf16)],
@@ -392,7 +397,7 @@
         + [((size, columns), bf16)] * 4
         + [((size, size), f32)] * 3
         + [((LANES, 2 * LANES), f32)],
-        at, table, own, swap(own, "rows", 1), diagonal, high, low, rows, n_smem=2, flops=10**10, moved=10 << 20,
+        at, table, cross, diagonal, high, low, rows, n_smem=2, flops=10**10, moved=10 << 20,
     )
     return modes
 

time: 158 us -> 170 us (1.076)
  waiting for transfers between devices: 61.1 us -> 69.7 us
  other arithmetic: 0.89 us -> 7.51 us
  Pallas kernels: 53.7 us -> 50.8 us
    ppermute x30 -> x35, waiting for transfers between devices: 61.1 us -> 69.7 us  [swap(): return lax.ppermute(value, axis, [(i, i ^ offset) for i in range(size)])]
    convert_element_type x0 -> x5, other arithmetic: none -> 5.11 us  [the longest x3 2.86 us: on_device(): plane = plane + swap(block.astype(f16), 'rows', offset).astype(f32)]
    pallas_call x5 -> x4, Pallas kernels: 53.7 us -> 50.8 us  [call(): pl.pallas_call(body, out_shape=[jax.ShapeDtypeStruct(shape, dtype) for sh...]
    unnamed x37 -> x42, local copies, waits for them, and re-layouts: 5.67 us -> 3.5 us
    ppermute x30 -> x35, starting transfers between devices: 35.5 us -> 35.3 us  [swap(): return lax.ppermute(value, axis, [(i, i ^ offset) for i in range(size)])]
  transfers between devices with their start and end apart: 30 -> 35, of which waited for: 12 -> 21; matrix products, arithmetic and copies ran while one was open for 2% -> 2% of each run, Pallas kernels for 8% -> 0%
where the time goes in v2:
time: 170 us; the launch traced here: 169 us
  waiting for transfers between devices  69.7 us (41%)
  Pallas kernels  50.8 us (30%)
  starting transfers between devices  35.3 us (21%)
  other arithmetic  7.51 us (4%)
  local copies, waits for them, and re-layouts  4.99 us (3%)
    ppermute x35, waiting for transfers between devices, swap(): return lax.ppermute(value, axis, [(i, i ^ offset) for i in range(size)])  69.7 us
    pallas_call x4, Pallas kernels, call(): pl.pallas_call(body, out_shape=[jax.ShapeDtypeStruct(shape, dtype) for sh...  50.8 us
    ppermute x35, starting transfers between devices, swap(): return lax.ppermute(value, axis, [(i, i ^ offset) for i in range(size)])  35.3 us
    unnamed x42, local copies, waits for them, and re-layouts  3.5 us
  transfers between devices with their start and end apart: 35, of which 21 were waited for; matrix products, arithmetic and copies ran while one was open for 2% of the time, Pallas kernels for 0%

profile of v2, /device:TPU:0, one launch (start us, length us, event | category | flops | bytes accessed | tf_op | source)
XLA Modules:
  0.0 169.3 jit_solution(18222835675228646721)
XLA Ops:
  0.0 1.5 constant_dynamic-slice_fusion
  1.5 0.5 collective-permute-start
  2.0 1.3 collective-permute-done.refs_1_.refs_9_
  3.3 0.7 copy-done.1
  4.1 2.9 %shard_map.37 = f32[392,128]{1,0:T(8,128)} custom-call(bf16[3072,256]{1,0:T(8,128)(2,1)} %refs_0_.1, bf16[768,256]{1,0:T(8,128)(2,1)} %copy-done.1), custom_call_target="tpu_custom_call" | custom-call | flops 301989888 | bytes 1572864 | tf_op jit(solution)/shard_map/pallas_call | solution.py:336
  7.0 0.4 collective-permute-start.1
  7.4 1.3 collective-permute-done.1
  8.7 0.9 add.52
  9.6 2.9 %collective-permute-start.2 = (f32[392,128]{1,0:T(8,128)S(1)}, f32[392,128]{1,0:T(8,128)S(1)}, u32[]{:S(2)}, u32[]{:S(2)}) collective-permute-start(f32[392,128]{1,0:T(8,128)S(1)} %add.52), channel_id=1, source_target_pairs={{0,8},{4,12},{8,0},{12,4},{16,24},{20,28},{24,16},{28,20},{1,9},{5... | collective-permute-start | bytes 602120 | tf_op jit(solution)/shard_map/ppermute | solution.py:45
  12.5 3.6 %collective-permute-start.8 = (bf16[768,256]{1,0:T(8,128)(2,1)S(1)}, bf16[768,256]{1,0:T(8,128)(2,1)S(1)}, u32[]{:S(2)}, u32[]{:S(2)}) collective-permute-start(bf16[768,256]{1,0:T(8,128)(2,1)S(1)} %get-tuple-element.25), channel_id=1, source_target_pairs={{0,3},{1,2},{2,1},{3,0},{4,7},{5,6},{6,5},{7,4},{8,11},{9,10},{10,... | collective-permute-start | bytes 1179656 | tf_op jit(solution)/shard_map/ppermute | solution.py:45
  16.1 0.8 collective-permute-start.7
  16.9 0.9 collective-permute-done.2
  17.9 1.8 %collective-permute-start.3 = (f32[392,128]{1,0:T(8,128)S(1)}, f32[392,128]{1,0:T(8,128)S(1)}, u32[]{:S(2)}, u32[]{:S(2)}) collective-permute-start(f32[392,128]{1,0:T(8,128)S(1)} %add.53), channel_id=1, source_target_pairs={{0,16},{4,20},{8,24},{12,28},{16,0},{20,4},{24,8},{28,12},{1,17},{... | collective-permute-start | bytes 602120 | tf_op jit(solution)/shard_map/ppermute | solution.py:45
  19.7 4.8 %collective-permute-done.3 = f32[392,128]{1,0:T(8,128)S(1)} collective-permute-done((f32[392,128]{1,0:T(8,128)S(1)}, f32[392,128]{1,0:T(8,128)S(1)}, u32[]{:S(2)}, u32[]{:S(2)}) %collective-permute-start.3) | collective-permute-done | bytes 200736 | tf_op jit(solution)/shard_map/ppermute | solution.py:45
  24.5 1.6 collective-permute-start.4
  26.1 0.3 collective-permute-done.8.refs_8_
  26.4 8.4 %collective-permute-done.6.refs_6_ = bf16[768,256]{1,0:T(8,128)(2,1)S(1)} collective-permute-done((bf16[768,256]{1,0:T(8,128)(2,1)S(1)}, bf16[768,256]{1,0:T(8,128)(2,1)S(1)}, u32[]{:S(2)}, u32[]{:S(2)}) %collective-permute-start.6) | collective-permute-done | bytes 393248 | tf_op jit(solution)/shard_map/ppermute | solution.py:45
  34.8 14.9 %collective-permute-done.7.refs_7_ = bf16[768,256]{1,0:T(8,128)(2,1)S(1)} collective-permute-done((bf16[768,256]{1,0:T(8,128)(2,1)S(1)}, bf16[768,256]{1,0:T(8,128)(2,1)S(1)}, u32[]{:S(2)}, u32[]{:S(2)}) %collective-permute-start.7) | collective-permute-done | bytes 393248 | tf_op jit(solution)/shard_map/ppermute | solution.py:45
  49.8 0.7 pad_add_fusion.refs_0_
  50.5 3.8 %collective-permute-done.5 = f32[8,128]{1,0:T(8,128)S(1)} collective-permute-done((f32[8,128]{1,0:T(8,128)S(1)}, f32[8,128]{1,0:T(8,128)S(1)}, u32[]{:S(2)}, u32[]{:S(2)}) %collective-permute-start.5) | collective-permute-done | bytes 4128 | tf_op jit(solution)/shard_map/ppermute | solution.py:45
  54.3 0.7 add_reduce_fusion
  55.7 0.7 copy-done.7
  56.7 6.4 %shard_map.38 = (bf16[768,1024]{1,0:T(8,128)(2,1)}, f32[176,128]{1,0:T(8,128)}, f32[384,128]{1,0:T(8,128)}, f32[384,128]{1,0:T(8,128)}, f32[384,128]{1,0:T(8,128)}, /*index=5*/f32[384,128]{1,0:T(8,128)}) custom-call(s32[3]{0:T(128)} %pad_add_fusion.refs_0_, s32[48]{0:T(128)} %constant.47.clone.refs_1_, f32[1]{0:T(128)} %bitcast.3.refs_2_, ...), custom_call_target="tpu_custom_call" | custom-call | flops 603979776 | bytes 6291456 | tf_op jit(solution)/shard_map/pallas_call | solution.py:336
  63.1 1.0 convert_element_type.39
  64.1 0.9 convert_element_type.41
  65.1 0.9 convert_element_type.43
  66.0 1.6 collective-permute-start.14
  67.6 0.5 collective-permute-start.13
  68.1 1.5 collective-permute-start.12
  69.6 3.0 %collective-permute-done.14 = f16[384,128]{1,0:T(8,128)(2,1)S(1)} collective-permute-done((f16[384,128]{1,0:T(8,128)(2,1)S(1)}, f16[384,128]{1,0:T(8,128)(2,1)S(1)}, u32[]{:S(2)}, u32[]{:S(2)}) %collective-permute-start.14) | collective-permute-done | bytes 98336 | tf_op jit(solution)/shard_map/ppermute | solution.py:45
  72.6 0.5 collective-permute-done.13
  73.2 1.0 add_convert_fusion.1
  74.2 2.5 %collective-permute-start.17 = (f16[384,128]{1,0:T(8,128)(2,1)S(1)}, f16[384,128]{1,0:T(8,128)(2,1)S(1)}, u32[]{:S(2)}, u32[]{:S(2)}) collective-permute-start(f16[384,128]{1,0:T(8,128)(2,1)S(1)} %add_convert_fusion.1), channel_id=1, source_target_pairs={{0,3},{1,2},{2,1},{3,0},{4,7},{5,6},{6,5},{7,4},{8,11},{9,10},{10,... | collective-permute-start | bytes 294920 | tf_op jit(solution)/shard_map/ppermute | solution.py:45
  76.7 1.9 %collective-permute-start.15 = (f16[384,128]{1,0:T(8,128)(2,1)S(1)}, f16[384,128]{1,0:T(8,128)(2,1)S(1)}, u32[]{:S(2)}, u32[]{:S(2)}) collective-permute-start(f16[384,128]{1,0:T(8,128)(2,1)S(1)} %add_convert_fusion.1), channel_id=1, source_target_pairs={{0,1},{1,0},{2,3},{3,2},{4,5},{5,4},{6,7},{7,6},{8,9},{9,8},{10,11... | collective-permute-start | bytes 294920 | tf_op jit(solution)/shard_map/ppermute | solution.py:45
  78.6 2.5 %collective-permute-start.27 = (f32[176,128]{1,0:T(8,128)}, f32[176,128]{1,0:T(8,128)S(1)}, u32[]{:S(2)}, u32[]{:S(2)}) collective-permute-start(f32[176,128]{1,0:T(8,128)} %get-tuple-element.18), channel_id=1, source_target_pairs={{0,3},{1,2},{2,1},{3,0},{4,7},{5,6},{6,5},{7,4},{8,11},{9,10},{10,... | collective-permute-start | bytes 270344 | tf_op jit(solution)/shard_map/ppermute | solution.py:45
  81.1 0.6 collective-permute-done.17
  81.7 3.8 %collective-permute-start.25 = (f32[176,128]{1,0:T(8,128)}, f32[176,128]{1,0:T(8,128)S(1)}, u32[]{:S(2)}, u32[]{:S(2)}) collective-permute-start(f32[176,128]{1,0:T(8,128)} %get-tuple-element.18), channel_id=1, source_target_pairs={{0,1},{1,0},{2,3},{3,2},{4,5},{5,4},{6,7},{7,6},{8,9},{9,8},{10,11... | collective-permute-start | bytes 270344 | tf_op jit(solution)/shard_map/ppermute | solution.py:45
  85.5 3.8 %collective-permute-done.16 = f16[384,128]{1,0:T(8,128)(2,1)S(1)} collective-permute-done((f16[384,128]{1,0:T(8,128)(2,1)S(1)}, f16[384,128]{1,0:T(8,128)(2,1)S(1)}, u32[]{:S(2)}, u32[]{:S(2)}) %collective-permute-start.16) | collective-permute-done | bytes 98336 | tf_op jit(solution)/shard_map/ppermute | solution.py:45
  89.4 1.4 collective-permute-start.18
  90.7 1.4 collective-permute-done.26
  92.3 1.7 %collective-permute-start.30 = (f32[4,176,128]{2,1,0:T(8,128)S(1)}, f32[4,176,128]{2,1,0:T(8,128)S(1)}, u32[]{:S(2)}, u32[]{:S(2)}) collective-permute-start(f32[4,176,128]{2,1,0:T(8,128)S(1)} %pad_maximum_fusion.refs_1_), channel_id=1, source_target_pairs={{0,24},{4,28},{8,16},{12,20},{16,8},{20,12},{24,0},{28,4},{1,25},{... | collective-permute-start | bytes 1081352 | tf_op jit(solution)/shard_map/ppermute | solution.py:45
  94.0 1.1 collective-permute-start.29
  95.2 0.7 collective-permute-start.28
  95.9 1.3 collective-permute-start.19
  97.2 16.6 %collective-permute-done.19 = f16[384,128]{1,0:T(8,128)(2,1)S(1)} collective-permute-done((f16[384,128]{1,0:T(8,128)(2,1)S(1)}, f16[384,128]{1,0:T(8,128)(2,1)S(1)}, u32[]{:S(2)}, u32[]{:S(2)}) %collective-permute-start.19) | collective-permute-done | bytes 98336 | tf_op jit(solution)/shard_map/ppermute | solution.py:45
  113.9 1.6 collective-permute-start.20
  115.6 4.0 %collective-permute-done.20 = f16[384,128]{1,0:T(8,128)(2,1)S(1)} collective-permute-done((f16[384,128]{1,0:T(8,128)(2,1)S(1)}, f16[384,128]{1,0:T(8,128)(2,1)S(1)}, u32[]{:S(2)}, u32[]{:S(2)}) %collective-permute-start.20) | collective-permute-done | bytes 98336 | tf_op jit(solution)/shard_map/ppermute | solution.py:45
  119.5 1.3 collective-permute-done.21
  120.8 0.2 collective-permute-start.22
  121.0 1.1 collective-permute-done.22
  122.1 0.2 collective-permute-start.23
  122.3 1.1 collective-permute-done.23
  123.4 0.2 collective-permute-start.24
  123.6 0.4 collective-permute-start.34
  123.9 0.2 collective-permute-start.33
  124.1 0.4 collective-permute-start.32
  124.5 0.2 collective-permute-done.24
  124.8 1.3 convert_element_type.51.refs_2_
  126.1 0.2 collective-permute-done.32.refs_6_
  126.3 0.5 copy-done.10
  126.9 0.2 copy-done.15
  127.1 0.8 copy-done.16
  127.8 4.3 %shard_map.39 = (bf16[512,1024]{1,0:T(8,128)(2,1)}, bf16[512,1024]{1,0:T(8,128)(2,1)}, f32[4,384,128]{2,1,0:T(8,128)}) custom-call(s32[3]{0:T(128)} %pad_add_fusion.refs_0_, f32[4,176,128]{2,1,0:T(8,128)} %copy-done.2, f32[4,176,128]{2,1,0:T(8,128)} %copy-done.13, f32[4,176,128]{2,1,0:T(8,128)} %copy-done.12, f32[4,176,128]{2,1,0:T(8,128)} %copy-done.11, ...), custom_call_target="tpu_custom_call" | custom-call | bytes 8388608 | tf_op jit(solution)/shard_map/pallas_call | solution.py:336
  132.1 37.2 %shard_map.40 = bf16[768,512]{1,0:T(8,128)(2,1)} custom-call(s32[3]{0:T(128)} %pad_add_fusion.refs_0_, s32[48]{0:T(128)} %constant.47.clone.refs_1_, f32[8,384,128]{2,1,0:T(8,128)} %convert_element_type.51.refs_2_, f32[4,384,128]{2,1,0:T(8,128)} %get-tuple-element.19.refs_3_, bf16[512,1024]{1,0:T(8,128)(2,1)} %get-tuple-element.20.refs_4_, ...), custom_call_target="tpu_custom_call" | custom-call | flops 10000000000 | bytes 10485760 | tf_op jit(solution)/shard_map/pallas_call | solution.py:336
  (68 shorter events, 1.1 us)
Async XLA Ops:
  1.5 16.4 %copy-start = (bf16[768,256]{1,0:T(8,128)(2,1)}, bf16[768,256]{1,0:T(8,128)(2,1)S(1)}, u32[]{:S(2)}) copy-start(bf16[768,256]{1,0:T(8,128)(2,1)S(1)} %get-tuple-element.27.refs_5_) | copy-start | bytes 1179652
  1.5 1.9 %collective-permute-start = (bf16[768,256]{1,0:T(8,128)(2,1)S(1)}, bf16[768,256]{1,0:T(8,128)(2,1)S(1)}, u32[]{:S(2)}, u32[]{:S(2)}) collective-permute-start(bf16[768,256]{1,0:T(8,128)(2,1)S(1)} %get-tuple-element.27.refs_5_), channel_id=1, source_target_pairs={{0,4},{4,0},{8,12},{12,8},{16,20},{20,16},{24,28},{28,24},{1,5},{5... | collective-permute-start | bytes 1179656 | tf_op jit(solution)/shard_map/ppermute | solution.py:45
  3.3 0.7 copy-start.1
  7.0 1.7 collective-permute-start.1
  9.6 8.2 %collective-permute-start.2 = (f32[392,128]{1,0:T(8,128)S(1)}, f32[392,128]{1,0:T(8,128)S(1)}, u32[]{:S(2)}, u32[]{:S(2)}) collective-permute-start(f32[392,128]{1,0:T(8,128)S(1)} %add.52), channel_id=1, source_target_pairs={{0,8},{4,12},{8,0},{12,4},{16,24},{20,28},{24,16},{28,20},{1,9},{5... | collective-permute-start | bytes 602120 | tf_op jit(solution)/shard_map/ppermute | solution.py:45
  12.5 13.8 %collective-permute-start.8 = (bf16[768,256]{1,0:T(8,128)(2,1)S(1)}, bf16[768,256]{1,0:T(8,128)(2,1)S(1)}, u32[]{:S(2)}, u32[]{:S(2)}) collective-permute-start(bf16[768,256]{1,0:T(8,128)(2,1)S(1)} %get-tuple-element.25), channel_id=1, source_target_pairs={{0,3},{1,2},{2,1},{3,0},{4,7},{5,6},{6,5},{7,4},{8,11},{9,10},{10,... | collective-permute-start | bytes 1179656 | tf_op jit(solution)/shard_map/ppermute | solution.py:45
  16.1 18.6 %collective-permute-start.6 = (bf16[768,256]{1,0:T(8,128)(2,1)S(1)}, bf16[768,256]{1,0:T(8,128)(2,1)S(1)}, u32[]{:S(2)}, u32[]{:S(2)}) collective-permute-start(bf16[768,256]{1,0:T(8,128)(2,1)S(1)} %get-tuple-element.26), channel_id=1, source_target_pairs={{0,1},{1,0},{2,3},{3,2},{4,5},{5,4},{6,7},{7,6},{8,9},{9,8},{10,11... | collective-permute-start | bytes 1179656 | tf_op jit(solution)/shard_map/ppermute | solution.py:45
  16.1 33.6 %collective-permute-start.7 = (bf16[768,256]{1,0:T(8,128)(2,1)S(1)}, bf16[768,256]{1,0:T(8,128)(2,1)S(1)}, u32[]{:S(2)}, u32[]{:S(2)}) collective-permute-start(bf16[768,256]{1,0:T(8,128)(2,1)S(1)} %get-tuple-element.28), channel_id=1, source_target_pairs={{0,2},{1,3},{2,0},{3,1},{4,6},{5,7},{6,4},{7,5},{8,10},{9,11},{10,... | collective-permute-start | bytes 1179656 | tf_op jit(solution)/shard_map/ppermute | solution.py:45
  17.9 6.6 %collective-permute-start.3 = (f32[392,128]{1,0:T(8,128)S(1)}, f32[392,128]{1,0:T(8,128)S(1)}, u32[]{:S(2)}, u32[]{:S(2)}) collective-permute-start(f32[392,128]{1,0:T(8,128)S(1)} %add.53), channel_id=1, source_target_pairs={{0,16},{4,20},{8,24},{12,28},{16,0},{20,4},{24,8},{28,12},{1,17},{... | collective-permute-start | bytes 602120 | tf_op jit(solution)/shard_map/ppermute | solution.py:45
  24.5 31.2 %copy-start.3 = (f32[392,128]{1,0:T(8,128)}, f32[392,128]{1,0:T(8,128)S(1)}, u32[]{:S(2)}) copy-start(f32[392,128]{1,0:T(8,128)S(1)} %add.54.refs_4_) | copy-start | bytes 602116
  24.5 25.2 %collective-permute-start.4 = (f32[8,128]{1,0:T(8,128)S(1)}, f32[8,128]{1,0:T(8,128)S(1)}, u32[]{:S(2)}, u32[]{:S(2)}) collective-permute-start(f32[8,128]{1,0:T(8,128)S(1)} %slice.4), channel_id=1, source_target_pairs={{0,1},{1,0},{2,3},{3,2},{4,5},{5,4},{6,7},{7,6},{8,9},{9,8},{10,11... | collective-permute-start | bytes 12296 | tf_op jit(solution)/shard_map/ppermute | solution.py:45
  26.4 29.3 %copy-start.4 = (bf16[768,256]{1,0:T(8,128)(2,1)}, bf16[768,256]{1,0:T(8,128)(2,1)S(1)}, u32[]{:S(2)}) copy-start(bf16[768,256]{1,0:T(8,128)(2,1)S(1)} %collective-permute-done.8.refs_8_) | copy-start | bytes 1179652
  26.4 29.3 %collective-permute-start.11 = (bf16[768,256]{1,0:T(8,128)(2,1)S(1)}, bf16[768,256]{1,0:T(8,128)(2,1)S(1)}, u32[]{:S(2)}, u32[]{:S(2)}) collective-permute-start(bf16[768,256]{1,0:T(8,128)(2,1)S(1)} %collective-permute-done.8.refs_8_), channel_id=1, source_target_pairs={{0,4},{4,0},{8,12},{12,8},{16,20},{20,16},{24,28},{28,24},{1,5},{5... | collective-permute-start | bytes 1179656 | tf_op jit(solution)/shard_map/ppermute | solution.py:45
  34.8 20.9 %copy-start.5 = (bf16[768,256]{1,0:T(8,128)(2,1)}, bf16[768,256]{1,0:T(8,128)(2,1)S(1)}, u32[]{:S(2)}) copy-start(bf16[768,256]{1,0:T(8,128)(2,1)S(1)} %collective-permute-done.6.refs_6_) | copy-start | bytes 1179652
  34.8 20.9 %collective-permute-start.9 = (bf16[768,256]{1,0:T(8,128)(2,1)S(1)}, bf16[768,256]{1,0:T(8,128)(2,1)S(1)}, u32[]{:S(2)}, u32[]{:S(2)}) collective-permute-start(bf16[768,256]{1,0:T(8,128)(2,1)S(1)} %collective-permute-done.6.refs_6_), channel_id=1, source_target_pairs={{0,4},{4,0},{8,12},{12,8},{16,20},{20,16},{24,28},{28,24},{1,5},{5... | collective-permute-start | bytes 1179656 | tf_op jit(solution)/shard_map/ppermute | solution.py:45
  49.7 6.0 %copy-start.6 = (bf16[768,256]{1,0:T(8,128)(2,1)}, bf16[768,256]{1,0:T(8,128)(2,1)S(1)}, u32[]{:S(2)}) copy-start(bf16[768,256]{1,0:T(8,128)(2,1)S(1)} %collective-permute-done.7.refs_7_) | copy-start | bytes 1179652
  49.7 6.0 %collective-permute-start.10 = (bf16[768,256]{1,0:T(8,128)(2,1)S(1)}, bf16[768,256]{1,0:T(8,128)(2,1)S(1)}, u32[]{:S(2)}, u32[]{:S(2)}) collective-permute-start(bf16[768,256]{1,0:T(8,128)(2,1)S(1)} %collective-permute-done.7.refs_7_), channel_id=1, source_target_pairs={{0,4},{4,0},{8,12},{12,8},{16,20},{20,16},{24,28},{28,24},{1,5},{5... | collective-permute-start | bytes 1179656 | tf_op jit(solution)/shard_map/ppermute | solution.py:45
  49.7 4.6 %collective-permute-start.5 = (f32[8,128]{1,0:T(8,128)S(1)}, f32[8,128]{1,0:T(8,128)S(1)}, u32[]{:S(2)}, u32[]{:S(2)}) collective-permute-start(f32[8,128]{1,0:T(8,128)S(1)} %slice_add_fusion), channel_id=1, source_target_pairs={{0,2},{1,3},{2,0},{3,1},{4,6},{5,7},{6,4},{7,5},{8,10},{9,11},{10,... | collective-permute-start | bytes 12296 | tf_op jit(solution)/shard_map/ppermute | solution.py:45
  55.6 0.8 copy-start.7
  55.7 0.9 copy-start.8
  55.7 1.0 copy-start.9
  63.1 29.1 %copy-start.17 = (f32[176,128]{1,0:T(8,128)S(1)}, f32[176,128]{1,0:T(8,128)}, u32[]{:S(2)}) copy-start(f32[176,128]{1,0:T(8,128)} %get-tuple-element.18) | copy-start | bytes 270340
  66.0 6.6 %collective-permute-start.14 = (f16[384,128]{1,0:T(8,128)(2,1)S(1)}, f16[384,128]{1,0:T(8,128)(2,1)S(1)}, u32[]{:S(2)}, u32[]{:S(2)}) collective-permute-start(f16[384,128]{1,0:T(8,128)(2,1)S(1)} %convert_element_type.43), channel_id=1, source_target_pairs={{0,24},{4,28},{8,16},{12,20},{16,8},{20,12},{24,0},{28,4},{1,25},{... | collective-permute-start | bytes 294920 | tf_op jit(solution)/shard_map/ppermute | solution.py:45
  67.6 5.5 %collective-permute-start.13 = (f16[384,128]{1,0:T(8,128)(2,1)S(1)}, f16[384,128]{1,0:T(8,128)(2,1)S(1)}, u32[]{:S(2)}, u32[]{:S(2)}) collective-permute-start(f16[384,128]{1,0:T(8,128)(2,1)S(1)} %convert_element_type.41), channel_id=1, source_target_pairs={{0,16},{4,20},{8,24},{12,28},{16,0},{20,4},{24,8},{28,12},{1,17},{... | collective-permute-start | bytes 294920 | tf_op jit(solution)/shard_map/ppermute | solution.py:45
  68.1 5.1 %collective-permute-start.12 = (f16[384,128]{1,0:T(8,128)(2,1)S(1)}, f16[384,128]{1,0:T(8,128)(2,1)S(1)}, u32[]{:S(2)}, u32[]{:S(2)}) collective-permute-start(f16[384,128]{1,0:T(8,128)(2,1)S(1)} %convert_element_type.39), channel_id=1, source_target_pairs={{0,8},{4,12},{8,0},{12,4},{16,24},{20,28},{24,16},{28,20},{1,9},{5... | collective-permute-start | bytes 294920 | tf_op jit(solution)/shard_map/ppermute | solution.py:45
  74.2 7.5 %collective-permute-start.17 = (f16[384,128]{1,0:T(8,128)(2,1)S(1)}, f16[384,128]{1,0:T(8,128)(2,1)S(1)}, u32[]{:S(2)}, u32[]{:S(2)}) collective-permute-start(f16[384,128]{1,0:T(8,128)(2,1)S(1)} %add_convert_fusion.1), channel_id=1, source_target_pairs={{0,3},{1,2},{2,1},{3,0},{4,7},{5,6},{6,5},{7,4},{8,11},{9,10},{10,... | collective-permute-start | bytes 294920 | tf_op jit(solution)/shard_map/ppermute | solution.py:45
  76.7 12.6 %collective-permute-start.16 = (f16[384,128]{1,0:T(8,128)(2,1)S(1)}, f16[384,128]{1,0:T(8,128)(2,1)S(1)}, u32[]{:S(2)}, u32[]{:S(2)}) collective-permute-start(f16[384,128]{1,0:T(8,128)(2,1)S(1)} %add_convert_fusion.1), channel_id=1, source_target_pairs={{0,2},{1,3},{2,0},{3,1},{4,6},{5,7},{6,4},{7,5},{8,10},{9,11},{10,... | collective-permute-start | bytes 294920 | tf_op jit(solution)/shard_map/ppermute | solution.py:45
  76.7 12.6 %collective-permute-start.15 = (f16[384,128]{1,0:T(8,128)(2,1)S(1)}, f16[384,128]{1,0:T(8,128)(2,1)S(1)}, u32[]{:S(2)}, u32[]{:S(2)}) collective-permute-start(f16[384,128]{1,0:T(8,128)(2,1)S(1)} %add_convert_fusion.1), channel_id=1, source_target_pairs={{0,1},{1,0},{2,3},{3,2},{4,5},{5,4},{6,7},{7,6},{8,9},{9,8},{10,11... | collective-permute-start | bytes 294920 | tf_op jit(solution)/shard_map/ppermute | solution.py:45
  78.6 12.1 %collective-permute-start.27 = (f32[176,128]{1,0:T(8,128)}, f32[176,128]{1,0:T(8,128)S(1)}, u32[]{:S(2)}, u32[]{:S(2)}) collective-permute-start(f32[176,128]{1,0:T(8,128)} %get-tuple-element.18), channel_id=1, source_target_pairs={{0,3},{1,2},{2,1},{3,0},{4,7},{5,6},{6,5},{7,4},{8,11},{9,10},{10,... | collective-permute-start | bytes 270344 | tf_op jit(solution)/shard_map/ppermute | solution.py:45
  81.1 11.1 %collective-permute-start.26 = (f32[176,128]{1,0:T(8,128)}, f32[176,128]{1,0:T(8,128)S(1)}, u32[]{:S(2)}, u32[]{:S(2)}) collective-permute-start(f32[176,128]{1,0:T(8,128)} %get-tuple-element.18), channel_id=1, source_target_pairs={{0,2},{1,3},{2,0},{3,1},{4,6},{5,7},{6,4},{7,5},{8,10},{9,11},{10,... | collective-permute-start | bytes 270344 | tf_op jit(solution)/shard_map/ppermute | solution.py:45
  81.7 10.5 %collective-permute-start.25 = (f32[176,128]{1,0:T(8,128)}, f32[176,128]{1,0:T(8,128)S(1)}, u32[]{:S(2)}, u32[]{:S(2)}) collective-permute-start(f32[176,128]{1,0:T(8,128)} %get-tuple-element.18), channel_id=1, source_target_pairs={{0,1},{1,0},{2,3},{3,2},{4,5},{5,4},{6,7},{7,6},{8,9},{9,8},{10,11... | collective-permute-start | bytes 270344 | tf_op jit(solution)/shard_map/ppermute | solution.py:45
  89.4 6.5 %collective-permute-start.18 = (f16[384,128]{1,0:T(8,128)(2,1)S(1)}, f16[384,128]{1,0:T(8,128)(2,1)S(1)}, u32[]{:S(2)}, u32[]{:S(2)}) collective-permute-start(f16[384,128]{1,0:T(8,128)(2,1)S(1)} %get-tuple-element.24), channel_id=1, source_target_pairs={{0,8},{4,12},{8,0},{12,4},{16,24},{20,28},{24,16},{28,20},{1,9},{5... | collective-permute-start | bytes 294920 | tf_op jit(solution)/shard_map/ppermute | solution.py:45
  92.2 33.8 %copy-start.2 = (f32[4,176,128]{2,1,0:T(8,128)}, f32[4,176,128]{2,1,0:T(8,128)S(1)}, u32[]{:S(2)}) copy-start(f32[4,176,128]{2,1,0:T(8,128)S(1)} %pad_maximum_fusion.refs_1_) | copy-start | bytes 1081348
  92.2 33.8 %collective-permute-start.31 = (f32[4,176,128]{2,1,0:T(8,128)S(1)}, f32[4,176,128]{2,1,0:T(8,128)S(1)}, u32[]{:S(2)}, u32[]{:S(2)}) collective-permute-start(f32[4,176,128]{2,1,0:T(8,128)S(1)} %pad_maximum_fusion.refs_1_), channel_id=1, source_target_pairs={{0,4},{4,0},{8,12},{12,8},{16,20},{20,16},{24,28},{28,24},{1,5},{5... | collective-permute-start | bytes 1081352 | tf_op jit(solution)/shard_map/ppermute | solution.py:45
  92.3 31.3 %collective-permute-start.30 = (f32[4,176,128]{2,1,0:T(8,128)S(1)}, f32[4,176,128]{2,1,0:T(8,128)S(1)}, u32[]{:S(2)}, u32[]{:S(2)}) collective-permute-start(f32[4,176,128]{2,1,0:T(8,128)S(1)} %pad_maximum_fusion.refs_1_), channel_id=1, source_target_pairs={{0,24},{4,28},{8,16},{12,20},{16,8},{20,12},{24,0},{28,4},{1,25},{... | collective-permute-start | bytes 1081352 | tf_op jit(solution)/shard_map/ppermute | solution.py:45
  94.0 29.9 %collective-permute-start.29 = (f32[4,176,128]{2,1,0:T(8,128)S(1)}, f32[4,176,128]{2,1,0:T(8,128)S(1)}, u32[]{:S(2)}, u32[]{:S(2)}) collective-permute-start(f32[4,176,128]{2,1,0:T(8,128)S(1)} %pad_maximum_fusion.refs_1_), channel_id=1, source_target_pairs={{0,16},{4,20},{8,24},{12,28},{16,0},{20,4},{24,8},{28,12},{1,17},{... | collective-permute-start | bytes 1081352 | tf_op jit(solution)/shard_map/ppermute | solution.py:45
  95.2 28.9 %collective-permute-start.28 = (f32[4,176,128]{2,1,0:T(8,128)S(1)}, f32[4,176,128]{2,1,0:T(8,128)S(1)}, u32[]{:S(2)}, u32[]{:S(2)}) collective-permute-start(f32[4,176,128]{2,1,0:T(8,128)S(1)} %pad_maximum_fusion.refs_1_), channel_id=1, source_target_pairs={{0,8},{4,12},{8,0},{12,4},{16,24},{20,28},{24,16},{28,20},{1,9},{5... | collective-permute-start | bytes 1081352 | tf_op jit(solution)/shard_map/ppermute | solution.py:45
  95.9 18.0 %collective-permute-start.19 = (f16[384,128]{1,0:T(8,128)(2,1)S(1)}, f16[384,128]{1,0:T(8,128)(2,1)S(1)}, u32[]{:S(2)}, u32[]{:S(2)}) collective-permute-start(f16[384,128]{1,0:T(8,128)(2,1)S(1)} %get-tuple-element.24), channel_id=1, source_target_pairs={{0,16},{4,20},{8,24},{12,28},{16,0},{20,4},{24,8},{28,12},{1,17},{... | collective-permute-start | bytes 294920 | tf_op jit(solution)/shard_map/ppermute | solution.py:45
  113.9 5.6 %collective-permute-start.20 = (f16[384,128]{1,0:T(8,128)(2,1)S(1)}, f16[384,128]{1,0:T(8,128)(2,1)S(1)}, u32[]{:S(2)}, u32[]{:S(2)}) collective-permute-start(f16[384,128]{1,0:T(8,128)(2,1)S(1)} %get-tuple-element.24), channel_id=1, source_target_pairs={{0,24},{4,28},{8,16},{12,20},{16,8},{20,12},{24,0},{28,4},{1,25},{... | collective-permute-start | bytes 294920 | tf_op jit(solution)/shard_map/ppermute | solution.py:45
  119.5 1.3 collective-permute-start.21
  120.8 1.3 collective-permute-start.22
  122.1 1.3 collective-permute-start.23
  123.4 1.3 collective-permute-start.24
  123.6 2.7 %copy-start.11 = (f32[4,176,128]{2,1,0:T(8,128)}, f32[4,176,128]{2,1,0:T(8,128)S(1)}, u32[]{:S(2)}) copy-start(f32[4,176,128]{2,1,0:T(8,128)S(1)} %collective-permute-done.30.refs_4_) | copy-start | bytes 1081348
  123.6 2.4 %collective-permute-start.34 = (f32[4,176,128]{2,1,0:T(8,128)S(1)}, f32[4,176,128]{2,1,0:T(8,128)S(1)}, u32[]{:S(2)}, u32[]{:S(2)}) collective-permute-start(f32[4,176,128]{2,1,0:T(8,128)S(1)} %collective-permute-done.30.refs_4_), channel_id=1, source_target_pairs={{0,4},{4,0},{8,12},{12,8},{16,20},{20,16},{24,28},{28,24},{1,5},{5... | collective-permute-start | bytes 1081352 | tf_op jit(solution)/shard_map/ppermute | solution.py:45
  123.9 2.4 %copy-start.12 = (f32[4,176,128]{2,1,0:T(8,128)}, f32[4,176,128]{2,1,0:T(8,128)S(1)}, u32[]{:S(2)}) copy-start(f32[4,176,128]{2,1,0:T(8,128)S(1)} %collective-permute-done.29.refs_3_) | copy-start | bytes 1081348
  123.9 2.1 %collective-permute-start.33 = (f32[4,176,128]{2,1,0:T(8,128)S(1)}, f32[4,176,128]{2,1,0:T(8,128)S(1)}, u32[]{:S(2)}, u32[]{:S(2)}) collective-permute-start(f32[4,176,128]{2,1,0:T(8,128)S(1)} %collective-permute-done.29.refs_3_), channel_id=1, source_target_pairs={{0,4},{4,0},{8,12},{12,8},{16,20},{20,16},{24,28},{28,24},{1,5},{5... | collective-permute-start | bytes 1081352 | tf_op jit(solution)/shard_map/ppermute | solution.py:45
  124.1 2.2 %copy-start.13 = (f32[4,176,128]{2,1,0:T(8,128)}, f32[4,176,128]{2,1,0:T(8,128)S(1)}, u32[]{:S(2)}) copy-start(f32[4,176,128]{2,1,0:T(8,128)S(1)} %collective-permute-done.28.refs_2_) | copy-start | bytes 1081348
  124.1 2.2 %collective-permute-start.32 = (f32[4,176,128]{2,1,0:T(8,128)S(1)}, f32[4,176,128]{2,1,0:T(8,128)S(1)}, u32[]{:S(2)}, u32[]{:S(2)}) collective-permute-start(f32[4,176,128]{2,1,0:T(8,128)S(1)} %collective-permute-done.28.refs_2_), channel_id=1, source_target_pairs={{0,4},{4,0},{8,12},{12,8},{16,20},{20,16},{24,28},{28,24},{1,5},{5... | collective-permute-start | bytes 1081352 | tf_op jit(solution)/shard_map/ppermute | solution.py:45
  126.0 0.8 copy-start.10
  126.0 0.9 copy-start.14
  126.0 1.0 copy-start.15
  127.1 0.8 copy-start.16

commit v3 on v2

--- a/solution.py
+++ b/solution.py
@@ -21,7 +21,7 @@
 f32 = jnp.float32
 bf16 = jnp.bfloat16
 f16 = jnp.float16
-SCALE = 32.0
+TOP = 14.0
 VMEM = pl.BlockSpec(memory_space=pltpu.VMEM)
 ANY = pl.BlockSpec(memory_space=pl.ANY)
 SMEM = pl.BlockSpec(memory_space=pltpu.SMEM)
@@ -69,20 +69,23 @@
     return jnp.stack([value] + [swap(value, axis, offset) for offset in offsets])
 
 
+def encode(value, power):
+    return jnp.concatenate([value * jnp.exp2(TOP - power[:1]), power]).astype(f16)
+
+
+def decode(coded):
+    value, power = coded[:-SUB].astype(f32), coded[-SUB : 1 - SUB].astype(f32)
+    return value * jnp.exp2(power - TOP)
+
+
 def diagonal_kernel(bases, out):
     per_basis = bases.shape[1] // LANES
     columns = spans(per_basis, LANES)
-    energy = jnp.zeros((SUB, LANES), f32)
     for at, (i, j) in zip(spans(len(own_tiles(per_basis)), LANES), own_tiles(per_basis)):
-        tile = dot(bases[:, columns[i]], bases[:, columns[j]], TN)
-        out[at] = tile
-        if i == j:
-            tile = jnp.where(identity(LANES), tile, 0.0)
-            energy = energy + sum(tile[rows] for rows in spans(LANES // SUB, SUB))
-    out[at.stop :] = energy
-
-
-def cross_kernel(at_ref, table, scale, start, diagonal, *refs):
+        out[at] = dot(bases[:, columns[i]], bases[:, columns[j]], TN)
+
+
+def cross_kernel(at_ref, table, start, diagonal, *refs):
     n_batch = lax.axis_size("batch")
     pieces, (rows, message, *outs, both) = refs[: 2 * n_batch], refs[2 * n_batch :]
     chip, core, batch = at_ref[0], at_ref[1], at_ref[2]
@@ -99,14 +102,22 @@
     for k, lanes in enumerate(spans(size // LANES, LANES)):
         first = pl.multiple_of(index * share, SUB)
         message[part + k * share : part + (k + 1) * share] = start[pl.ds(first, share), lanes]
+
+    def add_squares(k, total):
+        chunk = both[pl.ds(pl.multiple_of(k * LANES, LANES), LANES), :].astype(f32)
+        chunk = chunk * chunk
+        return total + sum(chunk[r, c] for r in spans(LANES // SUB, SUB) for c in spans(chunk.shape[1] // LANES, LANES))
+
+    energy = lax.fori_loop(0, both.shape[0] // LANES, add_squares, jnp.zeros((SUB, LANES), f32))
     for offset, out in enumerate(outs):
         share = out.shape[0] // LANES
+        out[share * LANES :] = energy
         owner = 2 * lax.bitwise_xor(chip, offset) + core
         for j, at in enumerate(spans(share, LANES)):
             place = 2 * (owner * share + j)
             left = pl.multiple_of(table[place] * LANES, LANES)
             right = pl.multiple_of(table[place + 1] * LANES, LANES)
-            out[at] = dot(both[:, pl.ds(left, LANES)], both[:, pl.ds(right, LANES)], TN) * scale[0]
+            out[at] = dot(both[:, pl.ds(left, LANES)], both[:, pl.ds(right, LANES)], TN)
 
 
 def spread(value, index):
@@ -222,11 +233,12 @@
     def place(k, carry):
         other, offset = k // (devices // 2), lax.rem(k, devices // 2)
         owner = 2 * lax.bitwise_xor(chip, offset) + lax.bitwise_xor(core, other)
+        unit = jnp.exp2(cross[k, share * LANES : share * LANES + 1, :] - TOP) * factor
         for j, inner in enumerate(spans(share, LANES)):
             at = 2 * (owner * share + j)
             row = pl.ds(pl.multiple_of(table[at] * LANES, LANES), LANES)
             column = pl.ds(pl.multiple_of(table[at + 1] * LANES, LANES), LANES)
-            for ref, value in zip(pair, split(cross[k, inner, :] * (1.0 / SCALE))):
+            for ref, value in zip(pair, split(cross[k, inner, :] * unit)):
                 ref[row, column] = value
                 ref[column, row] = value.T
         return carry
@@ -351,36 +363,34 @@
 
     own_count = len(own_tiles(per_basis))
     (diagonal,) = call(
-        diagonal_kernel, [((own_count * LANES + SUB, LANES), f32)], [], bases,
+        diagonal_kernel, [((own_count * LANES, LANES), f32)], [], bases,
         flops=2 * local_rows * own_count * LANES * LANES, moved=bases.size * 2, after=other_pieces[:1],
     )
-    for offset in (1 << k for k in range(n_rows.bit_length() - 1)):
-        diagonal = diagonal + swap(diagonal, "rows", offset)
-    energy = diagonal[own_count * LANES :]
-    for offset in (1 << k for k in range(n_batch.bit_length() - 1)):
-        energy = energy + swap(energy, "batch", offset)
-    scale = (SCALE * columns / jnp.sum(energy)).reshape(1)
+    diagonal = diagonal + swap(diagonal, "rows", 1)
+    diagonal = sum((swap(diagonal, "rows", offset) for offset in other_chips), diagonal)
 
     part = own_count * LANES // n_rows
     message_rows = part + start.size // n_rows // LANES
+    tile_rows = share * LANES
     rows, mine, *blocks = call(
         cross_kernel,
-        [((sub_rows, columns), bf16), ((message_rows, LANES), f32)] + [((share * LANES, LANES), f32)] * chips,
+        [((sub_rows, columns), bf16), ((message_rows, LANES), f32)] + [((tile_rows + SUB, LANES), f32)] * chips,
         [((2 * sub_rows, columns), bf16)],
-        at, table, scale, start, diagonal, *pieces, *other_pieces, n_smem=3,
+        at, table, start, diagonal, *pieces, *other_pieces, n_smem=2,
         flops=4 * sub_rows * chips * share * LANES * LANES, moved=6 << 20,
     )
-    plane = blocks[0]
-    for block, offset in zip(blocks[1:], other_chips):
-        plane = plane + swap(block.astype(f16), "rows", offset).astype(f32)
-    plane = plane.astype(f16)
-    total = plane.astype(f32)
-    for offset in other_batches:
-        total = total + swap(plane, "batch", offset).astype(f32)
-    total = total.astype(f16)
+    plane = sum((swap(block, "rows", offset) for block, offset in zip(blocks[1:], other_chips)), blocks[0])
+    power = jnp.floor(jnp.log2(jnp.sum(plane[tile_rows:]))) + 1
+    power = jnp.full((SUB, LANES), power, f32)
+    plane = encode(plane[:tile_rows], power)
+    planes = [plane] + [swap(plane, "batch", offset) for offset in other_batches]
+    total = sum(decode(value) for value in planes)
+    power = jnp.ceil(jnp.log2(sum(jnp.exp2(value[tile_rows:].astype(f32)) for value in planes)))
+    total = encode(total, power)
 
     mine = spread_copy(mine, "batch", other_batches)
     mine = [mine] + [swap(mine, "rows", offset) for offset in other_chips]
+    total, mine = lax.optimization_barrier((total, mine))
     high, low, diagonal = call(
         prepare_kernel,
         [((size, columns), bf16)] * 2 + [((n_batch, own_count * LANES, LANES), f32)],
@@ -388,8 +398,8 @@
         at, *mine, *(swap(block, "rows", 1) for block in mine), n_smem=1, moved=8 << 20,
     )
 
-    cross = [total] + [swap(total, "rows", offset) for offset in other_chips]
-    cross = jnp.stack(cross + [swap(block, "rows", 1) for block in cross]).astype(f32)
+    cross = spread_copy(total, "rows", other_chips)
+    cross = jnp.concatenate([cross, swap(cross, "rows", 1)]).astype(f32)
     (modes,) = call(
         solve_kernel,
         [((sub_rows, size), bf16)],

time: 170 us -> 142 us (0.84)
  waiting for transfers between devices: 69.7 us -> 47 us
  starting transfers between devices: 35.3 us -> 30.4 us
  Pallas kernels: 50.8 us -> 52.8 us
  other arithmetic: 7.51 us -> 5.55 us
    ppermute x35 -> x31, waiting for transfers between devices: 69.7 us -> 47 us  [swap(): return lax.ppermute(value, axis, [(i, i ^ offset) for i in range(size)])]
    ppermute x35 -> x31, starting transfers between devices: 35.3 us -> 30.4 us  [swap(): return lax.ppermute(value, axis, [(i, i ^ offset) for i in range(size)])]
    convert_element_type x5 -> x1, other arithmetic: 5.11 us -> 1.32 us  [on_device(): cross = jnp.concatenate([cross, swap(cross, 'rows', 1)]).astype(f32)]
    pallas_call x4, Pallas kernels: 50.8 us -> 52.8 us  [call(): pl.pallas_call(body, out_shape=[jax.ShapeDtypeStruct(shape, dtype) for sh...]
    unnamed x42 -> x36, local copies, waits for them, and re-layouts: 3.5 us -> 3.02 us
  transfers between devices with their start and end apart: 35 -> 31, of which waited for: 21 -> 12; matrix products, arithmetic and copies ran while one was open for 2% -> 3% of each run, Pallas kernels for 0% -> 5%
where the time goes in v3:
time: 142 us; the launch traced here: 141 us
  Pallas kernels  52.8 us (37%)
  waiting for transfers between devices  47 us (33%)
  starting transfers between devices  30.4 us (21%)
  other arithmetic  5.55 us (4%)
  local copies, waits for them, and re-layouts  4.62 us (3%)
    pallas_call x4, Pallas kernels, call(): pl.pallas_call(body, out_shape=[jax.ShapeDtypeStruct(shape, dtype) for sh...  52.8 us
    ppermute x31, waiting for transfers between devices, swap(): return lax.ppermute(value, axis, [(i, i ^ offset) for i in range(size)])  47 us
    ppermute x31, starting transfers between devices, swap(): return lax.ppermute(value, axis, [(i, i ^ offset) for i in range(size)])  30.4 us
    unnamed x36, local copies, waits for them, and re-layouts  3.02 us
  transfers between devices with their start and end apart: 31, of which 12 were waited for; matrix products, arithmetic and copies ran while one was open for 3% of the time, Pallas kernels for 5%

profile of v3, /device:TPU:0, one launch (start us, length us, event | category | flops | bytes accessed | tf_op | source)
XLA Modules:
  0.0 141.5 jit_solution(17480231430882570320)
XLA Ops:
  0.0 1.5 %constant_dynamic-slice_fusion = (bf16[768,256]{1,0:T(8,128)(2,1)S(1)}, bf16[768,256]{1,0:T(8,128)(2,1)S(1)}, bf16[768,256]{1,0:T(8,128)(2,1)S(1)}, bf16[768,256]{1,0:T(8,128)(2,1)S(1)}) fusion(bf16[3072,256]{1,0:T(8,128)(2,1)} %refs_0_.1, s32[]{:T(128)S(6)} %select_n.28, s32[]{:T(128)S(6)} %select_n.26, s32[]{:T(128)S(6)} %select_n.25, s32[]{:T(128)S(6)} %select_n.27), kind=kLoop, calls=%fused_computation.15 | loop fusion | bytes 3145744 | tf_op jit(solution)/shard_map/dynamic_slice | solution.py:360
  1.5 0.5 collective-permute-start
  2.0 4.7 %collective-permute-start.7 = (bf16[768,256]{1,0:T(8,128)(2,1)S(1)}, bf16[768,256]{1,0:T(8,128)(2,1)S(1)}, u32[]{:S(2)}, u32[]{:S(2)}) collective-permute-start(bf16[768,256]{1,0:T(8,128)(2,1)S(1)} %get-tuple-element.35), channel_id=1, source_target_pairs={{0,3},{1,2},{2,1},{3,0},{4,7},{5,6},{6,5},{7,4},{8,11},{9,10},{10,... | collective-permute-start | bytes 1179656 | tf_op jit(solution)/shard_map/ppermute | solution.py:45
  6.7 0.0 collective-permute-start.5
  6.7 0.6 collective-permute-start.6
  7.3 0.0 collective-permute-done.refs_1_.refs_8_
  7.3 0.7 copy-done.1
  8.1 2.9 %shard_map.37 = f32[384,128]{1,0:T(8,128)} custom-call(bf16[3072,256]{1,0:T(8,128)(2,1)} %refs_0_.1, bf16[768,256]{1,0:T(8,128)(2,1)} %copy-done.1), custom_call_target="tpu_custom_call" | custom-call | flops 301989888 | bytes 1572864 | tf_op jit(solution)/shard_map/pallas_call | solution.py:348
  11.0 1.6 %collective-permute-done.1 = f32[384,128]{1,0:T(8,128)S(1)} collective-permute-done((f32[384,128]{1,0:T(8,128)}, f32[384,128]{1,0:T(8,128)S(1)}, u32[]{:S(2)}, u32[]{:S(2)}) %collective-permute-start.1) | collective-permute-done | bytes 196640 | tf_op jit(solution)/shard_map/ppermute | solution.py:45
  12.6 1.0 add.68
  13.6 1.7 %collective-permute-start.2 = (f32[384,128]{1,0:T(8,128)S(1)}, f32[384,128]{1,0:T(8,128)S(1)}, u32[]{:S(2)}, u32[]{:S(2)}) collective-permute-start(f32[384,128]{1,0:T(8,128)S(1)} %add.68), channel_id=1, source_target_pairs={{0,8},{4,12},{8,0},{12,4},{16,24},{20,28},{24,16},{28,20},{1,9},{5... | collective-permute-start | bytes 589832 | tf_op jit(solution)/shard_map/ppermute | solution.py:45
  15.3 1.5 %collective-permute-start.3 = (f32[384,128]{1,0:T(8,128)S(1)}, f32[384,128]{1,0:T(8,128)S(1)}, u32[]{:S(2)}, u32[]{:S(2)}) collective-permute-start(f32[384,128]{1,0:T(8,128)S(1)} %add.68), channel_id=1, source_target_pairs={{0,16},{4,20},{8,24},{12,28},{16,0},{20,4},{24,8},{28,12},{1,17},{... | collective-permute-start | bytes 589832 | tf_op jit(solution)/shard_map/ppermute | solution.py:45
  16.8 2.5 %collective-permute-start.4 = (f32[384,128]{1,0:T(8,128)S(1)}, f32[384,128]{1,0:T(8,128)S(1)}, u32[]{:S(2)}, u32[]{:S(2)}) collective-permute-start(f32[384,128]{1,0:T(8,128)S(1)} %add.68), channel_id=1, source_target_pairs={{0,24},{4,28},{8,16},{12,20},{16,8},{20,12},{24,0},{28,4},{1,25},{... | collective-permute-start | bytes 589832 | tf_op jit(solution)/shard_map/ppermute | solution.py:45
  19.3 6.6 %collective-permute-done.5.refs_5_ = bf16[768,256]{1,0:T(8,128)(2,1)S(1)} collective-permute-done((bf16[768,256]{1,0:T(8,128)(2,1)S(1)}, bf16[768,256]{1,0:T(8,128)(2,1)S(1)}, u32[]{:S(2)}, u32[]{:S(2)}) %collective-permute-start.5) | collective-permute-done | bytes 393248 | tf_op jit(solution)/shard_map/ppermute | solution.py:45
  25.9 0.0 collective-permute-start.10
  26.0 14.9 %collective-permute-done.6.refs_6_ = bf16[768,256]{1,0:T(8,128)(2,1)S(1)} collective-permute-done((bf16[768,256]{1,0:T(8,128)(2,1)S(1)}, bf16[768,256]{1,0:T(8,128)(2,1)S(1)}, u32[]{:S(2)}, u32[]{:S(2)}) %collective-permute-start.6) | collective-permute-done | bytes 393248 | tf_op jit(solution)/shard_map/ppermute | solution.py:45
  40.8 0.0 collective-permute-done.2
  40.8 0.5 collective-permute-start.9
  41.3 0.6 pad_add_fusion.refs_0_
  41.9 0.7 add_add_fusion.1.refs_3_
  42.6 0.0 collective-permute-done.10.refs_11_
  42.6 0.0 collective-permute-done.8.refs_9_
  42.6 0.5 collective-permute-done.9.refs_10_
  43.1 0.3 copy-done.6
  43.4 0.2 copy-done.7
  43.5 0.7 copy-done.8
  44.3 8.3 %shard_map.38 = (bf16[768,1024]{1,0:T(8,128)(2,1)}, f32[176,128]{1,0:T(8,128)}, f32[392,128]{1,0:T(8,128)}, f32[392,128]{1,0:T(8,128)}, f32[392,128]{1,0:T(8,128)}, /*index=5*/f32[392,128]{1,0:T(8,128)}) custom-call(s32[3]{0:T(128)} %pad_add_fusion.refs_0_, s32[48]{0:T(128)} %constant.60.clone.refs_1_, f32[256,512]{1,0:T(8,128)} %refs_2_.1, ...), custom_call_target="tpu_custom_call" | custom-call | flops 603979776 | bytes 6291456 | tf_op jit(solution)/shard_map/pallas_call | solution.py:348
  52.6 1.6 %collective-permute-start.11 = (f32[392,128]{1,0:T(8,128)}, f32[392,128]{1,0:T(8,128)S(1)}, u32[]{:S(2)}, u32[]{:S(2)}) collective-permute-start(f32[392,128]{1,0:T(8,128)} %get-tuple-element.20), channel_id=1, source_target_pairs={{0,8},{4,12},{8,0},{12,4},{16,24},{20,28},{24,16},{28,20},{1,9},{5... | collective-permute-start | bytes 602120 | tf_op jit(solution)/shard_map/ppermute | solution.py:45
  54.1 1.5 %collective-permute-start.12 = (f32[392,128]{1,0:T(8,128)}, f32[392,128]{1,0:T(8,128)S(1)}, u32[]{:S(2)}, u32[]{:S(2)}) collective-permute-start(f32[392,128]{1,0:T(8,128)} %get-tuple-element.21), channel_id=1, source_target_pairs={{0,16},{4,20},{8,24},{12,28},{16,0},{20,4},{24,8},{28,12},{1,17},{... | collective-permute-start | bytes 602120 | tf_op jit(solution)/shard_map/ppermute | solution.py:45
  55.7 0.5 collective-permute-start.13
  56.1 2.5 %collective-permute-start.19 = (f32[176,128]{1,0:T(8,128)}, f32[176,128]{1,0:T(8,128)S(1)}, u32[]{:S(2)}, u32[]{:S(2)}) collective-permute-start(f32[176,128]{1,0:T(8,128)} %get-tuple-element.23), channel_id=1, source_target_pairs={{0,3},{1,2},{2,1},{3,0},{4,7},{5,6},{6,5},{7,4},{8,11},{9,10},{10,... | collective-permute-start | bytes 270344 | tf_op jit(solution)/shard_map/ppermute | solution.py:45
  58.7 0.0 collective-permute-start.17
  58.7 2.0 %collective-permute-done.11 = f32[392,128]{1,0:T(8,128)S(1)} collective-permute-done((f32[392,128]{1,0:T(8,128)}, f32[392,128]{1,0:T(8,128)S(1)}, u32[]{:S(2)}, u32[]{:S(2)}) %collective-permute-start.11) | collective-permute-done | bytes 200736 | tf_op jit(solution)/shard_map/ppermute | solution.py:45
  60.7 0.0 collective-permute-start.18
  60.7 4.6 %collective-permute-done.12 = f32[392,128]{1,0:T(8,128)S(1)} collective-permute-done((f32[392,128]{1,0:T(8,128)}, f32[392,128]{1,0:T(8,128)S(1)}, u32[]{:S(2)}, u32[]{:S(2)}) %collective-permute-start.12) | collective-permute-done | bytes 200736 | tf_op jit(solution)/shard_map/ppermute | solution.py:45
  65.3 1.0 add_add_fusion
  66.4 0.6 slice_reduce_fusion
  67.8 0.1 collective-permute-start.14
  67.9 3.1 %collective-permute-start.15 = (f16[392,128]{1,0:T(8,128)(2,1)S(1)}, f16[392,128]{1,0:T(8,128)(2,1)S(1)}, u32[]{:S(2)}, u32[]{:S(2)}) collective-permute-start(f16[392,128]{1,0:T(8,128)(2,1)S(1)} %concatenate.11), channel_id=1, source_target_pairs={{0,2},{1,3},{2,0},{3,1},{4,6},{5,7},{6,4},{7,5},{8,10},{9,11},{10,... | collective-permute-start | bytes 301064 | tf_op jit(solution)/shard_map/ppermute | solution.py:45
  70.9 1.3 collective-permute-start.16
  72.3 0.0 copy-start.2
  72.3 1.3 collective-permute-start.20
  73.6 0.8 collective-permute-start.21
  74.5 1.5 %collective-permute-start.22 = (f32[4,176,128]{2,1,0:T(8,128)S(1)}, f32[4,176,128]{2,1,0:T(8,128)S(1)}, u32[]{:S(2)}, u32[]{:S(2)}) collective-permute-start(f32[4,176,128]{2,1,0:T(8,128)S(1)} %pad_maximum_fusion.1.refs_1_), channel_id=1, source_target_pairs={{0,24},{4,28},{8,16},{12,20},{16,8},{20,12},{24,0},{28,4},{1,25},{... | collective-permute-start | bytes 1081352 | tf_op jit(solution)/shard_map/ppermute | solution.py:45
  76.0 2.0 %collective-permute-done.15 = f16[392,128]{1,0:T(8,128)(2,1)S(1)} collective-permute-done((f16[392,128]{1,0:T(8,128)(2,1)S(1)}, f16[392,128]{1,0:T(8,128)(2,1)S(1)}, u32[]{:S(2)}, u32[]{:S(2)}) %collective-permute-start.15) | collective-permute-done | bytes 100384 | tf_op jit(solution)/shard_map/ppermute | solution.py:45
  78.1 0.1 multiply_convert_fusion
  78.3 5.4 %collective-permute-done.20.refs_2_ = f32[4,176,128]{2,1,0:T(8,128)S(1)} collective-permute-done((f32[4,176,128]{2,1,0:T(8,128)S(1)}, f32[4,176,128]{2,1,0:T(8,128)S(1)}, u32[]{:S(2)}, u32[]{:S(2)}) %collective-permute-start.20) | collective-permute-done | bytes 360480 | tf_op jit(solution)/shard_map/ppermute | solution.py:45
  83.7 6.1 %collective-permute-done.21.refs_3_ = f32[4,176,128]{2,1,0:T(8,128)S(1)} collective-permute-done((f32[4,176,128]{2,1,0:T(8,128)S(1)}, f32[4,176,128]{2,1,0:T(8,128)S(1)}, u32[]{:S(2)}, u32[]{:S(2)}) %collective-permute-start.21) | collective-permute-done | bytes 360480 | tf_op jit(solution)/shard_map/ppermute | solution.py:45
  89.8 0.7 collective-permute-start.23
  90.5 1.1 collective-permute-start.24
  91.6 1.8 %collective-permute-start.25 = (f16[392,128]{1,0:T(8,128)(2,1)S(1)}, f16[392,128]{1,0:T(8,128)(2,1)S(1)}, u32[]{:S(2)}, u32[]{:S(2)}) collective-permute-start(f16[392,128]{1,0:T(8,128)(2,1)S(1)} %pad_maximum_fusion.2), channel_id=1, source_target_pairs={{0,24},{4,28},{8,16},{12,20},{16,8},{20,12},{24,0},{28,4},{1,25},{... | collective-permute-start | bytes 301064 | tf_op jit(solution)/shard_map/ppermute | solution.py:45
  93.4 0.1 collective-permute-start.27
  93.5 0.5 collective-permute-start.28
  94.0 0.5 collective-permute-done.23
  94.6 0.6 collective-permute-done.24
  95.2 2.0 %collective-permute-done.25 = f16[392,128]{1,0:T(8,128)(2,1)S(1)} collective-permute-done((f16[392,128]{1,0:T(8,128)(2,1)S(1)}, f16[392,128]{1,0:T(8,128)(2,1)S(1)}, u32[]{:S(2)}, u32[]{:S(2)}) %collective-permute-start.25) | collective-permute-done | bytes 100384 | tf_op jit(solution)/shard_map/ppermute | solution.py:45
  97.1 0.1 pad_maximum_fusion
  97.3 0.1 collective-permute-start.26
  97.5 0.8 copy-done.14
  98.4 0.1 copy-done.13
  98.5 4.3 %shard_map.39 = (bf16[512,1024]{1,0:T(8,128)(2,1)}, bf16[512,1024]{1,0:T(8,128)(2,1)}, f32[4,384,128]{2,1,0:T(8,128)}) custom-call(s32[3]{0:T(128)} %pad_add_fusion.refs_0_, f32[4,176,128]{2,1,0:T(8,128)} %copy-done.2, f32[4,176,128]{2,1,0:T(8,128)} %copy-done.9, f32[4,176,128]{2,1,0:T(8,128)} %copy-done.10, f32[4,176,128]{2,1,0:T(8,128)} %copy-done.11, ...), custom_call_target="tpu_custom_call" | custom-call | bytes 8388608 | tf_op jit(solution)/shard_map/pallas_call | solution.py:348
  102.8 0.1 constant_dynamic-update-slice_fusion
  102.9 1.3 convert_element_type.52.refs_2_
  104.2 37.3 %shard_map.40 = bf16[768,512]{1,0:T(8,128)(2,1)} custom-call(s32[3]{0:T(128)} %pad_add_fusion.refs_0_, s32[48]{0:T(128)} %constant.60.clone.refs_1_, f32[8,392,128]{2,1,0:T(8,128)} %convert_element_type.52.refs_2_, f32[4,384,128]{2,1,0:T(8,128)} %get-tuple-element.29.refs_3_, bf16[512,1024]{1,0:T(8,128)(2,1)} %get-tuple-element.30.refs_4_, ...), custom_call_target="tpu_custom_call" | custom-call | flops 10000000000 | bytes 10485760 | tf_op jit(solution)/shard_map/pallas_call | solution.py:348
  (57 shorter events, 0.4 us)
Async XLA Ops:
  1.5 41.2 %copy-start = (bf16[768,256]{1,0:T(8,128)(2,1)}, bf16[768,256]{1,0:T(8,128)(2,1)S(1)}, u32[]{:S(2)}) copy-start(bf16[768,256]{1,0:T(8,128)(2,1)S(1)} %get-tuple-element.37.refs_4_) | copy-start | bytes 1179652
  1.5 5.8 %collective-permute-start = (bf16[768,256]{1,0:T(8,128)(2,1)S(1)}, bf16[768,256]{1,0:T(8,128)(2,1)S(1)}, u32[]{:S(2)}, u32[]{:S(2)}) collective-permute-start(bf16[768,256]{1,0:T(8,128)(2,1)S(1)} %get-tuple-element.37.refs_4_), channel_id=1, source_target_pairs={{0,4},{4,0},{8,12},{12,8},{16,20},{20,16},{24,28},{28,24},{1,5},{5... | collective-permute-start | bytes 1179656 | tf_op jit(solution)/shard_map/ppermute | solution.py:45
  2.0 14.8 %collective-permute-start.7 = (bf16[768,256]{1,0:T(8,128)(2,1)S(1)}, bf16[768,256]{1,0:T(8,128)(2,1)S(1)}, u32[]{:S(2)}, u32[]{:S(2)}) collective-permute-start(bf16[768,256]{1,0:T(8,128)(2,1)S(1)} %get-tuple-element.35), channel_id=1, source_target_pairs={{0,3},{1,2},{2,1},{3,0},{4,7},{5,6},{6,5},{7,4},{8,11},{9,10},{10,... | collective-permute-start | bytes 1179656 | tf_op jit(solution)/shard_map/ppermute | solution.py:45
  6.7 19.3 %collective-permute-start.5 = (bf16[768,256]{1,0:T(8,128)(2,1)S(1)}, bf16[768,256]{1,0:T(8,128)(2,1)S(1)}, u32[]{:S(2)}, u32[]{:S(2)}) collective-permute-start(bf16[768,256]{1,0:T(8,128)(2,1)S(1)} %get-tuple-element.36), channel_id=1, source_target_pairs={{0,1},{1,0},{2,3},{3,2},{4,5},{5,4},{6,7},{7,6},{8,9},{9,8},{10,11... | collective-permute-start | bytes 1179656 | tf_op jit(solution)/shard_map/ppermute | solution.py:45
  6.7 34.2 %collective-permute-start.6 = (bf16[768,256]{1,0:T(8,128)(2,1)S(1)}, bf16[768,256]{1,0:T(8,128)(2,1)S(1)}, u32[]{:S(2)}, u32[]{:S(2)}) collective-permute-start(bf16[768,256]{1,0:T(8,128)(2,1)S(1)} %get-tuple-element.38), channel_id=1, source_target_pairs={{0,2},{1,3},{2,0},{3,1},{4,6},{5,7},{6,4},{7,5},{8,10},{9,11},{10,... | collective-permute-start | bytes 1179656 | tf_op jit(solution)/shard_map/ppermute | solution.py:45
  7.3 0.7 copy-start.1
  11.0 1.7 %collective-permute-start.1 = (f32[384,128]{1,0:T(8,128)}, f32[384,128]{1,0:T(8,128)S(1)}, u32[]{:S(2)}, u32[]{:S(2)}) collective-permute-start(f32[384,128]{1,0:T(8,128)} %shard_map.37), channel_id=1, source_target_pairs={{0,4},{4,0},{8,12},{12,8},{16,20},{20,16},{24,28},{28,24},{1,5},{5... | collective-permute-start | bytes 589832 | tf_op jit(solution)/shard_map/ppermute | solution.py:45
  13.6 27.2 %collective-permute-start.2 = (f32[384,128]{1,0:T(8,128)S(1)}, f32[384,128]{1,0:T(8,128)S(1)}, u32[]{:S(2)}, u32[]{:S(2)}) collective-permute-start(f32[384,128]{1,0:T(8,128)S(1)} %add.68), channel_id=1, source_target_pairs={{0,8},{4,12},{8,0},{12,4},{16,24},{20,28},{24,16},{28,20},{1,9},{5... | collective-permute-start | bytes 589832 | tf_op jit(solution)/shard_map/ppermute | solution.py:45
  15.3 26.6 %collective-permute-start.3 = (f32[384,128]{1,0:T(8,128)S(1)}, f32[384,128]{1,0:T(8,128)S(1)}, u32[]{:S(2)}, u32[]{:S(2)}) collective-permute-start(f32[384,128]{1,0:T(8,128)S(1)} %add.68), channel_id=1, source_target_pairs={{0,16},{4,20},{8,24},{12,28},{16,0},{20,4},{24,8},{28,12},{1,17},{... | collective-permute-start | bytes 589832 | tf_op jit(solution)/shard_map/ppermute | solution.py:45
  16.8 26.3 %copy-start.3 = (bf16[768,256]{1,0:T(8,128)(2,1)}, bf16[768,256]{1,0:T(8,128)(2,1)S(1)}, u32[]{:S(2)}) copy-start(bf16[768,256]{1,0:T(8,128)(2,1)S(1)} %collective-permute-done.7.refs_7_) | copy-start | bytes 1179652
  16.8 25.1 %collective-permute-start.4 = (f32[384,128]{1,0:T(8,128)S(1)}, f32[384,128]{1,0:T(8,128)S(1)}, u32[]{:S(2)}, u32[]{:S(2)}) collective-permute-start(f32[384,128]{1,0:T(8,128)S(1)} %add.68), channel_id=1, source_target_pairs={{0,24},{4,28},{8,16},{12,20},{16,8},{20,12},{24,0},{28,4},{1,25},{... | collective-permute-start | bytes 589832 | tf_op jit(solution)/shard_map/ppermute | solution.py:45
  25.9 17.2 %copy-start.4 = (bf16[768,256]{1,0:T(8,128)(2,1)}, bf16[768,256]{1,0:T(8,128)(2,1)S(1)}, u32[]{:S(2)}) copy-start(bf16[768,256]{1,0:T(8,128)(2,1)S(1)} %collective-permute-done.5.refs_5_) | copy-start | bytes 1179652
  25.9 16.7 %collective-permute-start.10 = (bf16[768,256]{1,0:T(8,128)(2,1)S(1)}, bf16[768,256]{1,0:T(8,128)(2,1)S(1)}, u32[]{:S(2)}, u32[]{:S(2)}) collective-permute-start(bf16[768,256]{1,0:T(8,128)(2,1)S(1)} %collective-permute-done.7.refs_7_), channel_id=1, source_target_pairs={{0,4},{4,0},{8,12},{12,8},{16,20},{20,16},{24,28},{28,24},{1,5},{5... | collective-permute-start | bytes 1179656 | tf_op jit(solution)/shard_map/ppermute | solution.py:45
  40.8 2.3 %copy-start.5 = (bf16[768,256]{1,0:T(8,128)(2,1)}, bf16[768,256]{1,0:T(8,128)(2,1)S(1)}, u32[]{:S(2)}) copy-start(bf16[768,256]{1,0:T(8,128)(2,1)S(1)} %collective-permute-done.6.refs_6_) | copy-start | bytes 1179652
  40.8 1.8 %collective-permute-start.8 = (bf16[768,256]{1,0:T(8,128)(2,1)S(1)}, bf16[768,256]{1,0:T(8,128)(2,1)S(1)}, u32[]{:S(2)}, u32[]{:S(2)}) collective-permute-start(bf16[768,256]{1,0:T(8,128)(2,1)S(1)} %collective-permute-done.5.refs_5_), channel_id=1, source_target_pairs={{0,4},{4,0},{8,12},{12,8},{16,20},{20,16},{24,28},{28,24},{1,5},{5... | collective-permute-start | bytes 1179656 | tf_op jit(solution)/shard_map/ppermute | solution.py:45
  40.8 2.3 %collective-permute-start.9 = (bf16[768,256]{1,0:T(8,128)(2,1)S(1)}, bf16[768,256]{1,0:T(8,128)(2,1)S(1)}, u32[]{:S(2)}, u32[]{:S(2)}) collective-permute-start(bf16[768,256]{1,0:T(8,128)(2,1)S(1)} %collective-permute-done.6.refs_6_), channel_id=1, source_target_pairs={{0,4},{4,0},{8,12},{12,8},{16,20},{20,16},{24,28},{28,24},{1,5},{5... | collective-permute-start | bytes 1179656 | tf_op jit(solution)/shard_map/ppermute | solution.py:45
  42.6 0.8 copy-start.6
  42.6 0.9 copy-start.7
  43.5 0.8 copy-start.8
  52.6 19.6 %copy-start.15 = (f32[176,128]{1,0:T(8,128)S(1)}, f32[176,128]{1,0:T(8,128)}, u32[]{:S(2)}) copy-start(f32[176,128]{1,0:T(8,128)} %get-tuple-element.23) | copy-start | bytes 270340
  52.6 8.1 %collective-permute-start.11 = (f32[392,128]{1,0:T(8,128)}, f32[392,128]{1,0:T(8,128)S(1)}, u32[]{:S(2)}, u32[]{:S(2)}) collective-permute-start(f32[392,128]{1,0:T(8,128)} %get-tuple-element.20), channel_id=1, source_target_pairs={{0,8},{4,12},{8,0},{12,4},{16,24},{20,28},{24,16},{28,20},{1,9},{5... | collective-permute-start | bytes 602120 | tf_op jit(solution)/shard_map/ppermute | solution.py:45
  54.1 11.2 %collective-permute-start.12 = (f32[392,128]{1,0:T(8,128)}, f32[392,128]{1,0:T(8,128)S(1)}, u32[]{:S(2)}, u32[]{:S(2)}) collective-permute-start(f32[392,128]{1,0:T(8,128)} %get-tuple-element.21), channel_id=1, source_target_pairs={{0,16},{4,20},{8,24},{12,28},{16,0},{20,4},{24,8},{28,12},{1,17},{... | collective-permute-start | bytes 602120 | tf_op jit(solution)/shard_map/ppermute | solution.py:45
  55.7 9.7 %collective-permute-start.13 = (f32[392,128]{1,0:T(8,128)}, f32[392,128]{1,0:T(8,128)S(1)}, u32[]{:S(2)}, u32[]{:S(2)}) collective-permute-start(f32[392,128]{1,0:T(8,128)} %get-tuple-element.22), channel_id=1, source_target_pairs={{0,24},{4,28},{8,16},{12,20},{16,8},{20,12},{24,0},{28,4},{1,25},{... | collective-permute-start | bytes 602120 | tf_op jit(solution)/shard_map/ppermute | solution.py:45
  56.1 14.8 %collective-permute-start.19 = (f32[176,128]{1,0:T(8,128)}, f32[176,128]{1,0:T(8,128)S(1)}, u32[]{:S(2)}, u32[]{:S(2)}) collective-permute-start(f32[176,128]{1,0:T(8,128)} %get-tuple-element.23), channel_id=1, source_target_pairs={{0,3},{1,2},{2,1},{3,0},{4,7},{5,6},{6,5},{7,4},{8,11},{9,10},{10,... | collective-permute-start | bytes 270344 | tf_op jit(solution)/shard_map/ppermute | solution.py:45
  58.7 13.6 %collective-permute-start.17 = (f32[176,128]{1,0:T(8,128)}, f32[176,128]{1,0:T(8,128)S(1)}, u32[]{:S(2)}, u32[]{:S(2)}) collective-permute-start(f32[176,128]{1,0:T(8,128)} %get-tuple-element.23), channel_id=1, source_target_pairs={{0,1},{1,0},{2,3},{3,2},{4,5},{5,4},{6,7},{7,6},{8,9},{9,8},{10,11... | collective-permute-start | bytes 270344 | tf_op jit(solution)/shard_map/ppermute | solution.py:45
  60.7 11.5 %collective-permute-start.18 = (f32[176,128]{1,0:T(8,128)}, f32[176,128]{1,0:T(8,128)S(1)}, u32[]{:S(2)}, u32[]{:S(2)}) collective-permute-start(f32[176,128]{1,0:T(8,128)} %get-tuple-element.23), channel_id=1, source_target_pairs={{0,2},{1,3},{2,0},{3,1},{4,6},{5,7},{6,4},{7,5},{8,10},{9,11},{10,... | collective-permute-start | bytes 270344 | tf_op jit(solution)/shard_map/ppermute | solution.py:45
  67.8 6.7 %collective-permute-start.14 = (f16[392,128]{1,0:T(8,128)(2,1)S(1)}, f16[392,128]{1,0:T(8,128)(2,1)S(1)}, u32[]{:S(2)}, u32[]{:S(2)}) collective-permute-start(f16[392,128]{1,0:T(8,128)(2,1)S(1)} %concatenate.11), channel_id=1, source_target_pairs={{0,1},{1,0},{2,3},{3,2},{4,5},{5,4},{6,7},{7,6},{8,9},{9,8},{10,11... | collective-permute-start | bytes 301064 | tf_op jit(solution)/shard_map/ppermute | solution.py:45
  67.9 10.2 %collective-permute-start.15 = (f16[392,128]{1,0:T(8,128)(2,1)S(1)}, f16[392,128]{1,0:T(8,128)(2,1)S(1)}, u32[]{:S(2)}, u32[]{:S(2)}) collective-permute-start(f16[392,128]{1,0:T(8,128)(2,1)S(1)} %concatenate.11), channel_id=1, source_target_pairs={{0,2},{1,3},{2,0},{3,1},{4,6},{5,7},{6,4},{7,5},{8,10},{9,11},{10,... | collective-permute-start | bytes 301064 | tf_op jit(solution)/shard_map/ppermute | solution.py:45
  70.9 7.1 %collective-permute-start.16 = (f16[392,128]{1,0:T(8,128)(2,1)S(1)}, f16[392,128]{1,0:T(8,128)(2,1)S(1)}, u32[]{:S(2)}, u32[]{:S(2)}) collective-permute-start(f16[392,128]{1,0:T(8,128)(2,1)S(1)} %concatenate.11), channel_id=1, source_target_pairs={{0,3},{1,2},{2,1},{3,0},{4,7},{5,6},{6,5},{7,4},{8,11},{9,10},{10,... | collective-permute-start | bytes 301064 | tf_op jit(solution)/shard_map/ppermute | solution.py:45
  72.3 26.1 %copy-start.2 = (f32[4,176,128]{2,1,0:T(8,128)}, f32[4,176,128]{2,1,0:T(8,128)S(1)}, u32[]{:S(2)}) copy-start(f32[4,176,128]{2,1,0:T(8,128)S(1)} %pad_maximum_fusion.1.refs_1_) | copy-start | bytes 1081348
  72.3 11.4 %collective-permute-start.20 = (f32[4,176,128]{2,1,0:T(8,128)S(1)}, f32[4,176,128]{2,1,0:T(8,128)S(1)}, u32[]{:S(2)}, u32[]{:S(2)}) collective-permute-start(f32[4,176,128]{2,1,0:T(8,128)S(1)} %pad_maximum_fusion.1.refs_1_), channel_id=1, source_target_pairs={{0,8},{4,12},{8,0},{12,4},{16,24},{20,28},{24,16},{28,20},{1,9},{5... | collective-permute-start | bytes 1081352 | tf_op jit(solution)/shard_map/ppermute | solution.py:45
  73.6 16.3 %collective-permute-start.21 = (f32[4,176,128]{2,1,0:T(8,128)S(1)}, f32[4,176,128]{2,1,0:T(8,128)S(1)}, u32[]{:S(2)}, u32[]{:S(2)}) collective-permute-start(f32[4,176,128]{2,1,0:T(8,128)S(1)} %pad_maximum_fusion.1.refs_1_), channel_id=1, source_target_pairs={{0,16},{4,20},{8,24},{12,28},{16,0},{20,4},{24,8},{28,12},{1,17},{... | collective-permute-start | bytes 1081352 | tf_op jit(solution)/shard_map/ppermute | solution.py:45
  74.5 15.3 %collective-permute-start.22 = (f32[4,176,128]{2,1,0:T(8,128)S(1)}, f32[4,176,128]{2,1,0:T(8,128)S(1)}, u32[]{:S(2)}, u32[]{:S(2)}) collective-permute-start(f32[4,176,128]{2,1,0:T(8,128)S(1)} %pad_maximum_fusion.1.refs_1_), channel_id=1, source_target_pairs={{0,24},{4,28},{8,16},{12,20},{16,8},{20,12},{24,0},{28,4},{1,25},{... | collective-permute-start | bytes 1081352 | tf_op jit(solution)/shard_map/ppermute | solution.py:45
  83.7 14.6 %copy-start.9 = (f32[4,176,128]{2,1,0:T(8,128)}, f32[4,176,128]{2,1,0:T(8,128)S(1)}, u32[]{:S(2)}) copy-start(f32[4,176,128]{2,1,0:T(8,128)S(1)} %collective-permute-done.20.refs_2_) | copy-start | bytes 1081348
  89.8 8.5 %copy-start.10 = (f32[4,176,128]{2,1,0:T(8,128)}, f32[4,176,128]{2,1,0:T(8,128)S(1)}, u32[]{:S(2)}) copy-start(f32[4,176,128]{2,1,0:T(8,128)S(1)} %collective-permute-done.21.refs_3_) | copy-start | bytes 1081348
  89.8 8.5 %copy-start.11 = (f32[4,176,128]{2,1,0:T(8,128)}, f32[4,176,128]{2,1,0:T(8,128)S(1)}, u32[]{:S(2)}) copy-start(f32[4,176,128]{2,1,0:T(8,128)S(1)} %collective-permute-done.22.refs_4_) | copy-start | bytes 1081348
  89.8 4.7 %collective-permute-start.23 = (f16[392,128]{1,0:T(8,128)(2,1)S(1)}, f16[392,128]{1,0:T(8,128)(2,1)S(1)}, u32[]{:S(2)}, u32[]{:S(2)}) collective-permute-start(f16[392,128]{1,0:T(8,128)(2,1)S(1)} %pad_maximum_fusion.2), channel_id=1, source_target_pairs={{0,8},{4,12},{8,0},{12,4},{16,24},{20,28},{24,16},{28,20},{1,9},{5... | collective-permute-start | bytes 301064 | tf_op jit(solution)/shard_map/ppermute | solution.py:45
  90.5 4.6 %collective-permute-start.24 = (f16[392,128]{1,0:T(8,128)(2,1)S(1)}, f16[392,128]{1,0:T(8,128)(2,1)S(1)}, u32[]{:S(2)}, u32[]{:S(2)}) collective-permute-start(f16[392,128]{1,0:T(8,128)(2,1)S(1)} %pad_maximum_fusion.2), channel_id=1, source_target_pairs={{0,16},{4,20},{8,24},{12,28},{16,0},{20,4},{24,8},{28,12},{1,17},{... | collective-permute-start | bytes 301064 | tf_op jit(solution)/shard_map/ppermute | solution.py:45
  91.6 5.5 %collective-permute-start.25 = (f16[392,128]{1,0:T(8,128)(2,1)S(1)}, f16[392,128]{1,0:T(8,128)(2,1)S(1)}, u32[]{:S(2)}, u32[]{:S(2)}) collective-permute-start(f16[392,128]{1,0:T(8,128)(2,1)S(1)} %pad_maximum_fusion.2), channel_id=1, source_target_pairs={{0,24},{4,28},{8,16},{12,20},{16,8},{20,12},{24,0},{28,4},{1,25},{... | collective-permute-start | bytes 301064 | tf_op jit(solution)/shard_map/ppermute | solution.py:45
  93.4 4.0 %collective-permute-start.27 = (f32[4,176,128]{2,1,0:T(8,128)S(1)}, f32[4,176,128]{2,1,0:T(8,128)S(1)}, u32[]{:S(2)}, u32[]{:S(2)}) collective-permute-start(f32[4,176,128]{2,1,0:T(8,128)S(1)} %pad_maximum_fusion.1.refs_1_), channel_id=1, source_target_pairs={{0,4},{4,0},{8,12},{12,8},{16,20},{20,16},{24,28},{28,24},{1,5},{5... | collective-permute-start | bytes 1081352 | tf_op jit(solution)/shard_map/ppermute | solution.py:45
  93.5 4.0 %collective-permute-start.28 = (f32[4,176,128]{2,1,0:T(8,128)S(1)}, f32[4,176,128]{2,1,0:T(8,128)S(1)}, u32[]{:S(2)}, u32[]{:S(2)}) collective-permute-start(f32[4,176,128]{2,1,0:T(8,128)S(1)} %collective-permute-done.20.refs_2_), channel_id=1, source_target_pairs={{0,4},{4,0},{8,12},{12,8},{16,20},{20,16},{24,28},{28,24},{1,5},{5... | collective-permute-start | bytes 1081352 | tf_op jit(solution)/shard_map/ppermute | solution.py:45
  94.5 3.0 %collective-permute-start.29 = (f32[4,176,128]{2,1,0:T(8,128)S(1)}, f32[4,176,128]{2,1,0:T(8,128)S(1)}, u32[]{:S(2)}, u32[]{:S(2)}) collective-permute-start(f32[4,176,128]{2,1,0:T(8,128)S(1)} %collective-permute-done.21.refs_3_), channel_id=1, source_target_pairs={{0,4},{4,0},{8,12},{12,8},{16,20},{20,16},{24,28},{28,24},{1,5},{5... | collective-permute-start | bytes 1081352 | tf_op jit(solution)/shard_map/ppermute | solution.py:45
  95.2 3.2 %collective-permute-start.30 = (f32[4,176,128]{2,1,0:T(8,128)S(1)}, f32[4,176,128]{2,1,0:T(8,128)}, u32[]{:S(2)}, u32[]{:S(2)}) collective-permute-start(f32[4,176,128]{2,1,0:T(8,128)S(1)} %collective-permute-done.22.refs_4_), channel_id=1, source_target_pairs={{0,4},{4,0},{8,12},{12,8},{16,20},{20,16},{24,28},{28,24},{1,5},{5... | collective-permute-start | bytes 1081352 | tf_op jit(solution)/shard_map/ppermute | solution.py:45
  97.3 5.5 %collective-permute-start.26 = (f16[4,392,128]{2,1,0:T(8,128)(2,1)S(1)}, f16[4,392,128]{2,1,0:T(8,128)(2,1)S(1)}, u32[]{:S(2)}, u32[]{:S(2)}) collective-permute-start(f16[4,392,128]{2,1,0:T(8,128)(2,1)S(1)} %pad_maximum_fusion), channel_id=1, source_target_pairs={{0,4},{4,0},{8,12},{12,8},{16,20},{20,16},{24,28},{28,24},{1,5},{5... | collective-permute-start | bytes 1204232 | tf_op jit(solution)/shard_map/ppermute | solution.py:45
  97.5 0.9 copy-start.12
  97.5 1.0 copy-start.13
  97.5 0.8 copy-start.14

commit v4 on v3

--- a/solution.py
+++ b/solution.py
@@ -1,4 +1,5 @@
 import functools
+import math
 
 import jax
 import jax.numpy as jnp
@@ -13,7 +14,7 @@
 PANEL = 32
 REPEAT = 4
 SHIFT = 2.0**-15
-WIDE = 256
+WIDE = 512
 ORTHO_TOL = 2.0**-8
 NN = ((1,), (0,))
 TN = ((0,), (0,))
@@ -22,6 +23,7 @@
 bf16 = jnp.bfloat16
 f16 = jnp.float16
 TOP = 14.0
+TINY = 2.0**-100
 VMEM = pl.BlockSpec(memory_space=pltpu.VMEM)
 ANY = pl.BlockSpec(memory_space=pl.ANY)
 SMEM = pl.BlockSpec(memory_space=pltpu.SMEM)
@@ -37,7 +39,12 @@
 
 
 def dot_split(left, right, dims):
-    return dot(left[0], right[0], dims) + dot(left[0], right[1], dims) + dot(left[1], right[0], dims)
+    (k_left,), (k_right,) = dims
+    return dot(
+        jnp.concatenate([left[0], left[0], left[1]], axis=k_left),
+        jnp.concatenate([right[0], right[1], right[0]], axis=k_right),
+        dims,
+    )
 
 
 def swap(value, axis, offset):
@@ -69,13 +76,22 @@
     return jnp.stack([value] + [swap(value, axis, offset) for offset in offsets])
 
 
-def encode(value, power):
-    return jnp.concatenate([value * jnp.exp2(TOP - power[:1]), power]).astype(f16)
+def encode(value):
+    power = jnp.floor(jnp.log2(jnp.maximum(value[-SUB:], TINY))) + 1
+    scaled = value[:-SUB].reshape(-1, SUB, LANES) * jnp.exp2(TOP - power)
+    return jnp.concatenate([scaled.reshape(-1, LANES), power]).astype(f16)
 
 
 def decode(coded):
-    value, power = coded[:-SUB].astype(f32), coded[-SUB : 1 - SUB].astype(f32)
-    return value * jnp.exp2(power - TOP)
+    value = coded.astype(f32)
+    bound = jnp.exp2(value[-SUB:])
+    scaled = value[:-SUB].reshape(-1, SUB, LANES) * (bound * 2.0**-TOP)
+    return jnp.concatenate([scaled.reshape(-1, LANES), bound])
+
+
+def largest(value):
+    groups = [jnp.abs(value[rows]) for rows in spans(value.shape[0] // SUB, SUB)]
+    return functools.reduce(jnp.maximum, groups)
 
 
 def diagonal_kernel(bases, out):
@@ -97,34 +113,34 @@
     rows[...] = both[:sub_rows]
     index = 2 * chip + core
     share, size = start.shape[0] // lax.axis_size("rows"), start.shape[1]
-    part = message.shape[0] - share * size // LANES
+    part = message.shape[0] - share * size // LANES - 2 * SUB
     message[:part] = diagonal[pl.ds(pl.multiple_of(index * part, SUB), part), :]
+    message[part : part + SUB] = largest(message[:part])
+    lower = part + SUB
     for k, lanes in enumerate(spans(size // LANES, LANES)):
         first = pl.multiple_of(index * share, SUB)
-        message[part + k * share : part + (k + 1) * share] = start[pl.ds(first, share), lanes]
-
-    def add_squares(k, total):
-        chunk = both[pl.ds(pl.multiple_of(k * LANES, LANES), LANES), :].astype(f32)
-        chunk = chunk * chunk
-        return total + sum(chunk[r, c] for r in spans(LANES // SUB, SUB) for c in spans(chunk.shape[1] // LANES, LANES))
-
-    energy = lax.fori_loop(0, both.shape[0] // LANES, add_squares, jnp.zeros((SUB, LANES), f32))
+        message[lower + k * share : lower + (k + 1) * share] = start[pl.ds(first, share), lanes]
+    message[lower + size // LANES * share :] = largest(message[lower : lower + size // LANES * share])
     for offset, out in enumerate(outs):
         share = out.shape[0] // LANES
-        out[share * LANES :] = energy
         owner = 2 * lax.bitwise_xor(chip, offset) + core
+        bound = jnp.zeros((SUB, LANES), f32)
         for j, at in enumerate(spans(share, LANES)):
             place = 2 * (owner * share + j)
             left = pl.multiple_of(table[place] * LANES, LANES)
             right = pl.multiple_of(table[place + 1] * LANES, LANES)
-            out[at] = dot(both[:, pl.ds(left, LANES)], both[:, pl.ds(right, LANES)], TN)
+            tile = dot(both[:, pl.ds(left, LANES)], both[:, pl.ds(right, LANES)], TN)
+            out[at] = tile
+            bound = jnp.maximum(bound, largest(tile))
+        out[share * LANES :] = bound
 
 
 def spread(value, index):
     return jnp.broadcast_to(value[index : index + 1, :], value.shape)
 
 
-def factor_block(work):
+def factor_block(work, background=()):
+    background = list(background)
     groups = PANEL // SUB
     sub = lax.broadcasted_iota(jnp.int32, (SUB, LANES), 0)
     for r0 in range(0, LANES, PANEL):
@@ -137,11 +153,17 @@
             for g in range(j // SUB, groups):
                 col[j, g] = jnp.broadcast_to(m[g][0][:, r0 + j : r0 + j + 1], (SUB, LANES))
         scale = [None] * groups
+        pivot = spread(col[0, 0], 0)
         for j in range(PANEL):
             gj, sj = divmod(j, SUB)
-            pivot = spread(col[j, gj], sj)
             inverse = 1.0 / pivot
             root = lax.rsqrt(pivot)
+            if j + 1 < PANEL:
+                g, k = divmod(j + 1, SUB)
+                entry = spread(col[j, g], k)
+                pivot = spread(col[j + 1, g], k) - entry * entry * inverse
+            if background and j % 8 == 4:
+                background.pop(0)()
             scale[gj] = root if scale[gj] is None else jnp.where(sub == sj, root, scale[gj])
             source = [spread(m[gj][t], sj) for t in range(2)]
             scaled = {g: col[j, g] * inverse for g in range(gj, groups)}
@@ -169,26 +191,44 @@
     return lax.broadcasted_iota(jnp.int32, (size, size), 0) == lax.broadcasted_iota(jnp.int32, (size, size), 1)
 
 
-def inverse_factor(a, e, x, work):
+def pair_of(ref, *at):
+    return ref[0, *at], ref[1, *at]
+
+
+def orthonormal_rows(a, rest, upper, work, out):
     size = a.shape[0]
-    e[...] = identity(size).astype(f32)
+    blocks = size // LANES
     lanes = lax.broadcasted_iota(jnp.int32, (LANES, size), 1)
+    upper[...] = jnp.zeros(upper.shape, bf16)
 
     def block(k, carry):
         at = pl.ds(pl.multiple_of(k * LANES, LANES), LANES)
+        last = pl.ds(pl.multiple_of(jnp.maximum(k - 1, 0) * LANES, LANES), LANES)
+        following = pl.ds(pl.multiple_of(jnp.minimum(k + 1, blocks - 1) * LANES, LANES), LANES)
         work[:, :LANES] = a[at, at]
         work[:, LANES:] = identity(LANES).astype(f32)
-        factor_block(work)
+        before = pair_of(upper)
+        later = [jnp.where(lanes >= (k + 1) * LANES, part.astype(f32), 0.0).astype(bf16) for part in before]
+        known = pair_of(out, last)
+
+        def update(ref, rows, left, right):
+            left = [part[:, rows] for part in left]
+            ref[rows] = ref[rows] - dot_split(left, right, TN)
+
+        background = [
+            functools.partial(update, ref, rows, left, right)
+            for ref, left, right in ((a, later, before), (rest, before, known))
+            for rows in spans(blocks, LANES)
+        ]
+        factor_block(work, background)
         own = split(work[:, LANES:])
-        x_rows = dot_split(own, split(e[at, :]), NN)
-        x[at, :] = x_rows
-        upper = dot_split(own, split(a[at, :]), NN)
-        upper = split(jnp.where(lanes >= (k + 1) * LANES, upper, 0.0))
-        a[...] = a[...] - dot_split(upper, upper, TN)
-        e[...] = e[...] - dot_split(upper, split(x_rows), TN)
+        rows = dot_split(own, split(a[at, :]), NN)
+        upper[0], upper[1] = split(jnp.where(lanes >= (k + 1) * LANES, rows, 0.0))
+        out[0, at], out[1, at] = split(dot_split(own, split(rest[at, :]), NN))
+        a[following, :] = a[following, :] - dot_split(pair_of(upper, slice(None), following), pair_of(upper), TN)
         return carry
 
-    lax.fori_loop(0, size // LANES, block, 0)
+    lax.fori_loop(0, blocks, block, 0)
 
 
 def prepare_kernel(at_ref, *refs):
@@ -207,7 +247,7 @@
             diagonal[group, pl.ds(pl.multiple_of(row * part, SUB), part), :] = block[z, :part, :]
             first = pl.multiple_of(group * basis + row * share, SUB)
             for k, lanes in enumerate(spans(size // LANES, LANES)):
-                lower = part + k * share
+                lower = part + SUB + k * share
                 whole[pl.ds(first, share), lanes] = block[z, lower : lower + share, :]
     for rows in spans(columns // LANES, LANES):
         high[:, rows], low[:, rows] = split(whole[rows, :].T)
@@ -233,14 +273,13 @@
     def place(k, carry):
         other, offset = k // (devices // 2), lax.rem(k, devices // 2)
         owner = 2 * lax.bitwise_xor(chip, offset) + lax.bitwise_xor(core, other)
-        unit = jnp.exp2(cross[k, share * LANES : share * LANES + 1, :] - TOP) * factor
         for j, inner in enumerate(spans(share, LANES)):
             at = 2 * (owner * share + j)
             row = pl.ds(pl.multiple_of(table[at] * LANES, LANES), LANES)
             column = pl.ds(pl.multiple_of(table[at + 1] * LANES, LANES), LANES)
-            for ref, value in zip(pair, split(cross[k, inner, :] * unit)):
-                ref[row, column] = value
-                ref[column, row] = value.T
+            tile = cross[k, inner, :] * factor
+            pair[0][row, column], pair[1][row, column] = split(tile)
+            pair[0][column, row], pair[1][column, row] = split(tile.T)
         return carry
 
     lax.fori_loop(0, devices, place, 0)
@@ -253,78 +292,89 @@
                     ref[columns, rows] = value.T
 
 
-def solve_kernel(at_ref, table, cross, diagonal, sh, sl, rows, modes, ah, al, ph, plo, qh, ql, a, e, x, work):
+def solve_kernel(at_ref, table, cross, diagonal, sh, sl, rows, modes, ah, al, lifted, q, a, rest, upper, work):
     size, columns = sh.shape
     per_basis = columns // LANES // diagonal.shape[0]
-    gram, p, q = (ah, al), (ph, plo), (qh, ql)
+    gram = (ah, al)
     factor = 1.0 / (trace_of(diagonal, per_basis) / columns)
     place_gram(at_ref, table, cross, diagonal, factor, gram)
 
     def lift(source, target):
+        left = pair_of(source)
+
         def chunk(n, carry):
             at = pl.ds(pl.multiple_of(n * WIDE, WIDE), WIDE)
-            before = source[0][:, at].astype(f32) + source[1][:, at].astype(f32)
-            after = before + dot_split((source[0][...], source[1][...]), (gram[0][:, at], gram[1][:, at]), NN)
-            target[0][:, at], target[1][:, at] = split(after)
+            before = source[0, :, at].astype(f32) + source[1, :, at].astype(f32)
+            after = before + dot_split(left, (gram[0][:, at], gram[1][:, at]), NN)
+            rest[:, at] = after
+            target[0, :, at], target[1, :, at] = split(after)
             return carry
 
         lax.fori_loop(0, columns // WIDE, chunk, 0)
 
-    def correlate():
+    def turn_of(step):
+        return lax.rem(step + REPEAT - 1, REPEAT)
+
+    def normalise(carry):
+        step, failed = carry
+        turn = turn_of(step)
+
+        @pl.when(step < 2)
+        def _():
+            q[0], q[1] = sh[...], sl[...]
+
+        @pl.when(step == 0)
+        def _():
+            lift(q, lifted)
+            q[...] = lifted[...]
+
+        @pl.when((step == 0) | (turn == 0))
+        def _():
+            lift(q, lifted)
+
+        @pl.when((step != 0) & (turn != 0))
+        def _():
+            lifted[...] = q[...]
+            rest[...] = q[0].astype(f32) + q[1].astype(f32)
+
+        for at in spans(size // (2 * LANES), 2 * LANES):
+            a[at, at.start :] = dot_split(pair_of(lifted, at), pair_of(lifted, slice(at.start, None)), NT)
+
+        @pl.when((step != 0) & (turn < 2))
+        def _():
+            eye = identity(LANES)
+            tiles = [a[at, at] for at in spans(size // LANES, LANES)]
+            shift = SHIFT * jnp.sum(sum(jnp.where(eye, tile, 0.0) for tile in tiles))
+            for at, tile in zip(spans(size // LANES, LANES), tiles):
+                a[at, at] = tile + jnp.where(eye, shift, 0.0)
+
+        orthonormal_rows(a, rest, upper, work, q)
+
+        worst = jnp.zeros((LANES, 1), f32)
         for at in spans(size // LANES, LANES):
-            a[at, at.start :] = dot_split((ph[at], plo[at]), (ph[at.start :], plo[at.start :]), NT)
-
-    def rotate():
-        for at in spans(size // LANES, LANES):
-            turned = dot_split(split(x[at, : at.stop]), (ph[: at.stop], plo[: at.stop]), NN)
-            qh[at], ql[at] = split(turned)
-
-    lift((sh, sl), q)
-    lift(q, p)
-    correlate()
-    inverse_factor(a, e, x, work)
-    rotate()
-
-    worst = jnp.zeros((), f32)
-    for at in spans(size // LANES, LANES):
-        gap = dot(qh[at], qh[...], NT)
-        here = lax.broadcasted_iota(jnp.int32, gap.shape, 0) + at.start == lax.broadcasted_iota(jnp.int32, gap.shape, 1)
-        gap = gap - here.astype(f32)
-        worst = jnp.maximum(worst, jnp.max(jnp.sum(gap * gap, axis=1, keepdims=True)))
-
-    @pl.when(jnp.logical_not(worst < ORTHO_TOL**2))
-    def _():
-        qh[...], ql[...] = sh[...], sl[...]
-
-        def again(k, carry):
-            turn = lax.rem(k, REPEAT)
-
-            @pl.when(turn == 0)
-            def _():
-                lift(q, p)
-
-            @pl.when(turn != 0)
-            def _():
-                ph[...], plo[...] = qh[...], ql[...]
-
-            correlate()
-
-            @pl.when(turn < 2)
-            def _():
-                eye = identity(LANES)
-                tiles = [a[at, at] for at in spans(size // LANES, LANES)]
-                shift = SHIFT * jnp.sum(sum(jnp.where(eye, tile, 0.0) for tile in tiles))
-                for at, tile in zip(spans(size // LANES, LANES), tiles):
-                    a[at, at] = tile + jnp.where(eye, shift, 0.0)
-
-            inverse_factor(a, e, x, work)
-            rotate()
-            return carry
-
-        lax.fori_loop(0, ITERS * REPEAT, again, 0)
-
-    for lo in range(0, size, WIDE):
-        modes[:, lo : lo + WIDE] = dot(rows[...], qh[lo : lo + WIDE], NT).astype(bf16)
+            gap = dot(q[0, at], q[0], NT)
+            here = lax.broadcasted_iota(jnp.int32, gap.shape, 0) + at.start == lax.broadcasted_iota(jnp.int32, gap.shape, 1)
+            gap = gap - here.astype(f32)
+            worst = jnp.maximum(worst, jnp.sum(gap * gap, axis=1, keepdims=True))
+        worst = jnp.max(worst)
+        for at in spans(size // WIDE, WIDE):
+            modes[:, at] = dot(rows[...], q[0, at], NT).astype(bf16)
+        good = worst < ORTHO_TOL**2
+        return step + 1, jnp.where((step == 0) & good, 0, failed)
+
+    lax.while_loop(
+        lambda carry: (carry[0] == 0) | ((carry[1] == 1) & (carry[0] <= ITERS * REPEAT)),
+        normalise,
+        (jnp.int32(0), jnp.int32(1)),
+    )
+
+
+def scratch_of(size, columns):
+    return (
+        [((columns, columns), bf16)] * 2
+        + [((2, size, columns), bf16)] * 2
+        + [((size, size), f32), ((size, columns), f32), ((2, LANES, size), bf16), ((LANES, 2 * LANES), f32)]
+    )
 
 
 def on_device(bases, start):
@@ -345,13 +395,15 @@
         def body(*refs):
             kernel(*refs[: len(args)], *refs[len(args) + len(after) :])
 
+        held = [(a.shape, a.dtype) for a in args] + outs + scratch
+        room = sum(math.prod(shape) * jnp.dtype(dtype).itemsize for shape, dtype in held)
         return pl.pallas_call(
             body,
             out_shape=[jax.ShapeDtypeStruct(shape, dtype) for shape, dtype in outs],
             in_specs=[SMEM] * n_smem + [VMEM] * (len(args) - n_smem) + [ANY] * len(after),
             out_specs=[VMEM] * len(outs),
             scratch_shapes=[pltpu.VMEM(shape, dtype) for shape, dtype in scratch],
-            compiler_params=pltpu.CompilerParams(vmem_limit_bytes=60 << 20),
+            compiler_params=pltpu.CompilerParams(vmem_limit_bytes=(6 << 20) + room),
             cost_estimate=pl.CostEstimate(flops=flops, bytes_accessed=moved, transcendentals=0),
         )(*args, *after)
 
@@ -370,7 +422,7 @@
     diagonal = sum((swap(diagonal, "rows", offset) for offset in other_chips), diagonal)
 
     part = own_count * LANES // n_rows
-    message_rows = part + start.size // n_rows // LANES
+    message_rows = part + start.size // n_rows // LANES + 2 * SUB
     tile_rows = share * LANES
     rows, mine, *blocks = call(
         cross_kernel,
@@ -380,33 +432,33 @@
         flops=4 * sub_rows * chips * share * LANES * LANES, moved=6 << 20,
     )
     plane = sum((swap(block, "rows", offset) for block, offset in zip(blocks[1:], other_chips)), blocks[0])
-    power = jnp.floor(jnp.log2(jnp.sum(plane[tile_rows:]))) + 1
-    power = jnp.full((SUB, LANES), power, f32)
-    plane = encode(plane[:tile_rows], power)
-    planes = [plane] + [swap(plane, "batch", offset) for offset in other_batches]
-    total = sum(decode(value) for value in planes)
-    power = jnp.ceil(jnp.log2(sum(jnp.exp2(value[tile_rows:].astype(f32)) for value in planes)))
-    total = encode(total, power)
-
+    planes = encode(plane)
+    planes = [planes] + [swap(planes, "batch", offset) for offset in other_batches]
+    total = encode(sum(decode(value) for value in planes))
+
+    mine = jnp.concatenate([encode(mine[: part + SUB]), encode(mine[part + SUB :])])
     mine = spread_copy(mine, "batch", other_batches)
     mine = [mine] + [swap(mine, "rows", offset) for offset in other_chips]
     total, mine = lax.optimization_barrier((total, mine))
+
+    def decode_message(blocks):
+        return jnp.stack([jnp.concatenate([decode(b[: part + SUB]), decode(b[part + SUB :])]) for b in blocks])
+
     high, low, diagonal = call(
         prepare_kernel,
         [((size, columns), bf16)] * 2 + [((n_batch, own_count * LANES, LANES), f32)],
         [((columns, size), f32)],
-        at, *mine, *(swap(block, "rows", 1) for block in mine), n_smem=1, moved=8 << 20,
+        at, *map(decode_message, mine + [swap(block, "rows", 1) for block in mine]), n_smem=1, moved=8 << 20,
     )
 
     cross = spread_copy(total, "rows", other_chips)
-    cross = jnp.concatenate([cross, swap(cross, "rows", 1)]).astype(f32)
+    cross, high, low, diagonal = lax.optimization_barrier((cross, high, low, diagonal))
+    cross = jnp.concatenate([cross, swap(cross, "rows", 1)])
+    cross = jax.vmap(decode)(cross)
     (modes,) = call(
         solve_kernel,
         [((sub_rows, size), bf16)],
-        [((columns, columns), bf16)] * 2
-        + [((size, columns), bf16)] * 4
-        + [((size, size), f32)] * 3
-        + [((LANES, 2 * LANES), f32)],
+        scratch_of(size, columns),
         at, table, cross, diagonal, high, low, rows, n_smem=2, flops=10**10, moved=10 << 20,
     )
     return modes

time: 142 us -> 121 us (0.85)
  Pallas kernels: 52.8 us -> 36.3 us
  local copies, waits for them, and re-layouts: 4.62 us -> 1.58 us
    pallas_call x4, Pallas kernels: 52.8 us -> 36.3 us  [call(): pl.pallas_call(body, out_shape=[jax.ShapeDtypeStruct(shape, dtype) for sh...]
    unnamed x36 -> x6, local copies, waits for them, and re-layouts: 3.02 us -> 0.01 us
  transfers between devices with their start and end apart: 31 -> 31, of which waited for: 12 -> 15; matrix products, arithmetic and copies ran while one was open for 3% -> 3% of each run, Pallas kernels for 5% -> 1%
where the time goes in v4:
time: 121 us
  waiting for transfers between devices  45.7 us (38%)
  Pallas kernels  36.3 us (30%)
  starting transfers between devices  31.1 us (26%)
  other arithmetic  4.26 us (4%)
  between operations  1.83 us (2%)
  local copies, waits for them, and re-layouts  1.58 us (1%)
    ppermute x31, waiting for transfers between devices, swap(): return lax.ppermute(value, axis, [(i, i ^ offset) for i in range(size)])  45.7 us
    pallas_call x4, Pallas kernels, call(): pl.pallas_call(body, out_shape=[jax.ShapeDtypeStruct(shape, dtype) for sh...  36.3 us
    ppermute x31, starting transfers between devices, swap(): return lax.ppermute(value, axis, [(i, i ^ offset) for i in range(size)])  31.1 us
  transfers between devices with their start and end apart: 31, of which 15 were waited for; matrix products, arithmetic and copies ran while one was open for 3% of the time, Pallas kernels for 1%

profile of v4, /device:TPU:0, one launch (start us, length us, event | category | flops | bytes accessed | tf_op | source)
XLA Modules:
  0.0 120.8 jit_solution(1292069850836155013)
XLA Ops:
  0.0 1.6 %constant_dynamic-slice_fusion = (bf16[768,256]{1,0:T(8,128)(2,1)S(1)}, bf16[768,256]{1,0:T(8,128)(2,1)S(1)}, bf16[768,256]{1,0:T(8,128)(2,1)S(1)}, bf16[768,256]{1,0:T(8,128)(2,1)S(1)}) fusion(bf16[3072,256]{1,0:T(8,128)(2,1)} %refs_0_.1, s32[]{:T(128)S(6)} %select_n.28, s32[]{:T(128)S(6)} %select_n.26, s32[]{:T(128)S(6)} %select_n.25, s32[]{:T(128)S(6)} %select_n.27), kind=kLoop, calls=%fused_computation.547 | loop fusion | bytes 3145744 | tf_op jit(solution)/shard_map/dynamic_slice | solution.py:412
  1.6 0.5 collective-permute-start
  2.1 4.7 %collective-permute-start.7 = (bf16[768,256]{1,0:T(8,128)(2,1)S(1)}, bf16[768,256]{1,0:T(8,128)(2,1)S(1)}, u32[]{:S(2)}, u32[]{:S(2)}) collective-permute-start(bf16[768,256]{1,0:T(8,128)(2,1)S(1)} %get-tuple-element.45), channel_id=1, source_target_pairs={{0,3},{1,2},{2,1},{3,0},{4,7},{5,6},{6,5},{7,4},{8,11},{9,10},{10,... | collective-permute-start | bytes 1179656 | tf_op jit(solution)/shard_map/ppermute | solution.py:52
  6.8 0.0 collective-permute-start.5
  6.8 0.0 collective-permute-done.refs_1_.refs_8_
  6.8 0.8 shard_map.37
  7.6 0.2 collective-permute-start.1
  7.8 0.6 collective-permute-start.6
  8.4 0.7 collective-permute-done.1
  9.1 1.6 %collective-permute-start.2 = (f32[384,128]{1,0:T(8,128)S(1)}, f32[384,128]{1,0:T(8,128)}, u32[]{:S(2)}, u32[]{:S(2)}) collective-permute-start(f32[384,128]{1,0:T(8,128)S(1)} %add.61), channel_id=1, source_target_pairs={{0,8},{4,12},{8,0},{12,4},{16,24},{20,28},{24,16},{28,20},{1,9},{5... | collective-permute-start | bytes 589832 | tf_op jit(solution)/shard_map/ppermute | solution.py:52
  10.7 1.5 %collective-permute-start.3 = (f32[384,128]{1,0:T(8,128)S(1)}, f32[384,128]{1,0:T(8,128)}, u32[]{:S(2)}, u32[]{:S(2)}) collective-permute-start(f32[384,128]{1,0:T(8,128)S(1)} %add.61), channel_id=1, source_target_pairs={{0,16},{4,20},{8,24},{12,28},{16,0},{20,4},{24,8},{28,12},{1,17},{... | collective-permute-start | bytes 589832 | tf_op jit(solution)/shard_map/ppermute | solution.py:52
  12.2 4.6 %collective-permute-done.7.refs_7_ = bf16[768,256]{1,0:T(8,128)(2,1)S(1)} collective-permute-done((bf16[768,256]{1,0:T(8,128)(2,1)S(1)}, bf16[768,256]{1,0:T(8,128)(2,1)S(1)}, u32[]{:S(2)}, u32[]{:S(2)}) %collective-permute-start.7) | collective-permute-done | bytes 393248 | tf_op jit(solution)/shard_map/ppermute | solution.py:52
  16.8 2.6 %collective-permute-start.4 = (f32[384,128]{1,0:T(8,128)S(1)}, f32[384,128]{1,0:T(8,128)}, u32[]{:S(2)}, u32[]{:S(2)}) collective-permute-start(f32[384,128]{1,0:T(8,128)S(1)} %add.61), channel_id=1, source_target_pairs={{0,24},{4,28},{8,16},{12,20},{16,8},{20,12},{24,0},{28,4},{1,25},{... | collective-permute-start | bytes 589832 | tf_op jit(solution)/shard_map/ppermute | solution.py:52
  19.4 6.6 %collective-permute-done.5.refs_5_ = bf16[768,256]{1,0:T(8,128)(2,1)S(1)} collective-permute-done((bf16[768,256]{1,0:T(8,128)(2,1)S(1)}, bf16[768,256]{1,0:T(8,128)(2,1)S(1)}, u32[]{:S(2)}, u32[]{:S(2)}) %collective-permute-start.5) | collective-permute-done | bytes 393248 | tf_op jit(solution)/shard_map/ppermute | solution.py:52
  26.0 0.0 collective-permute-start.10
  26.1 14.9 %collective-permute-done.6.refs_6_ = bf16[768,256]{1,0:T(8,128)(2,1)S(1)} collective-permute-done((bf16[768,256]{1,0:T(8,128)(2,1)S(1)}, bf16[768,256]{1,0:T(8,128)(2,1)S(1)}, u32[]{:S(2)}, u32[]{:S(2)}) %collective-permute-start.6) | collective-permute-done | bytes 393248 | tf_op jit(solution)/shard_map/ppermute | solution.py:52
  40.9 0.5 collective-permute-start.9
  41.4 0.1 pad_add_fusion.refs_0_
  41.5 0.0 collective-permute-done.3
  41.5 1.2 add_add_fusion.1.refs_3_
  42.7 0.0 collective-permute-done.10.refs_11_
  42.7 0.4 collective-permute-done.8.refs_9_
  43.1 0.2 collective-permute-done.9.refs_10_
  43.4 4.1 %shard_map.38 = (bf16[768,1024]{1,0:T(8,128)(2,1)S(1)}, f32[192,128]{1,0:T(8,128)S(1)}, f32[392,128]{1,0:T(8,128)S(1)}, f32[392,128]{1,0:T(8,128)S(1)}, f32[392,128]{1,0:T(8,128)S(1)}, /*index=5*/f32[392,128]{1,0:T(8,128)S(1)}) custom-call(s32[3]{0:T(128)S(1)} %pad_add_fusion.refs_0_, s32[48]{0:T(128)S(1)} %copy-done.2, f32[256,512]{1,0:T(8,128)S(1)} %copy-done.1, ...), custom_call_target="tpu_custom_call" | custom-call | flops 603979776 | bytes 6291456 | tf_op jit(solution)/shard_map/pallas_call | solution.py:400
  47.6 0.1 collective-permute-start.17
  47.6 1.6 %collective-permute-start.11 = (f32[392,128]{1,0:T(8,128)S(1)}, f32[392,128]{1,0:T(8,128)S(1)}, u32[]{:S(2)}, u32[]{:S(2)}) collective-permute-start(f32[392,128]{1,0:T(8,128)S(1)} %get-tuple-element.24), channel_id=1, source_target_pairs={{0,8},{4,12},{8,0},{12,4},{16,24},{20,28},{24,16},{28,20},{1,9},{5... | collective-permute-start | bytes 602120 | tf_op jit(solution)/shard_map/ppermute | solution.py:52
  49.2 1.5 %collective-permute-start.12 = (f32[392,128]{1,0:T(8,128)S(1)}, f32[392,128]{1,0:T(8,128)S(1)}, u32[]{:S(2)}, u32[]{:S(2)}) collective-permute-start(f32[392,128]{1,0:T(8,128)S(1)} %get-tuple-element.25), channel_id=1, source_target_pairs={{0,16},{4,20},{8,24},{12,28},{16,0},{20,4},{24,8},{28,12},{1,17},{... | collective-permute-start | bytes 602120 | tf_op jit(solution)/shard_map/ppermute | solution.py:52
  50.7 0.5 collective-permute-start.13
  51.2 3.0 %collective-permute-start.18 = (f16[192,128]{1,0:T(8,128)(2,1)S(1)}, f16[192,128]{1,0:T(8,128)(2,1)S(1)}, u32[]{:S(2)}, u32[]{:S(2)}) collective-permute-start(f16[192,128]{1,0:T(8,128)(2,1)S(1)} %get-tuple-element.130), channel_id=1, source_target_pairs={{0,2},{1,3},{2,0},{3,1},{4,6},{5,7},{6,4},{7,5},{8,10},{9,11},{10,... | collective-permute-start | bytes 147464 | tf_op jit(solution)/shard_map/ppermute | solution.py:52
  54.2 1.3 %collective-permute-start.19 = (f16[192,128]{1,0:T(8,128)(2,1)S(1)}, f16[192,128]{1,0:T(8,128)(2,1)S(1)}, u32[]{:S(2)}, u32[]{:S(2)}) collective-permute-start(f16[192,128]{1,0:T(8,128)(2,1)S(1)} %get-tuple-element.130), channel_id=1, source_target_pairs={{0,3},{1,2},{2,1},{3,0},{4,7},{5,6},{6,5},{7,4},{8,11},{9,10},{10,... | collective-permute-start | bytes 147464 | tf_op jit(solution)/shard_map/ppermute | solution.py:52
  55.5 1.2 collective-permute-done.18
  56.7 3.4 %collective-permute-done.19 = f16[192,128]{1,0:T(8,128)(2,1)S(1)} collective-permute-done((f16[192,128]{1,0:T(8,128)(2,1)S(1)}, f16[192,128]{1,0:T(8,128)(2,1)S(1)}, u32[]{:S(2)}, u32[]{:S(2)}) %collective-permute-start.19) | collective-permute-done | bytes 49184 | tf_op jit(solution)/shard_map/ppermute | solution.py:52
  60.1 0.1 pad_maximum_fusion.10
  60.2 1.6 %collective-permute-start.20 = (f16[4,192,128]{2,1,0:T(8,128)(2,1)S(1)}, f16[4,192,128]{2,1,0:T(8,128)(2,1)S(1)}, u32[]{:S(2)}, u32[]{:S(2)}) collective-permute-start(f16[4,192,128]{2,1,0:T(8,128)(2,1)S(1)} %pad_maximum_fusion.10), channel_id=1, source_target_pairs={{0,8},{4,12},{8,0},{12,4},{16,24},{20,28},{24,16},{28,20},{1,9},{5... | collective-permute-start | bytes 589832 | tf_op jit(solution)/shard_map/ppermute | solution.py:52
  61.7 1.5 %collective-permute-start.21 = (f16[4,192,128]{2,1,0:T(8,128)(2,1)S(1)}, f16[4,192,128]{2,1,0:T(8,128)(2,1)S(1)}, u32[]{:S(2)}, u32[]{:S(2)}) collective-permute-start(f16[4,192,128]{2,1,0:T(8,128)(2,1)S(1)} %pad_maximum_fusion.10), channel_id=1, source_target_pairs={{0,16},{4,20},{8,24},{12,28},{16,0},{20,4},{24,8},{28,12},{1,17},{... | collective-permute-start | bytes 589832 | tf_op jit(solution)/shard_map/ppermute | solution.py:52
  63.3 0.5 collective-permute-start.22
  63.7 0.1 add_add_fusion
  63.9 0.1 collective-permute-start.14
  64.0 1.9 %collective-permute-start.15 = (f16[392,128]{1,0:T(8,128)(2,1)S(1)}, f16[392,128]{1,0:T(8,128)(2,1)S(1)}, u32[]{:S(2)}, u32[]{:S(2)}) collective-permute-start(f16[392,128]{1,0:T(8,128)(2,1)S(1)} %get-tuple-element.124), channel_id=1, source_target_pairs={{0,2},{1,3},{2,0},{3,1},{4,6},{5,7},{6,4},{7,5},{8,10},{9,11},{10,... | collective-permute-start | bytes 301064 | tf_op jit(solution)/shard_map/ppermute | solution.py:52
  65.9 2.7 %collective-permute-done.14 = f16[392,128]{1,0:T(8,128)(2,1)S(1)} collective-permute-done((f16[392,128]{1,0:T(8,128)(2,1)S(1)}, f16[392,128]{1,0:T(8,128)(2,1)S(1)}, u32[]{:S(2)}, u32[]{:S(2)}) %collective-permute-start.14) | collective-permute-done | bytes 100384 | tf_op jit(solution)/shard_map/ppermute | solution.py:52
  68.6 1.3 %collective-permute-start.16 = (f16[392,128]{1,0:T(8,128)(2,1)S(1)}, f16[392,128]{1,0:T(8,128)(2,1)S(1)}, u32[]{:S(2)}, u32[]{:S(2)}) collective-permute-start(f16[392,128]{1,0:T(8,128)(2,1)S(1)} %get-tuple-element.124), channel_id=1, source_target_pairs={{0,3},{1,2},{2,1},{3,0},{4,7},{5,6},{6,5},{7,4},{8,11},{9,10},{10,... | collective-permute-start | bytes 301064 | tf_op jit(solution)/shard_map/ppermute | solution.py:52
  70.0 1.8 %collective-permute-done.15 = f16[392,128]{1,0:T(8,128)(2,1)S(1)} collective-permute-done((f16[392,128]{1,0:T(8,128)(2,1)S(1)}, f16[392,128]{1,0:T(8,128)(2,1)S(1)}, u32[]{:S(2)}, u32[]{:S(2)}) %collective-permute-start.15) | collective-permute-done | bytes 100384 | tf_op jit(solution)/shard_map/ppermute | solution.py:52
  71.8 3.2 %collective-permute-done.16 = f16[392,128]{1,0:T(8,128)(2,1)S(1)} collective-permute-done((f16[392,128]{1,0:T(8,128)(2,1)S(1)}, f16[392,128]{1,0:T(8,128)(2,1)S(1)}, u32[]{:S(2)}, u32[]{:S(2)}) %collective-permute-start.16) | collective-permute-done | bytes 100384 | tf_op jit(solution)/shard_map/ppermute | solution.py:52
  75.3 0.0 collective-permute-done.21
  75.3 0.0 collective-permute-done.22
  75.3 0.1 collective-permute-start.29
  75.4 0.5 collective-permute-start.28
  76.9 1.6 %collective-permute-start.23 = (f16[392,128]{1,0:T(8,128)(2,1)S(1)}, f16[392,128]{1,0:T(8,128)(2,1)S(1)}, u32[]{:S(2)}, u32[]{:S(2)}) collective-permute-start(f16[392,128]{1,0:T(8,128)(2,1)S(1)} %pad_maximum_fusion.12), channel_id=1, source_target_pairs={{0,8},{4,12},{8,0},{12,4},{16,24},{20,28},{24,16},{28,20},{1,9},{5... | collective-permute-start | bytes 301064 | tf_op jit(solution)/shard_map/ppermute | solution.py:52
  78.4 1.5 %collective-permute-start.24 = (f16[392,128]{1,0:T(8,128)(2,1)S(1)}, f16[392,128]{1,0:T(8,128)(2,1)S(1)}, u32[]{:S(2)}, u32[]{:S(2)}) collective-permute-start(f16[392,128]{1,0:T(8,128)(2,1)S(1)} %pad_maximum_fusion.12), channel_id=1, source_target_pairs={{0,16},{4,20},{8,24},{12,28},{16,0},{20,4},{24,8},{28,12},{1,17},{... | collective-permute-start | bytes 301064 | tf_op jit(solution)/shard_map/ppermute | solution.py:52
  80.0 0.5 collective-permute-start.25
  81.3 0.4 collective-permute-done.23
  81.7 0.0 collective-permute-start.27
  81.7 2.4 %collective-permute-done.24 = f16[392,128]{1,0:T(8,128)(2,1)S(1)} collective-permute-done((f16[392,128]{1,0:T(8,128)(2,1)S(1)}, f16[392,128]{1,0:T(8,128)(2,1)S(1)}, u32[]{:S(2)}, u32[]{:S(2)}) %collective-permute-start.24) | collective-permute-done | bytes 100384 | tf_op jit(solution)/shard_map/ppermute | solution.py:52
  84.2 0.0 collective-permute-start.26
  84.2 1.3 %collective-permute-done.25 = f16[392,128]{1,0:T(8,128)(2,1)S(1)} collective-permute-done((f16[392,128]{1,0:T(8,128)(2,1)S(1)}, f16[392,128]{1,0:T(8,128)(2,1)S(1)}, u32[]{:S(2)}, u32[]{:S(2)}) %collective-permute-start.25) | collective-permute-done | bytes 100384 | tf_op jit(solution)/shard_map/ppermute | solution.py:52
  85.5 0.1 pad_maximum_fusion.1
  85.6 0.0 collective-permute-done.29
  87.3 1.5 %shard_map.39 = (bf16[512,1024]{1,0:T(8,128)(2,1)S(1)}, bf16[512,1024]{1,0:T(8,128)(2,1)S(1)}, f32[4,384,128]{2,1,0:T(8,128)S(1)}) custom-call(s32[3]{0:T(128)S(1)} %pad_add_fusion.refs_0_, f32[4,192,128]{2,1,0:T(8,128)S(1)} %pad_maximum_fusion.2.refs_1_, f32[4,192,128]{2,1,0:T(8,128)S(1)} %pad_maximum_fusion.3.refs_2_, ...), custom_call_target="tpu_custom_call" | custom-call | bytes 8388608 | tf_op jit(solution)/shard_map/pallas_call | solution.py:400
  88.7 0.1 collective-permute-start.30
  88.8 1.7 %collective-permute-done.30 = f16[4,392,128]{2,1,0:T(8,128)(2,1)S(1)} collective-permute-done((f16[4,392,128]{2,1,0:T(8,128)(2,1)S(1)}, f16[4,392,128]{2,1,0:T(8,128)(2,1)S(1)}, u32[]{:S(2)}, u32[]{:S(2)}) %collective-permute-start.30) | collective-permute-done | bytes 401440 | tf_op jit(solution)/shard_map/ppermute | solution.py:52
  90.5 0.1 maximum_convert_fusion
  90.7 0.1 slice_multiply_fusion
  90.8 0.1 pad_maximum_fusion.refs_2_
  90.9 29.9 %shard_map.40 = bf16[768,512]{1,0:T(8,128)(2,1)} custom-call(s32[3]{0:T(128)S(1)} %pad_add_fusion.refs_0_, s32[48]{0:T(128)S(1)} %copy-done.2, f32[8,392,128]{2,1,0:T(8,128)S(1)} %pad_maximum_fusion.refs_2_, f32[4,384,128]{2,1,0:T(8,128)S(1)} %get-tuple-element.37.refs_3_, bf16[512,1024]{1,0:T(8,128)(2,1)S(1)} %get-tuple-element.38.refs_4_, ...), custom_call_target="tpu_custom_call" | custom-call | flops 10000000000 | bytes 10485760 | tf_op jit(solution)/shard_map/pallas_call | solution.py:400
  (254 shorter events, 2.4 us)
Async XLA Ops:
  0.0 6.8 %copy-start = (bf16[3072,256]{1,0:T(8,128)(2,1)S(1)}, bf16[3072,256]{1,0:T(8,128)(2,1)}, u32[]{:S(2)}) copy-start(bf16[3072,256]{1,0:T(8,128)(2,1)} %refs_0_.1) | copy-start | bytes 4718596
  1.6 5.2 %collective-permute-start = (bf16[768,256]{1,0:T(8,128)(2,1)S(1)}, bf16[768,256]{1,0:T(8,128)(2,1)S(1)}, u32[]{:S(2)}, u32[]{:S(2)}) collective-permute-start(bf16[768,256]{1,0:T(8,128)(2,1)S(1)} %get-tuple-element.47.refs_4_), channel_id=1, source_target_pairs={{0,4},{4,0},{8,12},{12,8},{16,20},{20,16},{24,28},{28,24},{1,5},{5... | collective-permute-start | bytes 1179656 | tf_op jit(solution)/shard_map/ppermute | solution.py:52
  2.1 14.7 %collective-permute-start.7 = (bf16[768,256]{1,0:T(8,128)(2,1)S(1)}, bf16[768,256]{1,0:T(8,128)(2,1)S(1)}, u32[]{:S(2)}, u32[]{:S(2)}) collective-permute-start(bf16[768,256]{1,0:T(8,128)(2,1)S(1)} %get-tuple-element.45), channel_id=1, source_target_pairs={{0,3},{1,2},{2,1},{3,0},{4,7},{5,6},{6,5},{7,4},{8,11},{9,10},{10,... | collective-permute-start | bytes 1179656 | tf_op jit(solution)/shard_map/ppermute | solution.py:52
  6.8 36.6 %copy-start.1 = (f32[256,512]{1,0:T(8,128)S(1)}, f32[256,512]{1,0:T(8,128)}, u32[]{:S(2)}) copy-start(f32[256,512]{1,0:T(8,128)} %refs_2_.1) | copy-start | bytes 1572868
  6.8 36.6 %copy-start.2 = (s32[48]{0:T(128)S(1)}, s32[48]{0:T(128)}, u32[]{:S(2)}) copy-start(s32[48]{0:T(128)} %constant.57.clone.refs_1_) | copy-start | bytes 580
  6.8 19.3 %collective-permute-start.5 = (bf16[768,256]{1,0:T(8,128)(2,1)S(1)}, bf16[768,256]{1,0:T(8,128)(2,1)S(1)}, u32[]{:S(2)}, u32[]{:S(2)}) collective-permute-start(bf16[768,256]{1,0:T(8,128)(2,1)S(1)} %get-tuple-element.46), channel_id=1, source_target_pairs={{0,1},{1,0},{2,3},{3,2},{4,5},{5,4},{6,7},{7,6},{8,9},{9,8},{10,11... | collective-permute-start | bytes 1179656 | tf_op jit(solution)/shard_map/ppermute | solution.py:52
  7.6 1.5 %collective-permute-start.1 = (f32[384,128]{1,0:T(8,128)S(1)}, f32[384,128]{1,0:T(8,128)S(1)}, u32[]{:S(2)}, u32[]{:S(2)}) collective-permute-start(f32[384,128]{1,0:T(8,128)S(1)} %shard_map.37), channel_id=1, source_target_pairs={{0,4},{4,0},{8,12},{12,8},{16,20},{20,16},{24,28},{28,24},{1,5},{5... | collective-permute-start | bytes 589832 | tf_op jit(solution)/shard_map/ppermute | solution.py:52
  7.8 33.1 %collective-permute-start.6 = (bf16[768,256]{1,0:T(8,128)(2,1)S(1)}, bf16[768,256]{1,0:T(8,128)(2,1)S(1)}, u32[]{:S(2)}, u32[]{:S(2)}) collective-permute-start(bf16[768,256]{1,0:T(8,128)(2,1)S(1)} %get-tuple-element.48), channel_id=1, source_target_pairs={{0,2},{1,3},{2,0},{3,1},{4,6},{5,7},{6,4},{7,5},{8,10},{9,11},{10,... | collective-permute-start | bytes 1179656 | tf_op jit(solution)/shard_map/ppermute | solution.py:52
  9.1 31.8 %collective-permute-start.2 = (f32[384,128]{1,0:T(8,128)S(1)}, f32[384,128]{1,0:T(8,128)}, u32[]{:S(2)}, u32[]{:S(2)}) collective-permute-start(f32[384,128]{1,0:T(8,128)S(1)} %add.61), channel_id=1, source_target_pairs={{0,8},{4,12},{8,0},{12,4},{16,24},{20,28},{24,16},{28,20},{1,9},{5... | collective-permute-start | bytes 589832 | tf_op jit(solution)/shard_map/ppermute | solution.py:52
  10.7 30.8 %collective-permute-start.3 = (f32[384,128]{1,0:T(8,128)S(1)}, f32[384,128]{1,0:T(8,128)}, u32[]{:S(2)}, u32[]{:S(2)}) collective-permute-start(f32[384,128]{1,0:T(8,128)S(1)} %add.61), channel_id=1, source_target_pairs={{0,16},{4,20},{8,24},{12,28},{16,0},{20,4},{24,8},{28,12},{1,17},{... | collective-permute-start | bytes 589832 | tf_op jit(solution)/shard_map/ppermute | solution.py:52
  16.8 24.7 %collective-permute-start.4 = (f32[384,128]{1,0:T(8,128)S(1)}, f32[384,128]{1,0:T(8,128)}, u32[]{:S(2)}, u32[]{:S(2)}) collective-permute-start(f32[384,128]{1,0:T(8,128)S(1)} %add.61), channel_id=1, source_target_pairs={{0,24},{4,28},{8,16},{12,20},{16,8},{20,12},{24,0},{28,4},{1,25},{... | collective-permute-start | bytes 589832 | tf_op jit(solution)/shard_map/ppermute | solution.py:52
  26.0 16.7 %collective-permute-start.10 = (bf16[768,256]{1,0:T(8,128)(2,1)S(1)}, bf16[768,256]{1,0:T(8,128)(2,1)S(1)}, u32[]{:S(2)}, u32[]{:S(2)}) collective-permute-start(bf16[768,256]{1,0:T(8,128)(2,1)S(1)} %collective-permute-done.7.refs_7_), channel_id=1, source_target_pairs={{0,4},{4,0},{8,12},{12,8},{16,20},{20,16},{24,28},{28,24},{1,5},{5... | collective-permute-start | bytes 1179656 | tf_op jit(solution)/shard_map/ppermute | solution.py:52
  40.9 2.2 %collective-permute-start.8 = (bf16[768,256]{1,0:T(8,128)(2,1)S(1)}, bf16[768,256]{1,0:T(8,128)(2,1)S(1)}, u32[]{:S(2)}, u32[]{:S(2)}) collective-permute-start(bf16[768,256]{1,0:T(8,128)(2,1)S(1)} %collective-permute-done.5.refs_5_), channel_id=1, source_target_pairs={{0,4},{4,0},{8,12},{12,8},{16,20},{20,16},{24,28},{28,24},{1,5},{5... | collective-permute-start | bytes 1179656 | tf_op jit(solution)/shard_map/ppermute | solution.py:52
  40.9 2.4 %collective-permute-start.9 = (bf16[768,256]{1,0:T(8,128)(2,1)S(1)}, bf16[768,256]{1,0:T(8,128)(2,1)}, u32[]{:S(2)}, u32[]{:S(2)}) collective-permute-start(bf16[768,256]{1,0:T(8,128)(2,1)S(1)} %collective-permute-done.6.refs_6_), channel_id=1, source_target_pairs={{0,4},{4,0},{8,12},{12,8},{16,20},{20,16},{24,28},{28,24},{1,5},{5... | collective-permute-start | bytes 1179656 | tf_op jit(solution)/shard_map/ppermute | solution.py:52
  47.6 6.6 %collective-permute-start.17 = (f16[192,128]{1,0:T(8,128)(2,1)S(1)}, f16[192,128]{1,0:T(8,128)(2,1)S(1)}, u32[]{:S(2)}, u32[]{:S(2)}) collective-permute-start(f16[192,128]{1,0:T(8,128)(2,1)S(1)} %get-tuple-element.130), channel_id=1, source_target_pairs={{0,1},{1,0},{2,3},{3,2},{4,5},{5,4},{6,7},{7,6},{8,9},{9,8},{10,11... | collective-permute-start | bytes 147464 | tf_op jit(solution)/shard_map/ppermute | solution.py:52
  47.6 15.6 %collective-permute-start.11 = (f32[392,128]{1,0:T(8,128)S(1)}, f32[392,128]{1,0:T(8,128)S(1)}, u32[]{:S(2)}, u32[]{:S(2)}) collective-permute-start(f32[392,128]{1,0:T(8,128)S(1)} %get-tuple-element.24), channel_id=1, source_target_pairs={{0,8},{4,12},{8,0},{12,4},{16,24},{20,28},{24,16},{28,20},{1,9},{5... | collective-permute-start | bytes 602120 | tf_op jit(solution)/shard_map/ppermute | solution.py:52
  49.2 14.5 %collective-permute-start.12 = (f32[392,128]{1,0:T(8,128)S(1)}, f32[392,128]{1,0:T(8,128)S(1)}, u32[]{:S(2)}, u32[]{:S(2)}) collective-permute-start(f32[392,128]{1,0:T(8,128)S(1)} %get-tuple-element.25), channel_id=1, source_target_pairs={{0,16},{4,20},{8,24},{12,28},{16,0},{20,4},{24,8},{28,12},{1,17},{... | collective-permute-start | bytes 602120 | tf_op jit(solution)/shard_map/ppermute | solution.py:52
  50.7 13.0 %collective-permute-start.13 = (f32[392,128]{1,0:T(8,128)S(1)}, f32[392,128]{1,0:T(8,128)S(1)}, u32[]{:S(2)}, u32[]{:S(2)}) collective-permute-start(f32[392,128]{1,0:T(8,128)S(1)} %get-tuple-element.26), channel_id=1, source_target_pairs={{0,24},{4,28},{8,16},{12,20},{16,8},{20,12},{24,0},{28,4},{1,25},{... | collective-permute-start | bytes 602120 | tf_op jit(solution)/shard_map/ppermute | solution.py:52
  51.2 5.5 %collective-permute-start.18 = (f16[192,128]{1,0:T(8,128)(2,1)S(1)}, f16[192,128]{1,0:T(8,128)(2,1)S(1)}, u32[]{:S(2)}, u32[]{:S(2)}) collective-permute-start(f16[192,128]{1,0:T(8,128)(2,1)S(1)} %get-tuple-element.130), channel_id=1, source_target_pairs={{0,2},{1,3},{2,0},{3,1},{4,6},{5,7},{6,4},{7,5},{8,10},{9,11},{10,... | collective-permute-start | bytes 147464 | tf_op jit(solution)/shard_map/ppermute | solution.py:52
  54.2 5.9 %collective-permute-start.19 = (f16[192,128]{1,0:T(8,128)(2,1)S(1)}, f16[192,128]{1,0:T(8,128)(2,1)S(1)}, u32[]{:S(2)}, u32[]{:S(2)}) collective-permute-start(f16[192,128]{1,0:T(8,128)(2,1)S(1)} %get-tuple-element.130), channel_id=1, source_target_pairs={{0,3},{1,2},{2,1},{3,0},{4,7},{5,6},{6,5},{7,4},{8,11},{9,10},{10,... | collective-permute-start | bytes 147464 | tf_op jit(solution)/shard_map/ppermute | solution.py:52
  60.2 15.1 %collective-permute-start.20 = (f16[4,192,128]{2,1,0:T(8,128)(2,1)S(1)}, f16[4,192,128]{2,1,0:T(8,128)(2,1)S(1)}, u32[]{:S(2)}, u32[]{:S(2)}) collective-permute-start(f16[4,192,128]{2,1,0:T(8,128)(2,1)S(1)} %pad_maximum_fusion.10), channel_id=1, source_target_pairs={{0,8},{4,12},{8,0},{12,4},{16,24},{20,28},{24,16},{28,20},{1,9},{5... | collective-permute-start | bytes 589832 | tf_op jit(solution)/shard_map/ppermute | solution.py:52
  61.7 13.6 %collective-permute-start.21 = (f16[4,192,128]{2,1,0:T(8,128)(2,1)S(1)}, f16[4,192,128]{2,1,0:T(8,128)(2,1)S(1)}, u32[]{:S(2)}, u32[]{:S(2)}) collective-permute-start(f16[4,192,128]{2,1,0:T(8,128)(2,1)S(1)} %pad_maximum_fusion.10), channel_id=1, source_target_pairs={{0,16},{4,20},{8,24},{12,28},{16,0},{20,4},{24,8},{28,12},{1,17},{... | collective-permute-start | bytes 589832 | tf_op jit(solution)/shard_map/ppermute | solution.py:52
  63.3 12.0 %collective-permute-start.22 = (f16[4,192,128]{2,1,0:T(8,128)(2,1)S(1)}, f16[4,192,128]{2,1,0:T(8,128)(2,1)S(1)}, u32[]{:S(2)}, u32[]{:S(2)}) collective-permute-start(f16[4,192,128]{2,1,0:T(8,128)(2,1)S(1)} %pad_maximum_fusion.10), channel_id=1, source_target_pairs={{0,24},{4,28},{8,16},{12,20},{16,8},{20,12},{24,0},{28,4},{1,25},{... | collective-permute-start | bytes 589832 | tf_op jit(solution)/shard_map/ppermute | solution.py:52
  63.9 4.7 %collective-permute-start.14 = (f16[392,128]{1,0:T(8,128)(2,1)S(1)}, f16[392,128]{1,0:T(8,128)(2,1)S(1)}, u32[]{:S(2)}, u32[]{:S(2)}) collective-permute-start(f16[392,128]{1,0:T(8,128)(2,1)S(1)} %get-tuple-element.124), channel_id=1, source_target_pairs={{0,1},{1,0},{2,3},{3,2},{4,5},{5,4},{6,7},{7,6},{8,9},{9,8},{10,11... | collective-permute-start | bytes 301064 | tf_op jit(solution)/shard_map/ppermute | solution.py:52
  64.0 7.8 %collective-permute-start.15 = (f16[392,128]{1,0:T(8,128)(2,1)S(1)}, f16[392,128]{1,0:T(8,128)(2,1)S(1)}, u32[]{:S(2)}, u32[]{:S(2)}) collective-permute-start(f16[392,128]{1,0:T(8,128)(2,1)S(1)} %get-tuple-element.124), channel_id=1, source_target_pairs={{0,2},{1,3},{2,0},{3,1},{4,6},{5,7},{6,4},{7,5},{8,10},{9,11},{10,... | collective-permute-start | bytes 301064 | tf_op jit(solution)/shard_map/ppermute | solution.py:52
  68.6 6.4 %collective-permute-start.16 = (f16[392,128]{1,0:T(8,128)(2,1)S(1)}, f16[392,128]{1,0:T(8,128)(2,1)S(1)}, u32[]{:S(2)}, u32[]{:S(2)}) collective-permute-start(f16[392,128]{1,0:T(8,128)(2,1)S(1)} %get-tuple-element.124), channel_id=1, source_target_pairs={{0,3},{1,2},{2,1},{3,0},{4,7},{5,6},{6,5},{7,4},{8,11},{9,10},{10,... | collective-permute-start | bytes 301064 | tf_op jit(solution)/shard_map/ppermute | solution.py:52
  75.3 10.3 %collective-permute-start.29 = (f16[4,192,128]{2,1,0:T(8,128)(2,1)S(1)}, f16[4,192,128]{2,1,0:T(8,128)(2,1)S(1)}, u32[]{:S(2)}, u32[]{:S(2)}) collective-permute-start(f16[4,192,128]{2,1,0:T(8,128)(2,1)S(1)} %collective-permute-done.22), channel_id=1, source_target_pairs={{0,4},{4,0},{8,12},{12,8},{16,20},{20,16},{24,28},{28,24},{1,5},{5... | collective-permute-start | bytes 589832 | tf_op jit(solution)/shard_map/ppermute | solution.py:52
  75.4 10.5 %collective-permute-start.28 = (f16[4,192,128]{2,1,0:T(8,128)(2,1)S(1)}, f16[4,192,128]{2,1,0:T(8,128)(2,1)S(1)}, u32[]{:S(2)}, u32[]{:S(2)}) collective-permute-start(f16[4,192,128]{2,1,0:T(8,128)(2,1)S(1)} %collective-permute-done.21), channel_id=1, source_target_pairs={{0,4},{4,0},{8,12},{12,8},{16,20},{20,16},{24,28},{28,24},{1,5},{5... | collective-permute-start | bytes 589832 | tf_op jit(solution)/shard_map/ppermute | solution.py:52
  76.9 4.9 %collective-permute-start.23 = (f16[392,128]{1,0:T(8,128)(2,1)S(1)}, f16[392,128]{1,0:T(8,128)(2,1)S(1)}, u32[]{:S(2)}, u32[]{:S(2)}) collective-permute-start(f16[392,128]{1,0:T(8,128)(2,1)S(1)} %pad_maximum_fusion.12), channel_id=1, source_target_pairs={{0,8},{4,12},{8,0},{12,4},{16,24},{20,28},{24,16},{28,20},{1,9},{5... | collective-permute-start | bytes 301064 | tf_op jit(solution)/shard_map/ppermute | solution.py:52
  78.4 5.8 %collective-permute-start.24 = (f16[392,128]{1,0:T(8,128)(2,1)S(1)}, f16[392,128]{1,0:T(8,128)(2,1)S(1)}, u32[]{:S(2)}, u32[]{:S(2)}) collective-permute-start(f16[392,128]{1,0:T(8,128)(2,1)S(1)} %pad_maximum_fusion.12), channel_id=1, source_target_pairs={{0,16},{4,20},{8,24},{12,28},{16,0},{20,4},{24,8},{28,12},{1,17},{... | collective-permute-start | bytes 301064 | tf_op jit(solution)/shard_map/ppermute | solution.py:52
  80.0 5.5 %collective-permute-start.25 = (f16[392,128]{1,0:T(8,128)(2,1)S(1)}, f16[392,128]{1,0:T(8,128)(2,1)S(1)}, u32[]{:S(2)}, u32[]{:S(2)}) collective-permute-start(f16[392,128]{1,0:T(8,128)(2,1)S(1)} %pad_maximum_fusion.12), channel_id=1, source_target_pairs={{0,24},{4,28},{8,16},{12,20},{16,8},{20,12},{24,0},{28,4},{1,25},{... | collective-permute-start | bytes 301064 | tf_op jit(solution)/shard_map/ppermute | solution.py:52
  81.7 4.4 %collective-permute-start.27 = (f16[4,192,128]{2,1,0:T(8,128)(2,1)S(1)}, f16[4,192,128]{2,1,0:T(8,128)(2,1)S(1)}, u32[]{:S(2)}, u32[]{:S(2)}) collective-permute-start(f16[4,192,128]{2,1,0:T(8,128)(2,1)S(1)} %collective-permute-done.20), channel_id=1, source_target_pairs={{0,4},{4,0},{8,12},{12,8},{16,20},{20,16},{24,28},{28,24},{1,5},{5... | collective-permute-start | bytes 589832 | tf_op jit(solution)/shard_map/ppermute | solution.py:52
  84.2 2.1 %collective-permute-start.26 = (f16[4,192,128]{2,1,0:T(8,128)(2,1)S(1)}, f16[4,192,128]{2,1,0:T(8,128)(2,1)S(1)}, u32[]{:S(2)}, u32[]{:S(2)}) collective-permute-start(f16[4,192,128]{2,1,0:T(8,128)(2,1)S(1)} %pad_maximum_fusion.10), channel_id=1, source_target_pairs={{0,4},{4,0},{8,12},{12,8},{16,20},{20,16},{24,28},{28,24},{1,5},{5... | collective-permute-start | bytes 589832 | tf_op jit(solution)/shard_map/ppermute | solution.py:52
  88.7 1.8 %collective-permute-start.30 = (f16[4,392,128]{2,1,0:T(8,128)(2,1)S(1)}, f16[4,392,128]{2,1,0:T(8,128)(2,1)S(1)}, u32[]{:S(2)}, u32[]{:S(2)}) collective-permute-start(f16[4,392,128]{2,1,0:T(8,128)(2,1)S(1)} %pad_maximum_fusion.1), channel_id=1, source_target_pairs={{0,4},{4,0},{8,12},{12,8},{16,20},{20,16},{24,28},{28,24},{1,5},{5... | collective-permute-start | bytes 1204232 | tf_op jit(solution)/shard_map/ppermute | solution.py:52

commit v5 on v4

--- a/solution.py
+++ b/solution.py
@@ -12,6 +12,7 @@
 LANES = 128
 SUB = 8
 PANEL = 32
+STEP = 16
 REPEAT = 4
 SHIFT = 2.0**-15
 WIDE = 512
@@ -149,16 +150,17 @@
             for g in range(groups)
         ]
         col = {}
+        scale = [None] * groups
         for j in range(PANEL):
-            for g in range(j // SUB, groups):
-                col[j, g] = jnp.broadcast_to(m[g][0][:, r0 + j : r0 + j + 1], (SUB, LANES))
-        scale = [None] * groups
-        pivot = spread(col[0, 0], 0)
-        for j in range(PANEL):
+            if j % STEP == 0:
+                for k in range(j, j + STEP):
+                    for g in range(k // SUB, groups):
+                        col[k, g] = jnp.broadcast_to(m[g][0][:, r0 + k : r0 + k + 1], (SUB, LANES))
+                pivot = spread(col[j, j // SUB], j % SUB)
             gj, sj = divmod(j, SUB)
             inverse = 1.0 / pivot
             root = lax.rsqrt(pivot)
-            if j + 1 < PANEL:
+            if (j + 1) % STEP:
                 g, k = divmod(j + 1, SUB)
                 entry = spread(col[j, g], k)
                 pivot = spread(col[j + 1, g], k) - entry * entry * inverse
@@ -167,7 +169,7 @@
             scale[gj] = root if scale[gj] is None else jnp.where(sub == sj, root, scale[gj])
             source = [spread(m[gj][t], sj) for t in range(2)]
             scaled = {g: col[j, g] * inverse for g in range(gj, groups)}
-            for k in range(j + 1, PANEL):
+            for k in range(j + 1, j - j % STEP + STEP):
                 entry = spread(col[j, k // SUB], k % SUB)
                 for g in range(k // SUB, groups):
                     col[k, g] = col[k, g] - scaled[g] * entry
@@ -431,7 +433,10 @@
         at, table, start, diagonal, *pieces, *other_pieces, n_smem=2,
         flops=4 * sub_rows * chips * share * LANES * LANES, moved=6 << 20,
     )
-    plane = sum((swap(block, "rows", offset) for block, offset in zip(blocks[1:], other_chips)), blocks[0])
+    blocks = [encode(block) for block in blocks]
+    blocks = blocks[:1] + [swap(block, "rows", offset) for block, offset in zip(blocks[1:], other_chips)]
+    blocks[1], mine = lax.optimization_barrier((blocks[1], mine))
+    plane = sum(decode(block) for block in blocks)
     planes = encode(plane)
     planes = [planes] + [swap(planes, "batch", offset) for offset in other_batches]
     total = encode(sum(decode(value) for value in planes))
@@ -452,7 +457,6 @@
     )
 
     cross = spread_copy(total, "rows", other_chips)
-    cross, high, low, diagonal = lax.optimization_barrier((cross, high, low, diagonal))
     cross = jnp.concatenate([cross, swap(cross, "rows", 1)])
     cross = jax.vmap(decode)(cross)
     (modes,) = call(

time: 121 us -> 115 us (0.950)
  waiting for transfers between devices: 45.7 us -> 37 us
  starting transfers between devices: 31.1 us -> 34.4 us
  Pallas kernels: 36.3 us -> 34.8 us
    ppermute x31, waiting for transfers between devices: 45.7 us -> 37 us  [swap(): return lax.ppermute(value, axis, [(i, i ^ offset) for i in range(size)])]
    ppermute x31, starting transfers between devices: 31.1 us -> 34.4 us  [swap(): return lax.ppermute(value, axis, [(i, i ^ offset) for i in range(size)])]
    pallas_call x4, Pallas kernels: 36.3 us -> 34.8 us  [call(): pl.pallas_call(body, out_shape=[jax.ShapeDtypeStruct(shape, dtype) for sh...]
  transfers between devices with their start and end apart: 31 -> 31, of which waited for: 15 -> 13; matrix products, arithmetic and copies ran while one was open for 3% -> 4% of each run, Pallas kernels for 1% -> 2%
where the time goes in v5:
time: 115 us
  waiting for transfers between devices  37 us (32%)
  Pallas kernels  34.8 us (30%)
  starting transfers between devices  34.4 us (30%)
  other arithmetic  4.78 us (4%)
  between operations  2.24 us (2%)
  local copies, waits for them, and re-layouts  1.84 us (2%)
    ppermute x31, waiting for transfers between devices, swap(): return lax.ppermute(value, axis, [(i, i ^ offset) for i in range(size)])  37 us
    pallas_call x4, Pallas kernels, call(): pl.pallas_call(body, out_shape=[jax.ShapeDtypeStruct(shape, dtype) for sh...  34.8 us
    ppermute x31, starting transfers between devices, swap(): return lax.ppermute(value, axis, [(i, i ^ offset) for i in range(size)])  34.4 us
  transfers between devices with their start and end apart: 31, of which 13 were waited for; matrix products, arithmetic and copies ran while one was open for 4% of the time, Pallas kernels for 2%

profile of v5, /device:TPU:0, one launch (start us, length us, event | category | flops | bytes accessed | tf_op | source)
XLA Modules:
  0.0 115.1 jit_solution(8128987490606560227)
XLA Ops:
  0.0 1.6 %constant_dynamic-slice_fusion = (bf16[768,256]{1,0:T(8,128)(2,1)S(1)}, bf16[768,256]{1,0:T(8,128)(2,1)S(1)}, bf16[768,256]{1,0:T(8,128)(2,1)S(1)}, bf16[768,256]{1,0:T(8,128)(2,1)S(1)}) fusion(bf16[3072,256]{1,0:T(8,128)(2,1)} %refs_0_.1, s32[]{:T(128)S(6)} %select_n.28, s32[]{:T(128)S(6)} %select_n.26, s32[]{:T(128)S(6)} %select_n.25, s32[]{:T(128)S(6)} %select_n.27), kind=kLoop, calls=%fused_computation.592 | loop fusion | bytes 3145744 | tf_op jit(solution)/shard_map/dynamic_slice | solution.py:414
  1.6 0.5 collective-permute-start
  2.1 4.7 %collective-permute-start.7 = (bf16[768,256]{1,0:T(8,128)(2,1)S(1)}, bf16[768,256]{1,0:T(8,128)(2,1)S(1)}, u32[]{:S(2)}, u32[]{:S(2)}) collective-permute-start(bf16[768,256]{1,0:T(8,128)(2,1)S(1)} %get-tuple-element.45), channel_id=1, source_target_pairs={{0,3},{1,2},{2,1},{3,0},{4,7},{5,6},{6,5},{7,4},{8,11},{9,10},{10,... | collective-permute-start | bytes 1179656 | tf_op jit(solution)/shard_map/ppermute | solution.py:53
  6.8 0.6 collective-permute-start.6
  7.4 0.0 collective-permute-done.refs_1_.refs_8_
  7.4 0.8 shard_map.37
  8.2 0.1 collective-permute-start.1
  8.3 1.4 %collective-permute-done.1 = f32[384,128]{1,0:T(8,128)S(1)} collective-permute-done((f32[384,128]{1,0:T(8,128)S(1)}, f32[384,128]{1,0:T(8,128)S(1)}, u32[]{:S(2)}, u32[]{:S(2)}) %collective-permute-start.1) | collective-permute-done | bytes 196640 | tf_op jit(solution)/shard_map/ppermute | solution.py:53
  9.8 1.7 %collective-permute-start.2 = (f32[384,128]{1,0:T(8,128)S(1)}, f32[384,128]{1,0:T(8,128)}, u32[]{:S(2)}, u32[]{:S(2)}) collective-permute-start(f32[384,128]{1,0:T(8,128)S(1)} %add.73), channel_id=1, source_target_pairs={{0,8},{4,12},{8,0},{12,4},{16,24},{20,28},{24,16},{28,20},{1,9},{5... | collective-permute-start | bytes 589832 | tf_op jit(solution)/shard_map/ppermute | solution.py:53
  11.5 1.5 %collective-permute-start.3 = (f32[384,128]{1,0:T(8,128)S(1)}, f32[384,128]{1,0:T(8,128)}, u32[]{:S(2)}, u32[]{:S(2)}) collective-permute-start(f32[384,128]{1,0:T(8,128)S(1)} %add.73), channel_id=1, source_target_pairs={{0,16},{4,20},{8,24},{12,28},{16,0},{20,4},{24,8},{28,12},{1,17},{... | collective-permute-start | bytes 589832 | tf_op jit(solution)/shard_map/ppermute | solution.py:53
  13.0 3.8 %collective-permute-done.7.refs_7_ = bf16[768,256]{1,0:T(8,128)(2,1)S(1)} collective-permute-done((bf16[768,256]{1,0:T(8,128)(2,1)S(1)}, bf16[768,256]{1,0:T(8,128)(2,1)S(1)}, u32[]{:S(2)}, u32[]{:S(2)}) %collective-permute-start.7) | collective-permute-done | bytes 393248 | tf_op jit(solution)/shard_map/ppermute | solution.py:53
  16.8 2.6 %collective-permute-start.4 = (f32[384,128]{1,0:T(8,128)S(1)}, f32[384,128]{1,0:T(8,128)}, u32[]{:S(2)}, u32[]{:S(2)}) collective-permute-start(f32[384,128]{1,0:T(8,128)S(1)} %add.73), channel_id=1, source_target_pairs={{0,24},{4,28},{8,16},{12,20},{16,8},{20,12},{24,0},{28,4},{1,25},{... | collective-permute-start | bytes 589832 | tf_op jit(solution)/shard_map/ppermute | solution.py:53
  19.4 6.6 %collective-permute-done.5.refs_5_ = bf16[768,256]{1,0:T(8,128)(2,1)S(1)} collective-permute-done((bf16[768,256]{1,0:T(8,128)(2,1)S(1)}, bf16[768,256]{1,0:T(8,128)(2,1)S(1)}, u32[]{:S(2)}, u32[]{:S(2)}) %collective-permute-start.5) | collective-permute-done | bytes 393248 | tf_op jit(solution)/shard_map/ppermute | solution.py:53
  26.0 0.0 collective-permute-start.10
  26.1 14.9 %collective-permute-done.6.refs_6_ = bf16[768,256]{1,0:T(8,128)(2,1)S(1)} collective-permute-done((bf16[768,256]{1,0:T(8,128)(2,1)S(1)}, bf16[768,256]{1,0:T(8,128)(2,1)S(1)}, u32[]{:S(2)}, u32[]{:S(2)}) %collective-permute-start.6) | collective-permute-done | bytes 393248 | tf_op jit(solution)/shard_map/ppermute | solution.py:53
  40.9 0.0 collective-permute-start.8
  40.9 0.0 collective-permute-done.2
  40.9 0.5 collective-permute-start.9
  41.4 0.1 pad_add_fusion.refs_0_
  41.5 1.2 %add_add_fusion.refs_3_ = f32[384,128]{1,0:T(8,128)S(1)} fusion(f32[384,128]{1,0:T(8,128)} %collective-permute-done.4, f32[384,128]{1,0:T(8,128)} %collective-permute-done.3, f32[384,128]{1,0:T(8,128)S(1)} %add.73, f32[384,128]{1,0:T(8,128)} %collective-permute-done.2), kind=kLoop, calls=%fused_computation.38 | loop fusion | flops 147456 | bytes 983040 | tf_op jit(solution)/shard_map/add | solution.py:424
  42.7 0.0 collective-permute-done.10.refs_11_
  42.7 0.4 collective-permute-done.8.refs_9_
  43.1 0.2 collective-permute-done.9.refs_10_
  43.4 4.1 %shard_map.38 = (bf16[768,1024]{1,0:T(8,128)(2,1)S(1)}, f32[192,128]{1,0:T(8,128)S(1)}, f32[392,128]{1,0:T(8,128)S(1)}, f32[392,128]{1,0:T(8,128)S(1)}, f32[392,128]{1,0:T(8,128)S(1)}, /*index=5*/f32[392,128]{1,0:T(8,128)S(1)}) custom-call(s32[3]{0:T(128)S(1)} %pad_add_fusion.refs_0_, s32[48]{0:T(128)S(1)} %copy-done.2, f32[256,512]{1,0:T(8,128)S(1)} %copy-done.1, ...), custom_call_target="tpu_custom_call" | custom-call | flops 603979776 | bytes 6291456 | tf_op jit(solution)/shard_map/pallas_call | solution.py:402
  47.6 1.6 %collective-permute-start.11 = (f16[392,128]{1,0:T(8,128)(2,1)S(1)}, f16[392,128]{1,0:T(8,128)(2,1)S(1)}, u32[]{:S(2)}, u32[]{:S(2)}) collective-permute-start(f16[392,128]{1,0:T(8,128)(2,1)S(1)} %pad_maximum_fusion.11), channel_id=1, source_target_pairs={{0,8},{4,12},{8,0},{12,4},{16,24},{20,28},{24,16},{28,20},{1,9},{5... | collective-permute-start | bytes 301064 | tf_op jit(solution)/shard_map/ppermute | solution.py:53
  49.3 1.6 %collective-permute-start.12 = (f16[392,128]{1,0:T(8,128)(2,1)S(1)}, f16[392,128]{1,0:T(8,128)(2,1)S(1)}, u32[]{:S(2)}, u32[]{:S(2)}) collective-permute-start(f16[392,128]{1,0:T(8,128)(2,1)S(1)} %pad_maximum_fusion.12), channel_id=1, source_target_pairs={{0,16},{4,20},{8,24},{12,28},{16,0},{20,4},{24,8},{28,12},{1,17},{... | collective-permute-start | bytes 301064 | tf_op jit(solution)/shard_map/ppermute | solution.py:53
  51.0 0.5 collective-permute-start.13
  51.5 1.0 collective-permute-done.11
  52.6 0.1 collective-permute-start.17
  52.7 3.1 %collective-permute-start.18 = (f16[192,128]{1,0:T(8,128)(2,1)S(1)}, f16[192,128]{1,0:T(8,128)(2,1)S(1)}, u32[]{:S(2)}, u32[]{:S(2)}) collective-permute-start(f16[192,128]{1,0:T(8,128)(2,1)S(1)} %get-tuple-element.142), channel_id=1, source_target_pairs={{0,2},{1,3},{2,0},{3,1},{4,6},{5,7},{6,4},{7,5},{8,10},{9,11},{10,... | collective-permute-start | bytes 147464 | tf_op jit(solution)/shard_map/ppermute | solution.py:53
  55.7 1.3 %collective-permute-start.19 = (f16[192,128]{1,0:T(8,128)(2,1)S(1)}, f16[192,128]{1,0:T(8,128)(2,1)S(1)}, u32[]{:S(2)}, u32[]{:S(2)}) collective-permute-start(f16[192,128]{1,0:T(8,128)(2,1)S(1)} %get-tuple-element.142), channel_id=1, source_target_pairs={{0,3},{1,2},{2,1},{3,0},{4,7},{5,6},{6,5},{7,4},{8,11},{9,10},{10,... | collective-permute-start | bytes 147464 | tf_op jit(solution)/shard_map/ppermute | solution.py:53
  57.1 0.0 collective-permute-done.12
  57.2 0.0 collective-permute-done.13
  57.4 0.1 collective-permute-start.14
  57.5 3.1 %collective-permute-start.15 = (f16[392,128]{1,0:T(8,128)(2,1)S(1)}, f16[392,128]{1,0:T(8,128)(2,1)S(1)}, u32[]{:S(2)}, u32[]{:S(2)}) collective-permute-start(f16[392,128]{1,0:T(8,128)(2,1)S(1)} %get-tuple-element.136), channel_id=1, source_target_pairs={{0,2},{1,3},{2,0},{3,1},{4,6},{5,7},{6,4},{7,5},{8,10},{9,11},{10,... | collective-permute-start | bytes 301064 | tf_op jit(solution)/shard_map/ppermute | solution.py:53
  60.6 1.4 %collective-permute-start.16 = (f16[392,128]{1,0:T(8,128)(2,1)S(1)}, f16[392,128]{1,0:T(8,128)(2,1)S(1)}, u32[]{:S(2)}, u32[]{:S(2)}) collective-permute-start(f16[392,128]{1,0:T(8,128)(2,1)S(1)} %get-tuple-element.136), channel_id=1, source_target_pairs={{0,3},{1,2},{2,1},{3,0},{4,7},{5,6},{6,5},{7,4},{8,11},{9,10},{10,... | collective-permute-start | bytes 301064 | tf_op jit(solution)/shard_map/ppermute | solution.py:53
  62.0 0.0 collective-permute-done.18
  62.0 0.3 collective-permute-done.19
  62.3 0.1 pad_maximum_fusion.10
  62.4 1.9 %collective-permute-start.20 = (f16[4,192,128]{2,1,0:T(8,128)(2,1)S(1)}, f16[4,192,128]{2,1,0:T(8,128)(2,1)S(1)}, u32[]{:S(2)}, u32[]{:S(2)}) collective-permute-start(f16[4,192,128]{2,1,0:T(8,128)(2,1)S(1)} %pad_maximum_fusion.10), channel_id=1, source_target_pairs={{0,8},{4,12},{8,0},{12,4},{16,24},{20,28},{24,16},{28,20},{1,9},{5... | collective-permute-start | bytes 589832 | tf_op jit(solution)/shard_map/ppermute | solution.py:53
  64.3 1.5 %collective-permute-start.21 = (f16[4,192,128]{2,1,0:T(8,128)(2,1)S(1)}, f16[4,192,128]{2,1,0:T(8,128)(2,1)S(1)}, u32[]{:S(2)}, u32[]{:S(2)}) collective-permute-start(f16[4,192,128]{2,1,0:T(8,128)(2,1)S(1)} %pad_maximum_fusion.10), channel_id=1, source_target_pairs={{0,16},{4,20},{8,24},{12,28},{16,0},{20,4},{24,8},{28,12},{1,17},{... | collective-permute-start | bytes 589832 | tf_op jit(solution)/shard_map/ppermute | solution.py:53
  65.8 1.3 %collective-permute-start.22 = (f16[4,192,128]{2,1,0:T(8,128)(2,1)S(1)}, f16[4,192,128]{2,1,0:T(8,128)(2,1)S(1)}, u32[]{:S(2)}, u32[]{:S(2)}) collective-permute-start(f16[4,192,128]{2,1,0:T(8,128)(2,1)S(1)} %pad_maximum_fusion.10), channel_id=1, source_target_pairs={{0,24},{4,28},{8,16},{12,20},{16,8},{20,12},{24,0},{28,4},{1,25},{... | collective-permute-start | bytes 589832 | tf_op jit(solution)/shard_map/ppermute | solution.py:53
  67.2 0.7 collective-permute-done.15
  68.2 1.0 collective-permute-done.20
  69.2 3.5 %collective-permute-done.21 = f16[4,192,128]{2,1,0:T(8,128)(2,1)S(1)} collective-permute-done((f16[4,192,128]{2,1,0:T(8,128)(2,1)S(1)}, f16[4,192,128]{2,1,0:T(8,128)(2,1)S(1)}, u32[]{:S(2)}, u32[]{:S(2)}) %collective-permute-start.21) | collective-permute-done | bytes 196640 | tf_op jit(solution)/shard_map/ppermute | solution.py:53
  72.6 0.0 collective-permute-start.30
  72.9 0.6 collective-permute-start.29
  74.2 0.8 collective-permute-start.23
  75.1 0.9 collective-permute-start.24
  76.0 1.8 %collective-permute-start.25 = (f16[392,128]{1,0:T(8,128)(2,1)S(1)}, f16[392,128]{1,0:T(8,128)(2,1)S(1)}, u32[]{:S(2)}, u32[]{:S(2)}) collective-permute-start(f16[392,128]{1,0:T(8,128)(2,1)S(1)} %pad_maximum_fusion.15), channel_id=1, source_target_pairs={{0,24},{4,28},{8,16},{12,20},{16,8},{20,12},{24,0},{28,4},{1,25},{... | collective-permute-start | bytes 301064 | tf_op jit(solution)/shard_map/ppermute | solution.py:53
  78.7 0.9 collective-permute-done.23
  79.6 0.0 collective-permute-start.28
  79.6 2.3 %collective-permute-done.24 = f16[392,128]{1,0:T(8,128)(2,1)S(1)} collective-permute-done((f16[392,128]{1,0:T(8,128)(2,1)S(1)}, f16[392,128]{1,0:T(8,128)(2,1)S(1)}, u32[]{:S(2)}, u32[]{:S(2)}) %collective-permute-start.24) | collective-permute-done | bytes 100384 | tf_op jit(solution)/shard_map/ppermute | solution.py:53
  81.9 0.0 collective-permute-start.27
  81.9 0.0 collective-permute-done.25
  81.9 0.1 pad_maximum_fusion.1
  82.0 0.6 collective-permute-start.26
  83.0 0.0 collective-permute-done.29
  84.7 1.5 %shard_map.39 = (bf16[512,1024]{1,0:T(8,128)(2,1)S(1)}, bf16[512,1024]{1,0:T(8,128)(2,1)S(1)}, f32[4,384,128]{2,1,0:T(8,128)S(1)}) custom-call(s32[3]{0:T(128)S(1)} %pad_add_fusion.refs_0_, f32[4,192,128]{2,1,0:T(8,128)S(1)} %pad_maximum_fusion.2.refs_1_, f32[4,192,128]{2,1,0:T(8,128)S(1)} %pad_maximum_fusion.3.refs_2_, ...), custom_call_target="tpu_custom_call" | custom-call | bytes 8388608 | tf_op jit(solution)/shard_map/pallas_call | solution.py:402
  86.2 0.1 constant_dynamic-update-slice_fusion
  86.3 0.1 convert_element_type.299
  86.4 0.1 slice_multiply_fusion
  86.5 0.1 pad_maximum_fusion.refs_2_
  86.7 28.4 %shard_map.40 = bf16[768,512]{1,0:T(8,128)(2,1)} custom-call(s32[3]{0:T(128)S(1)} %pad_add_fusion.refs_0_, s32[48]{0:T(128)S(1)} %copy-done.2, f32[8,392,128]{2,1,0:T(8,128)S(1)} %pad_maximum_fusion.refs_2_, f32[4,384,128]{2,1,0:T(8,128)S(1)} %get-tuple-element.33.refs_3_, bf16[512,1024]{1,0:T(8,128)(2,1)S(1)} %get-tuple-element.34.refs_4_, ...), custom_call_target="tpu_custom_call" | custom-call | flops 10000000000 | bytes 10485760 | tf_op jit(solution)/shard_map/pallas_call | solution.py:402
  (318 shorter events, 3.2 us)
Async XLA Ops:
  0.0 7.4 %copy-start = (bf16[3072,256]{1,0:T(8,128)(2,1)S(1)}, bf16[3072,256]{1,0:T(8,128)(2,1)}, u32[]{:S(2)}) copy-start(bf16[3072,256]{1,0:T(8,128)(2,1)} %refs_0_.1) | copy-start | bytes 4718596
  1.6 5.8 %collective-permute-start = (bf16[768,256]{1,0:T(8,128)(2,1)S(1)}, bf16[768,256]{1,0:T(8,128)(2,1)S(1)}, u32[]{:S(2)}, u32[]{:S(2)}) collective-permute-start(bf16[768,256]{1,0:T(8,128)(2,1)S(1)} %get-tuple-element.47.refs_4_), channel_id=1, source_target_pairs={{0,4},{4,0},{8,12},{12,8},{16,20},{20,16},{24,28},{28,24},{1,5},{5... | collective-permute-start | bytes 1179656 | tf_op jit(solution)/shard_map/ppermute | solution.py:53
  2.1 14.7 %collective-permute-start.7 = (bf16[768,256]{1,0:T(8,128)(2,1)S(1)}, bf16[768,256]{1,0:T(8,128)(2,1)S(1)}, u32[]{:S(2)}, u32[]{:S(2)}) collective-permute-start(bf16[768,256]{1,0:T(8,128)(2,1)S(1)} %get-tuple-element.45), channel_id=1, source_target_pairs={{0,3},{1,2},{2,1},{3,0},{4,7},{5,6},{6,5},{7,4},{8,11},{9,10},{10,... | collective-permute-start | bytes 1179656 | tf_op jit(solution)/shard_map/ppermute | solution.py:53
  6.8 19.3 %collective-permute-start.5 = (bf16[768,256]{1,0:T(8,128)(2,1)S(1)}, bf16[768,256]{1,0:T(8,128)(2,1)S(1)}, u32[]{:S(2)}, u32[]{:S(2)}) collective-permute-start(bf16[768,256]{1,0:T(8,128)(2,1)S(1)} %get-tuple-element.46), channel_id=1, source_target_pairs={{0,1},{1,0},{2,3},{3,2},{4,5},{5,4},{6,7},{7,6},{8,9},{9,8},{10,11... | collective-permute-start | bytes 1179656 | tf_op jit(solution)/shard_map/ppermute | solution.py:53
  6.8 36.6 %copy-start.1 = (f32[256,512]{1,0:T(8,128)S(1)}, f32[256,512]{1,0:T(8,128)}, u32[]{:S(2)}) copy-start(f32[256,512]{1,0:T(8,128)} %refs_2_.1) | copy-start | bytes 1572868
  6.8 36.6 %copy-start.2 = (s32[48]{0:T(128)S(1)}, s32[48]{0:T(128)}, u32[]{:S(2)}) copy-start(s32[48]{0:T(128)} %constant.57.clone.refs_1_) | copy-start | bytes 580
  6.8 34.1 %collective-permute-start.6 = (bf16[768,256]{1,0:T(8,128)(2,1)S(1)}, bf16[768,256]{1,0:T(8,128)(2,1)S(1)}, u32[]{:S(2)}, u32[]{:S(2)}) collective-permute-start(bf16[768,256]{1,0:T(8,128)(2,1)S(1)} %get-tuple-element.48), channel_id=1, source_target_pairs={{0,2},{1,3},{2,0},{3,1},{4,6},{5,7},{6,4},{7,5},{8,10},{9,11},{10,... | collective-permute-start | bytes 1179656 | tf_op jit(solution)/shard_map/ppermute | solution.py:53
  8.2 1.5 %collective-permute-start.1 = (f32[384,128]{1,0:T(8,128)S(1)}, f32[384,128]{1,0:T(8,128)S(1)}, u32[]{:S(2)}, u32[]{:S(2)}) collective-permute-start(f32[384,128]{1,0:T(8,128)S(1)} %shard_map.37), channel_id=1, source_target_pairs={{0,4},{4,0},{8,12},{12,8},{16,20},{20,16},{24,28},{28,24},{1,5},{5... | collective-permute-start | bytes 589832 | tf_op jit(solution)/shard_map/ppermute | solution.py:53
  9.8 31.2 %collective-permute-start.2 = (f32[384,128]{1,0:T(8,128)S(1)}, f32[384,128]{1,0:T(8,128)}, u32[]{:S(2)}, u32[]{:S(2)}) collective-permute-start(f32[384,128]{1,0:T(8,128)S(1)} %add.73), channel_id=1, source_target_pairs={{0,8},{4,12},{8,0},{12,4},{16,24},{20,28},{24,16},{28,20},{1,9},{5... | collective-permute-start | bytes 589832 | tf_op jit(solution)/shard_map/ppermute | solution.py:53
  11.5 30.0 %collective-permute-start.3 = (f32[384,128]{1,0:T(8,128)S(1)}, f32[384,128]{1,0:T(8,128)}, u32[]{:S(2)}, u32[]{:S(2)}) collective-permute-start(f32[384,128]{1,0:T(8,128)S(1)} %add.73), channel_id=1, source_target_pairs={{0,16},{4,20},{8,24},{12,28},{16,0},{20,4},{24,8},{28,12},{1,17},{... | collective-permute-start | bytes 589832 | tf_op jit(solution)/shard_map/ppermute | solution.py:53
  16.8 24.7 %collective-permute-start.4 = (f32[384,128]{1,0:T(8,128)S(1)}, f32[384,128]{1,0:T(8,128)}, u32[]{:S(2)}, u32[]{:S(2)}) collective-permute-start(f32[384,128]{1,0:T(8,128)S(1)} %add.73), channel_id=1, source_target_pairs={{0,24},{4,28},{8,16},{12,20},{16,8},{20,12},{24,0},{28,4},{1,25},{... | collective-permute-start | bytes 589832 | tf_op jit(solution)/shard_map/ppermute | solution.py:53
  26.0 16.7 %collective-permute-start.10 = (bf16[768,256]{1,0:T(8,128)(2,1)S(1)}, bf16[768,256]{1,0:T(8,128)(2,1)S(1)}, u32[]{:S(2)}, u32[]{:S(2)}) collective-permute-start(bf16[768,256]{1,0:T(8,128)(2,1)S(1)} %collective-permute-done.7.refs_7_), channel_id=1, source_target_pairs={{0,4},{4,0},{8,12},{12,8},{16,20},{20,16},{24,28},{28,24},{1,5},{5... | collective-permute-start | bytes 1179656 | tf_op jit(solution)/shard_map/ppermute | solution.py:53
  40.9 2.2 %collective-permute-start.8 = (bf16[768,256]{1,0:T(8,128)(2,1)S(1)}, bf16[768,256]{1,0:T(8,128)(2,1)S(1)}, u32[]{:S(2)}, u32[]{:S(2)}) collective-permute-start(bf16[768,256]{1,0:T(8,128)(2,1)S(1)} %collective-permute-done.5.refs_5_), channel_id=1, source_target_pairs={{0,4},{4,0},{8,12},{12,8},{16,20},{20,16},{24,28},{28,24},{1,5},{5... | collective-permute-start | bytes 1179656 | tf_op jit(solution)/shard_map/ppermute | solution.py:53
  40.9 2.4 %collective-permute-start.9 = (bf16[768,256]{1,0:T(8,128)(2,1)S(1)}, bf16[768,256]{1,0:T(8,128)(2,1)}, u32[]{:S(2)}, u32[]{:S(2)}) collective-permute-start(bf16[768,256]{1,0:T(8,128)(2,1)S(1)} %collective-permute-done.6.refs_6_), channel_id=1, source_target_pairs={{0,4},{4,0},{8,12},{12,8},{16,20},{20,16},{24,28},{28,24},{1,5},{5... | collective-permute-start | bytes 1179656 | tf_op jit(solution)/shard_map/ppermute | solution.py:53
  47.6 4.9 %collective-permute-start.11 = (f16[392,128]{1,0:T(8,128)(2,1)S(1)}, f16[392,128]{1,0:T(8,128)(2,1)S(1)}, u32[]{:S(2)}, u32[]{:S(2)}) collective-permute-start(f16[392,128]{1,0:T(8,128)(2,1)S(1)} %pad_maximum_fusion.11), channel_id=1, source_target_pairs={{0,8},{4,12},{8,0},{12,4},{16,24},{20,28},{24,16},{28,20},{1,9},{5... | collective-permute-start | bytes 301064 | tf_op jit(solution)/shard_map/ppermute | solution.py:53
  49.3 7.8 %collective-permute-start.12 = (f16[392,128]{1,0:T(8,128)(2,1)S(1)}, f16[392,128]{1,0:T(8,128)(2,1)S(1)}, u32[]{:S(2)}, u32[]{:S(2)}) collective-permute-start(f16[392,128]{1,0:T(8,128)(2,1)S(1)} %pad_maximum_fusion.12), channel_id=1, source_target_pairs={{0,16},{4,20},{8,24},{12,28},{16,0},{20,4},{24,8},{28,12},{1,17},{... | collective-permute-start | bytes 301064 | tf_op jit(solution)/shard_map/ppermute | solution.py:53
  51.0 6.2 %collective-permute-start.13 = (f16[392,128]{1,0:T(8,128)(2,1)S(1)}, f16[392,128]{1,0:T(8,128)(2,1)S(1)}, u32[]{:S(2)}, u32[]{:S(2)}) collective-permute-start(f16[392,128]{1,0:T(8,128)(2,1)S(1)} %pad_maximum_fusion.13), channel_id=1, source_target_pairs={{0,24},{4,28},{8,16},{12,20},{16,8},{20,12},{24,0},{28,4},{1,25},{... | collective-permute-start | bytes 301064 | tf_op jit(solution)/shard_map/ppermute | solution.py:53
  52.6 8.0 %collective-permute-start.17 = (f16[192,128]{1,0:T(8,128)(2,1)S(1)}, f16[192,128]{1,0:T(8,128)(2,1)S(1)}, u32[]{:S(2)}, u32[]{:S(2)}) collective-permute-start(f16[192,128]{1,0:T(8,128)(2,1)S(1)} %get-tuple-element.142), channel_id=1, source_target_pairs={{0,1},{1,0},{2,3},{3,2},{4,5},{5,4},{6,7},{7,6},{8,9},{9,8},{10,11... | collective-permute-start | bytes 147464 | tf_op jit(solution)/shard_map/ppermute | solution.py:53
  52.7 9.3 %collective-permute-start.18 = (f16[192,128]{1,0:T(8,128)(2,1)S(1)}, f16[192,128]{1,0:T(8,128)(2,1)S(1)}, u32[]{:S(2)}, u32[]{:S(2)}) collective-permute-start(f16[192,128]{1,0:T(8,128)(2,1)S(1)} %get-tuple-element.142), channel_id=1, source_target_pairs={{0,2},{1,3},{2,0},{3,1},{4,6},{5,7},{6,4},{7,5},{8,10},{9,11},{10,... | collective-permute-start | bytes 147464 | tf_op jit(solution)/shard_map/ppermute | solution.py:53
  55.7 6.6 %collective-permute-start.19 = (f16[192,128]{1,0:T(8,128)(2,1)S(1)}, f16[192,128]{1,0:T(8,128)(2,1)S(1)}, u32[]{:S(2)}, u32[]{:S(2)}) collective-permute-start(f16[192,128]{1,0:T(8,128)(2,1)S(1)} %get-tuple-element.142), channel_id=1, source_target_pairs={{0,3},{1,2},{2,1},{3,0},{4,7},{5,6},{6,5},{7,4},{8,11},{9,10},{10,... | collective-permute-start | bytes 147464 | tf_op jit(solution)/shard_map/ppermute | solution.py:53
  57.4 8.4 %collective-permute-start.14 = (f16[392,128]{1,0:T(8,128)(2,1)S(1)}, f16[392,128]{1,0:T(8,128)(2,1)S(1)}, u32[]{:S(2)}, u32[]{:S(2)}) collective-permute-start(f16[392,128]{1,0:T(8,128)(2,1)S(1)} %get-tuple-element.136), channel_id=1, source_target_pairs={{0,1},{1,0},{2,3},{3,2},{4,5},{5,4},{6,7},{7,6},{8,9},{9,8},{10,11... | collective-permute-start | bytes 301064 | tf_op jit(solution)/shard_map/ppermute | solution.py:53
  57.5 10.4 %collective-permute-start.15 = (f16[392,128]{1,0:T(8,128)(2,1)S(1)}, f16[392,128]{1,0:T(8,128)(2,1)S(1)}, u32[]{:S(2)}, u32[]{:S(2)}) collective-permute-start(f16[392,128]{1,0:T(8,128)(2,1)S(1)} %get-tuple-element.136), channel_id=1, source_target_pairs={{0,2},{1,3},{2,0},{3,1},{4,6},{5,7},{6,4},{7,5},{8,10},{9,11},{10,... | collective-permute-start | bytes 301064 | tf_op jit(solution)/shard_map/ppermute | solution.py:53
  60.6 7.3 %collective-permute-start.16 = (f16[392,128]{1,0:T(8,128)(2,1)S(1)}, f16[392,128]{1,0:T(8,128)(2,1)S(1)}, u32[]{:S(2)}, u32[]{:S(2)}) collective-permute-start(f16[392,128]{1,0:T(8,128)(2,1)S(1)} %get-tuple-element.136), channel_id=1, source_target_pairs={{0,3},{1,2},{2,1},{3,0},{4,7},{5,6},{6,5},{7,4},{8,11},{9,10},{10,... | collective-permute-start | bytes 301064 | tf_op jit(solution)/shard_map/ppermute | solution.py:53
  62.4 6.8 %collective-permute-start.20 = (f16[4,192,128]{2,1,0:T(8,128)(2,1)S(1)}, f16[4,192,128]{2,1,0:T(8,128)(2,1)S(1)}, u32[]{:S(2)}, u32[]{:S(2)}) collective-permute-start(f16[4,192,128]{2,1,0:T(8,128)(2,1)S(1)} %pad_maximum_fusion.10), channel_id=1, source_target_pairs={{0,8},{4,12},{8,0},{12,4},{16,24},{20,28},{24,16},{28,20},{1,9},{5... | collective-permute-start | bytes 589832 | tf_op jit(solution)/shard_map/ppermute | solution.py:53
  64.3 8.4 %collective-permute-start.21 = (f16[4,192,128]{2,1,0:T(8,128)(2,1)S(1)}, f16[4,192,128]{2,1,0:T(8,128)(2,1)S(1)}, u32[]{:S(2)}, u32[]{:S(2)}) collective-permute-start(f16[4,192,128]{2,1,0:T(8,128)(2,1)S(1)} %pad_maximum_fusion.10), channel_id=1, source_target_pairs={{0,16},{4,20},{8,24},{12,28},{16,0},{20,4},{24,8},{28,12},{1,17},{... | collective-permute-start | bytes 589832 | tf_op jit(solution)/shard_map/ppermute | solution.py:53
  65.8 6.8 %collective-permute-start.22 = (f16[4,192,128]{2,1,0:T(8,128)(2,1)S(1)}, f16[4,192,128]{2,1,0:T(8,128)(2,1)S(1)}, u32[]{:S(2)}, u32[]{:S(2)}) collective-permute-start(f16[4,192,128]{2,1,0:T(8,128)(2,1)S(1)} %pad_maximum_fusion.10), channel_id=1, source_target_pairs={{0,24},{4,28},{8,16},{12,20},{16,8},{20,12},{24,0},{28,4},{1,25},{... | collective-permute-start | bytes 589832 | tf_op jit(solution)/shard_map/ppermute | solution.py:53
  72.6 10.1 %collective-permute-start.30 = (f16[4,192,128]{2,1,0:T(8,128)(2,1)S(1)}, f16[4,192,128]{2,1,0:T(8,128)(2,1)S(1)}, u32[]{:S(2)}, u32[]{:S(2)}) collective-permute-start(f16[4,192,128]{2,1,0:T(8,128)(2,1)S(1)} %collective-permute-done.22), channel_id=1, source_target_pairs={{0,4},{4,0},{8,12},{12,8},{16,20},{20,16},{24,28},{28,24},{1,5},{5... | collective-permute-start | bytes 589832 | tf_op jit(solution)/shard_map/ppermute | solution.py:53
  72.9 10.1 %collective-permute-start.29 = (f16[4,192,128]{2,1,0:T(8,128)(2,1)S(1)}, f16[4,192,128]{2,1,0:T(8,128)(2,1)S(1)}, u32[]{:S(2)}, u32[]{:S(2)}) collective-permute-start(f16[4,192,128]{2,1,0:T(8,128)(2,1)S(1)} %collective-permute-done.21), channel_id=1, source_target_pairs={{0,4},{4,0},{8,12},{12,8},{16,20},{20,16},{24,28},{28,24},{1,5},{5... | collective-permute-start | bytes 589832 | tf_op jit(solution)/shard_map/ppermute | solution.py:53
  74.2 5.3 %collective-permute-start.23 = (f16[392,128]{1,0:T(8,128)(2,1)S(1)}, f16[392,128]{1,0:T(8,128)(2,1)S(1)}, u32[]{:S(2)}, u32[]{:S(2)}) collective-permute-start(f16[392,128]{1,0:T(8,128)(2,1)S(1)} %pad_maximum_fusion.15), channel_id=1, source_target_pairs={{0,8},{4,12},{8,0},{12,4},{16,24},{20,28},{24,16},{28,20},{1,9},{5... | collective-permute-start | bytes 301064 | tf_op jit(solution)/shard_map/ppermute | solution.py:53
  75.1 6.8 %collective-permute-start.24 = (f16[392,128]{1,0:T(8,128)(2,1)S(1)}, f16[392,128]{1,0:T(8,128)(2,1)S(1)}, u32[]{:S(2)}, u32[]{:S(2)}) collective-permute-start(f16[392,128]{1,0:T(8,128)(2,1)S(1)} %pad_maximum_fusion.15), channel_id=1, source_target_pairs={{0,16},{4,20},{8,24},{12,28},{16,0},{20,4},{24,8},{28,12},{1,17},{... | collective-permute-start | bytes 301064 | tf_op jit(solution)/shard_map/ppermute | solution.py:53
  76.0 5.9 %collective-permute-start.25 = (f16[392,128]{1,0:T(8,128)(2,1)S(1)}, f16[392,128]{1,0:T(8,128)(2,1)S(1)}, u32[]{:S(2)}, u32[]{:S(2)}) collective-permute-start(f16[392,128]{1,0:T(8,128)(2,1)S(1)} %pad_maximum_fusion.15), channel_id=1, source_target_pairs={{0,24},{4,28},{8,16},{12,20},{16,8},{20,12},{24,0},{28,4},{1,25},{... | collective-permute-start | bytes 301064 | tf_op jit(solution)/shard_map/ppermute | solution.py:53
  79.6 3.7 %collective-permute-start.28 = (f16[4,192,128]{2,1,0:T(8,128)(2,1)S(1)}, f16[4,192,128]{2,1,0:T(8,128)(2,1)S(1)}, u32[]{:S(2)}, u32[]{:S(2)}) collective-permute-start(f16[4,192,128]{2,1,0:T(8,128)(2,1)S(1)} %collective-permute-done.20), channel_id=1, source_target_pairs={{0,4},{4,0},{8,12},{12,8},{16,20},{20,16},{24,28},{28,24},{1,5},{5... | collective-permute-start | bytes 589832 | tf_op jit(solution)/shard_map/ppermute | solution.py:53
  81.9 1.6 %collective-permute-start.27 = (f16[4,192,128]{2,1,0:T(8,128)(2,1)S(1)}, f16[4,192,128]{2,1,0:T(8,128)(2,1)S(1)}, u32[]{:S(2)}, u32[]{:S(2)}) collective-permute-start(f16[4,192,128]{2,1,0:T(8,128)(2,1)S(1)} %pad_maximum_fusion.10), channel_id=1, source_target_pairs={{0,4},{4,0},{8,12},{12,8},{16,20},{20,16},{24,28},{28,24},{1,5},{5... | collective-permute-start | bytes 589832 | tf_op jit(solution)/shard_map/ppermute | solution.py:53
  82.0 4.1 %collective-permute-start.26 = (f16[4,392,128]{2,1,0:T(8,128)(2,1)S(1)}, f16[4,392,128]{2,1,0:T(8,128)(2,1)S(1)}, u32[]{:S(2)}, u32[]{:S(2)}) collective-permute-start(f16[4,392,128]{2,1,0:T(8,128)(2,1)S(1)} %pad_maximum_fusion.1), channel_id=1, source_target_pairs={{0,4},{4,0},{8,12},{12,8},{16,20},{20,16},{24,28},{28,24},{1,5},{5... | collective-permute-start | bytes 1204232 | tf_op jit(solution)/shard_map/ppermute | solution.py:53

commit v6 on v5

--- a/solution.py
+++ b/solution.py
@@ -88,6 +88,11 @@
     bound = jnp.exp2(value[-SUB:])
     scaled = value[:-SUB].reshape(-1, SUB, LANES) * (bound * 2.0**-TOP)
     return jnp.concatenate([scaled.reshape(-1, LANES), bound])
+
+
+def unscale(value, power):
+    unit = jnp.exp2(power - TOP)
+    return jnp.concatenate([value[rows] * unit for rows in spans(value.shape[0] // SUB, SUB)])
 
 
 def largest(value):
@@ -246,11 +251,13 @@
         row = 2 * lax.bitwise_xor(chip, offset) + lax.bitwise_xor(core, other)
         for z in range(n_batch):
             group = lax.bitwise_xor(batch, z)
-            diagonal[group, pl.ds(pl.multiple_of(row * part, SUB), part), :] = block[z, :part, :]
+            own = pl.ds(pl.multiple_of(row * part, SUB), part)
+            diagonal[group, own, :] = unscale(block[z, :part, :], block[z, part : part + SUB, :])
+            power = block[z, block.shape[1] - SUB :, :]
             first = pl.multiple_of(group * basis + row * share, SUB)
             for k, lanes in enumerate(spans(size // LANES, LANES)):
                 lower = part + SUB + k * share
-                whole[pl.ds(first, share), lanes] = block[z, lower : lower + share, :]
+                whole[pl.ds(first, share), lanes] = unscale(block[z, lower : lower + share, :], power)
     for rows in spans(columns // LANES, LANES):
         high[:, rows], low[:, rows] = split(whole[rows, :].T)
 
@@ -446,14 +453,12 @@
     mine = [mine] + [swap(mine, "rows", offset) for offset in other_chips]
     total, mine = lax.optimization_barrier((total, mine))
 
-    def decode_message(blocks):
-        return jnp.stack([jnp.concatenate([decode(b[: part + SUB]), decode(b[part + SUB :])]) for b in blocks])
-
     high, low, diagonal = call(
         prepare_kernel,
         [((size, columns), bf16)] * 2 + [((n_batch, own_count * LANES, LANES), f32)],
         [((columns, size), f32)],
-        at, *map(decode_message, mine + [swap(block, "rows", 1) for block in mine]), n_smem=1, moved=8 << 20,
+        at, *(block.astype(f32) for block in mine + [swap(block, "rows", 1) for block in mine]),
+        n_smem=1, moved=8 << 20,
     )
 
     cross = spread_copy(total, "rows", other_chips)

time: 115 us -> 112 us (0.974)
  other arithmetic: 4.78 us -> 2.94 us
  between operations: 2.24 us -> 0.57 us
  transfers between devices with their start and end apart: 31 -> 31, of which waited for: 13 -> 13; matrix products, arithmetic and copies ran while one was open for 4% -> 2% of each run, Pallas kernels for 2% -> 2%
where the time goes in v6:
time: 112 us
  waiting for transfers between devices  37.1 us (33%)
  Pallas kernels  34.9 us (31%)
  starting transfers between devices  33.7 us (30%)
  other arithmetic  2.94 us (3%)
  local copies, waits for them, and re-layouts  2.52 us (2%)
    ppermute x31, waiting for transfers between devices, swap(): return lax.ppermute(value, axis, [(i, i ^ offset) for i in range(size)])  37.1 us
    pallas_call x4, Pallas kernels, call(): pl.pallas_call(body, out_shape=[jax.ShapeDtypeStruct(shape, dtype) for sh...  34.9 us
    ppermute x31, starting transfers between devices, swap(): return lax.ppermute(value, axis, [(i, i ^ offset) for i in range(size)])  33.7 us
  transfers between devices with their start and end apart: 31, of which 13 were waited for; matrix products, arithmetic and copies ran while one was open for 2% of the time, Pallas kernels for 2%

profile of v6, /device:TPU:0, one launch (start us, length us, event | category | flops | bytes accessed | tf_op | source)
XLA Modules:
  0.0 111.8 jit_solution(6240664988805970976)
XLA Ops:
  0.0 1.6 %constant_dynamic-slice_fusion = (bf16[768,256]{1,0:T(8,128)(2,1)S(1)}, bf16[768,256]{1,0:T(8,128)(2,1)S(1)}, bf16[768,256]{1,0:T(8,128)(2,1)S(1)}, bf16[768,256]{1,0:T(8,128)(2,1)S(1)}) fusion(bf16[3072,256]{1,0:T(8,128)(2,1)} %refs_0_.1, s32[]{:T(128)S(6)} %select_n.28, s32[]{:T(128)S(6)} %select_n.26, s32[]{:T(128)S(6)} %select_n.25, s32[]{:T(128)S(6)} %select_n.27), kind=kLoop, calls=%fused_computation.104 | loop fusion | bytes 3145744 | tf_op jit(solution)/shard_map/dynamic_slice | solution.py:421
  1.6 0.5 collective-permute-start
  2.1 4.7 %collective-permute-start.7 = (bf16[768,256]{1,0:T(8,128)(2,1)S(1)}, bf16[768,256]{1,0:T(8,128)(2,1)S(1)}, u32[]{:S(2)}, u32[]{:S(2)}) collective-permute-start(bf16[768,256]{1,0:T(8,128)(2,1)S(1)} %get-tuple-element.45), channel_id=1, source_target_pairs={{0,3},{1,2},{2,1},{3,0},{4,7},{5,6},{6,5},{7,4},{8,11},{9,10},{10,... | collective-permute-start | bytes 1179656 | tf_op jit(solution)/shard_map/ppermute | solution.py:53
  6.8 0.6 collective-permute-start.6
  7.4 0.0 collective-permute-done.refs_1_.refs_8_
  7.4 0.8 shard_map.37
  8.2 0.1 collective-permute-start.1
  8.3 1.4 %collective-permute-done.1 = f32[384,128]{1,0:T(8,128)S(1)} collective-permute-done((f32[384,128]{1,0:T(8,128)S(1)}, f32[384,128]{1,0:T(8,128)S(1)}, u32[]{:S(2)}, u32[]{:S(2)}) %collective-permute-start.1) | collective-permute-done | bytes 196640 | tf_op jit(solution)/shard_map/ppermute | solution.py:53
  9.8 1.7 %collective-permute-start.2 = (f32[384,128]{1,0:T(8,128)S(1)}, f32[384,128]{1,0:T(8,128)S(1)}, u32[]{:S(2)}, u32[]{:S(2)}) collective-permute-start(f32[384,128]{1,0:T(8,128)S(1)} %add.73), channel_id=1, source_target_pairs={{0,8},{4,12},{8,0},{12,4},{16,24},{20,28},{24,16},{28,20},{1,9},{5... | collective-permute-start | bytes 589832 | tf_op jit(solution)/shard_map/ppermute | solution.py:53
  11.5 1.5 %collective-permute-start.3 = (f32[384,128]{1,0:T(8,128)S(1)}, f32[384,128]{1,0:T(8,128)}, u32[]{:S(2)}, u32[]{:S(2)}) collective-permute-start(f32[384,128]{1,0:T(8,128)S(1)} %add.73), channel_id=1, source_target_pairs={{0,16},{4,20},{8,24},{12,28},{16,0},{20,4},{24,8},{28,12},{1,17},{... | collective-permute-start | bytes 589832 | tf_op jit(solution)/shard_map/ppermute | solution.py:53
  13.0 3.8 %collective-permute-done.7.refs_7_ = bf16[768,256]{1,0:T(8,128)(2,1)S(1)} collective-permute-done((bf16[768,256]{1,0:T(8,128)(2,1)S(1)}, bf16[768,256]{1,0:T(8,128)(2,1)S(1)}, u32[]{:S(2)}, u32[]{:S(2)}) %collective-permute-start.7) | collective-permute-done | bytes 393248 | tf_op jit(solution)/shard_map/ppermute | solution.py:53
  16.8 2.6 %collective-permute-start.4 = (f32[384,128]{1,0:T(8,128)S(1)}, f32[384,128]{1,0:T(8,128)}, u32[]{:S(2)}, u32[]{:S(2)}) collective-permute-start(f32[384,128]{1,0:T(8,128)S(1)} %add.73), channel_id=1, source_target_pairs={{0,24},{4,28},{8,16},{12,20},{16,8},{20,12},{24,0},{28,4},{1,25},{... | collective-permute-start | bytes 589832 | tf_op jit(solution)/shard_map/ppermute | solution.py:53
  19.4 6.6 %collective-permute-done.5.refs_5_ = bf16[768,256]{1,0:T(8,128)(2,1)S(1)} collective-permute-done((bf16[768,256]{1,0:T(8,128)(2,1)S(1)}, bf16[768,256]{1,0:T(8,128)(2,1)S(1)}, u32[]{:S(2)}, u32[]{:S(2)}) %collective-permute-start.5) | collective-permute-done | bytes 393248 | tf_op jit(solution)/shard_map/ppermute | solution.py:53
  26.0 0.0 collective-permute-start.10
  26.1 14.9 %collective-permute-done.6.refs_6_ = bf16[768,256]{1,0:T(8,128)(2,1)S(1)} collective-permute-done((bf16[768,256]{1,0:T(8,128)(2,1)S(1)}, bf16[768,256]{1,0:T(8,128)(2,1)S(1)}, u32[]{:S(2)}, u32[]{:S(2)}) %collective-permute-start.6) | collective-permute-done | bytes 393248 | tf_op jit(solution)/shard_map/ppermute | solution.py:53
  40.9 0.0 collective-permute-start.8
  40.9 0.0 collective-permute-done.2
  40.9 0.7 copy-done.3
  41.6 0.5 collective-permute-start.9
  42.1 0.1 pad_add_fusion.refs_0_
  42.2 0.0 collective-permute-done.3
  42.2 0.0 collective-permute-done.4
  42.2 1.2 %add_add_fusion.refs_3_ = f32[384,128]{1,0:T(8,128)S(1)} fusion(f32[384,128]{1,0:T(8,128)} %collective-permute-done.4, f32[384,128]{1,0:T(8,128)} %collective-permute-done.3, f32[384,128]{1,0:T(8,128)S(1)} %add.73, f32[384,128]{1,0:T(8,128)} %copy-done.3), kind=kLoop, calls=%fused_computation.30 | loop fusion | flops 147456 | bytes 983040 | tf_op jit(solution)/shard_map/add | solution.py:431
  43.4 0.0 collective-permute-done.10.refs_11_
  43.4 0.0 collective-permute-done.8.refs_9_
  43.4 0.2 collective-permute-done.9.refs_10_
  43.6 4.1 %shard_map.38 = (bf16[768,1024]{1,0:T(8,128)(2,1)S(1)}, f32[192,128]{1,0:T(8,128)S(1)}, f32[392,128]{1,0:T(8,128)S(1)}, f32[392,128]{1,0:T(8,128)S(1)}, f32[392,128]{1,0:T(8,128)S(1)}, /*index=5*/f32[392,128]{1,0:T(8,128)S(1)}) custom-call(s32[3]{0:T(128)S(1)} %pad_add_fusion.refs_0_, s32[48]{0:T(128)S(1)} %copy-done.2, f32[256,512]{1,0:T(8,128)S(1)} %copy-done.1, ...), custom_call_target="tpu_custom_call" | custom-call | flops 603979776 | bytes 6291456 | tf_op jit(solution)/shard_map/pallas_call | solution.py:409
  47.8 1.6 %collective-permute-start.11 = (f16[392,128]{1,0:T(8,128)(2,1)S(1)}, f16[392,128]{1,0:T(8,128)(2,1)S(1)}, u32[]{:S(2)}, u32[]{:S(2)}) collective-permute-start(f16[392,128]{1,0:T(8,128)(2,1)S(1)} %pad_maximum_fusion.3), channel_id=1, source_target_pairs={{0,8},{4,12},{8,0},{12,4},{16,24},{20,28},{24,16},{28,20},{1,9},{5... | collective-permute-start | bytes 301064 | tf_op jit(solution)/shard_map/ppermute | solution.py:53
  49.5 1.6 %collective-permute-start.12 = (f16[392,128]{1,0:T(8,128)(2,1)S(1)}, f16[392,128]{1,0:T(8,128)(2,1)S(1)}, u32[]{:S(2)}, u32[]{:S(2)}) collective-permute-start(f16[392,128]{1,0:T(8,128)(2,1)S(1)} %pad_maximum_fusion.4), channel_id=1, source_target_pairs={{0,16},{4,20},{8,24},{12,28},{16,0},{20,4},{24,8},{28,12},{1,17},{... | collective-permute-start | bytes 301064 | tf_op jit(solution)/shard_map/ppermute | solution.py:53
  51.2 0.5 collective-permute-start.13
  51.8 1.2 %collective-permute-done.11 = f16[392,128]{1,0:T(8,128)(2,1)S(1)} collective-permute-done((f16[392,128]{1,0:T(8,128)(2,1)S(1)}, f16[392,128]{1,0:T(8,128)(2,1)S(1)}, u32[]{:S(2)}, u32[]{:S(2)}) %collective-permute-start.11) | collective-permute-done | bytes 100384 | tf_op jit(solution)/shard_map/ppermute | solution.py:53
  53.1 0.1 collective-permute-start.17
  53.2 3.1 %collective-permute-start.18 = (f16[192,128]{1,0:T(8,128)(2,1)S(1)}, f16[192,128]{1,0:T(8,128)(2,1)S(1)}, u32[]{:S(2)}, u32[]{:S(2)}) collective-permute-start(f16[192,128]{1,0:T(8,128)(2,1)S(1)} %get-tuple-element.78), channel_id=1, source_target_pairs={{0,2},{1,3},{2,0},{3,1},{4,6},{5,7},{6,4},{7,5},{8,10},{9,11},{10,... | collective-permute-start | bytes 147464 | tf_op jit(solution)/shard_map/ppermute | solution.py:53
  56.2 1.3 %collective-permute-start.19 = (f16[192,128]{1,0:T(8,128)(2,1)S(1)}, f16[192,128]{1,0:T(8,128)(2,1)S(1)}, u32[]{:S(2)}, u32[]{:S(2)}) collective-permute-start(f16[192,128]{1,0:T(8,128)(2,1)S(1)} %get-tuple-element.78), channel_id=1, source_target_pairs={{0,3},{1,2},{2,1},{3,0},{4,7},{5,6},{6,5},{7,4},{8,11},{9,10},{10,... | collective-permute-start | bytes 147464 | tf_op jit(solution)/shard_map/ppermute | solution.py:53
  57.6 0.0 collective-permute-done.12
  57.6 0.0 collective-permute-done.13
  57.8 0.1 fusion.1
  57.9 0.1 collective-permute-start.14
  58.0 3.1 %collective-permute-start.15 = (f16[392,128]{1,0:T(8,128)(2,1)S(1)}, f16[392,128]{1,0:T(8,128)(2,1)S(1)}, u32[]{:S(2)}, u32[]{:S(2)}) collective-permute-start(f16[392,128]{1,0:T(8,128)(2,1)S(1)} %get-tuple-element.72), channel_id=1, source_target_pairs={{0,2},{1,3},{2,0},{3,1},{4,6},{5,7},{6,4},{7,5},{8,10},{9,11},{10,... | collective-permute-start | bytes 301064 | tf_op jit(solution)/shard_map/ppermute | solution.py:53
  61.1 1.4 %collective-permute-start.16 = (f16[392,128]{1,0:T(8,128)(2,1)S(1)}, f16[392,128]{1,0:T(8,128)(2,1)S(1)}, u32[]{:S(2)}, u32[]{:S(2)}) collective-permute-start(f16[392,128]{1,0:T(8,128)(2,1)S(1)} %get-tuple-element.72), channel_id=1, source_target_pairs={{0,3},{1,2},{2,1},{3,0},{4,7},{5,6},{6,5},{7,4},{8,11},{9,10},{10,... | collective-permute-start | bytes 301064 | tf_op jit(solution)/shard_map/ppermute | solution.py:53
  62.5 0.3 collective-permute-done.19
  62.8 0.1 pad_maximum_fusion.2
  62.8 2.0 %collective-permute-start.20 = (f16[4,192,128]{2,1,0:T(8,128)(2,1)S(1)}, f16[4,192,128]{2,1,0:T(8,128)(2,1)S(1)}, u32[]{:S(2)}, u32[]{:S(2)}) collective-permute-start(f16[4,192,128]{2,1,0:T(8,128)(2,1)S(1)} %pad_maximum_fusion.2), channel_id=1, source_target_pairs={{0,8},{4,12},{8,0},{12,4},{16,24},{20,28},{24,16},{28,20},{1,9},{5... | collective-permute-start | bytes 589832 | tf_op jit(solution)/shard_map/ppermute | solution.py:53
  64.8 1.5 %collective-permute-start.21 = (f16[4,192,128]{2,1,0:T(8,128)(2,1)S(1)}, f16[4,192,128]{2,1,0:T(8,128)(2,1)S(1)}, u32[]{:S(2)}, u32[]{:S(2)}) collective-permute-start(f16[4,192,128]{2,1,0:T(8,128)(2,1)S(1)} %pad_maximum_fusion.2), channel_id=1, source_target_pairs={{0,16},{4,20},{8,24},{12,28},{16,0},{20,4},{24,8},{28,12},{1,17},{... | collective-permute-start | bytes 589832 | tf_op jit(solution)/shard_map/ppermute | solution.py:53
  66.3 1.1 collective-permute-start.22
  67.5 1.0 collective-permute-done.15
  68.8 1.0 collective-permute-done.20
  69.8 3.8 %collective-permute-done.21 = f16[4,192,128]{2,1,0:T(8,128)(2,1)S(1)} collective-permute-done((f16[4,192,128]{2,1,0:T(8,128)(2,1)S(1)}, f16[4,192,128]{2,1,0:T(8,128)(2,1)S(1)}, u32[]{:S(2)}, u32[]{:S(2)}) %collective-permute-start.21) | collective-permute-done | bytes 196640 | tf_op jit(solution)/shard_map/ppermute | solution.py:53
  73.6 1.4 %collective-permute-start.23 = (f16[392,128]{1,0:T(8,128)(2,1)S(1)}, f16[392,128]{1,0:T(8,128)(2,1)S(1)}, u32[]{:S(2)}, u32[]{:S(2)}) collective-permute-start(f16[392,128]{1,0:T(8,128)(2,1)S(1)} %pad_maximum_fusion.7), channel_id=1, source_target_pairs={{0,8},{4,12},{8,0},{12,4},{16,24},{20,28},{24,16},{28,20},{1,9},{5... | collective-permute-start | bytes 301064 | tf_op jit(solution)/shard_map/ppermute | solution.py:53
  75.0 0.2 collective-permute-start.24
  75.2 1.9 %collective-permute-start.25 = (f16[392,128]{1,0:T(8,128)(2,1)S(1)}, f16[392,128]{1,0:T(8,128)(2,1)S(1)}, u32[]{:S(2)}, u32[]{:S(2)}) collective-permute-start(f16[392,128]{1,0:T(8,128)(2,1)S(1)} %pad_maximum_fusion.7), channel_id=1, source_target_pairs={{0,24},{4,28},{8,16},{12,20},{16,8},{20,12},{24,0},{28,4},{1,25},{... | collective-permute-start | bytes 301064 | tf_op jit(solution)/shard_map/ppermute | solution.py:53
  77.1 0.1 collective-permute-start.27
  77.2 0.6 collective-permute-start.28
  77.9 0.3 collective-permute-done.23
  78.2 1.4 %collective-permute-done.24 = f16[392,128]{1,0:T(8,128)(2,1)S(1)} collective-permute-done((f16[392,128]{1,0:T(8,128)(2,1)S(1)}, f16[392,128]{1,0:T(8,128)(2,1)S(1)}, u32[]{:S(2)}, u32[]{:S(2)}) %collective-permute-start.24) | collective-permute-done | bytes 100384 | tf_op jit(solution)/shard_map/ppermute | solution.py:53
  79.6 1.1 collective-permute-done.25
  80.7 0.1 pad_maximum_fusion.1
  80.9 0.1 collective-permute-start.26
  81.3 1.5 %shard_map.39 = (bf16[512,1024]{1,0:T(8,128)(2,1)S(1)}, bf16[512,1024]{1,0:T(8,128)(2,1)S(1)}, f32[4,384,128]{2,1,0:T(8,128)S(1)}) custom-call(s32[3]{0:T(128)S(1)} %pad_add_fusion.refs_0_, f32[4,192,128]{2,1,0:T(8,128)S(1)} %convert_element_type.68.refs_1_, f32[4,192,128]{2,1,0:T(8,128)S(1)} %convert_element_type.69.refs_2_, ...), custom_call_target="tpu_custom_call" | custom-call | bytes 8388608 | tf_op jit(solution)/shard_map/pallas_call | solution.py:409
  82.8 0.1 constant_dynamic-update-slice_fusion
  82.9 0.1 convert_element_type.67
  83.1 0.1 slice_multiply_fusion
  83.2 0.1 pad_maximum_fusion.refs_2_
  83.3 28.5 %shard_map.40 = bf16[768,512]{1,0:T(8,128)(2,1)} custom-call(s32[3]{0:T(128)S(1)} %pad_add_fusion.refs_0_, s32[48]{0:T(128)S(1)} %copy-done.2, f32[8,392,128]{2,1,0:T(8,128)S(1)} %pad_maximum_fusion.refs_2_, f32[4,384,128]{2,1,0:T(8,128)S(1)} %get-tuple-element.33.refs_3_, bf16[512,1024]{1,0:T(8,128)(2,1)S(1)} %get-tuple-element.34.refs_4_, ...), custom_call_target="tpu_custom_call" | custom-call | flops 10000000000 | bytes 10485760 | tf_op jit(solution)/shard_map/pallas_call | solution.py:409
  (80 shorter events, 1.3 us)
Async XLA Ops:
  0.0 7.4 %copy-start = (bf16[3072,256]{1,0:T(8,128)(2,1)S(1)}, bf16[3072,256]{1,0:T(8,128)(2,1)}, u32[]{:S(2)}) copy-start(bf16[3072,256]{1,0:T(8,128)(2,1)} %refs_0_.1) | copy-start | bytes 4718596
  1.6 5.8 %collective-permute-start = (bf16[768,256]{1,0:T(8,128)(2,1)S(1)}, bf16[768,256]{1,0:T(8,128)(2,1)S(1)}, u32[]{:S(2)}, u32[]{:S(2)}) collective-permute-start(bf16[768,256]{1,0:T(8,128)(2,1)S(1)} %get-tuple-element.47.refs_4_), channel_id=1, source_target_pairs={{0,4},{4,0},{8,12},{12,8},{16,20},{20,16},{24,28},{28,24},{1,5},{5... | collective-permute-start | bytes 1179656 | tf_op jit(solution)/shard_map/ppermute | solution.py:53
  2.1 14.7 %collective-permute-start.7 = (bf16[768,256]{1,0:T(8,128)(2,1)S(1)}, bf16[768,256]{1,0:T(8,128)(2,1)S(1)}, u32[]{:S(2)}, u32[]{:S(2)}) collective-permute-start(bf16[768,256]{1,0:T(8,128)(2,1)S(1)} %get-tuple-element.45), channel_id=1, source_target_pairs={{0,3},{1,2},{2,1},{3,0},{4,7},{5,6},{6,5},{7,4},{8,11},{9,10},{10,... | collective-permute-start | bytes 1179656 | tf_op jit(solution)/shard_map/ppermute | solution.py:53
  6.8 19.3 %collective-permute-start.5 = (bf16[768,256]{1,0:T(8,128)(2,1)S(1)}, bf16[768,256]{1,0:T(8,128)(2,1)S(1)}, u32[]{:S(2)}, u32[]{:S(2)}) collective-permute-start(bf16[768,256]{1,0:T(8,128)(2,1)S(1)} %get-tuple-element.46), channel_id=1, source_target_pairs={{0,1},{1,0},{2,3},{3,2},{4,5},{5,4},{6,7},{7,6},{8,9},{9,8},{10,11... | collective-permute-start | bytes 1179656 | tf_op jit(solution)/shard_map/ppermute | solution.py:53
  6.8 36.8 %copy-start.1 = (f32[256,512]{1,0:T(8,128)S(1)}, f32[256,512]{1,0:T(8,128)}, u32[]{:S(2)}) copy-start(f32[256,512]{1,0:T(8,128)} %refs_2_.1) | copy-start | bytes 1572868
  6.8 36.8 %copy-start.2 = (s32[48]{0:T(128)S(1)}, s32[48]{0:T(128)}, u32[]{:S(2)}) copy-start(s32[48]{0:T(128)} %constant.57.clone.refs_1_) | copy-start | bytes 580
  6.8 34.1 %collective-permute-start.6 = (bf16[768,256]{1,0:T(8,128)(2,1)S(1)}, bf16[768,256]{1,0:T(8,128)(2,1)S(1)}, u32[]{:S(2)}, u32[]{:S(2)}) collective-permute-start(bf16[768,256]{1,0:T(8,128)(2,1)S(1)} %get-tuple-element.48), channel_id=1, source_target_pairs={{0,2},{1,3},{2,0},{3,1},{4,6},{5,7},{6,4},{7,5},{8,10},{9,11},{10,... | collective-permute-start | bytes 1179656 | tf_op jit(solution)/shard_map/ppermute | solution.py:53
  8.2 1.5 %collective-permute-start.1 = (f32[384,128]{1,0:T(8,128)S(1)}, f32[384,128]{1,0:T(8,128)S(1)}, u32[]{:S(2)}, u32[]{:S(2)}) collective-permute-start(f32[384,128]{1,0:T(8,128)S(1)} %shard_map.37), channel_id=1, source_target_pairs={{0,4},{4,0},{8,12},{12,8},{16,20},{20,16},{24,28},{28,24},{1,5},{5... | collective-permute-start | bytes 589832 | tf_op jit(solution)/shard_map/ppermute | solution.py:53
  9.8 31.2 %collective-permute-start.2 = (f32[384,128]{1,0:T(8,128)S(1)}, f32[384,128]{1,0:T(8,128)S(1)}, u32[]{:S(2)}, u32[]{:S(2)}) collective-permute-start(f32[384,128]{1,0:T(8,128)S(1)} %add.73), channel_id=1, source_target_pairs={{0,8},{4,12},{8,0},{12,4},{16,24},{20,28},{24,16},{28,20},{1,9},{5... | collective-permute-start | bytes 589832 | tf_op jit(solution)/shard_map/ppermute | solution.py:53
  11.5 30.7 %collective-permute-start.3 = (f32[384,128]{1,0:T(8,128)S(1)}, f32[384,128]{1,0:T(8,128)}, u32[]{:S(2)}, u32[]{:S(2)}) collective-permute-start(f32[384,128]{1,0:T(8,128)S(1)} %add.73), channel_id=1, source_target_pairs={{0,16},{4,20},{8,24},{12,28},{16,0},{20,4},{24,8},{28,12},{1,17},{... | collective-permute-start | bytes 589832 | tf_op jit(solution)/shard_map/ppermute | solution.py:53
  16.8 25.4 %collective-permute-start.4 = (f32[384,128]{1,0:T(8,128)S(1)}, f32[384,128]{1,0:T(8,128)}, u32[]{:S(2)}, u32[]{:S(2)}) collective-permute-start(f32[384,128]{1,0:T(8,128)S(1)} %add.73), channel_id=1, source_target_pairs={{0,24},{4,28},{8,16},{12,20},{16,8},{20,12},{24,0},{28,4},{1,25},{... | collective-permute-start | bytes 589832 | tf_op jit(solution)/shard_map/ppermute | solution.py:53
  26.0 17.3 %collective-permute-start.10 = (bf16[768,256]{1,0:T(8,128)(2,1)S(1)}, bf16[768,256]{1,0:T(8,128)(2,1)S(1)}, u32[]{:S(2)}, u32[]{:S(2)}) collective-permute-start(bf16[768,256]{1,0:T(8,128)(2,1)S(1)} %collective-permute-done.7.refs_7_), channel_id=1, source_target_pairs={{0,4},{4,0},{8,12},{12,8},{16,20},{20,16},{24,28},{28,24},{1,5},{5... | collective-permute-start | bytes 1179656 | tf_op jit(solution)/shard_map/ppermute | solution.py:53
  40.9 2.5 %collective-permute-start.8 = (bf16[768,256]{1,0:T(8,128)(2,1)S(1)}, bf16[768,256]{1,0:T(8,128)(2,1)S(1)}, u32[]{:S(2)}, u32[]{:S(2)}) collective-permute-start(bf16[768,256]{1,0:T(8,128)(2,1)S(1)} %collective-permute-done.5.refs_5_), channel_id=1, source_target_pairs={{0,4},{4,0},{8,12},{12,8},{16,20},{20,16},{24,28},{28,24},{1,5},{5... | collective-permute-start | bytes 1179656 | tf_op jit(solution)/shard_map/ppermute | solution.py:53
  40.9 0.7 copy-start.3
  41.6 2.0 %collective-permute-start.9 = (bf16[768,256]{1,0:T(8,128)(2,1)S(1)}, bf16[768,256]{1,0:T(8,128)(2,1)}, u32[]{:S(2)}, u32[]{:S(2)}) collective-permute-start(bf16[768,256]{1,0:T(8,128)(2,1)S(1)} %collective-permute-done.6.refs_6_), channel_id=1, source_target_pairs={{0,4},{4,0},{8,12},{12,8},{16,20},{20,16},{24,28},{28,24},{1,5},{5... | collective-permute-start | bytes 1179656 | tf_op jit(solution)/shard_map/ppermute | solution.py:53
  47.8 5.2 %collective-permute-start.11 = (f16[392,128]{1,0:T(8,128)(2,1)S(1)}, f16[392,128]{1,0:T(8,128)(2,1)S(1)}, u32[]{:S(2)}, u32[]{:S(2)}) collective-permute-start(f16[392,128]{1,0:T(8,128)(2,1)S(1)} %pad_maximum_fusion.3), channel_id=1, source_target_pairs={{0,8},{4,12},{8,0},{12,4},{16,24},{20,28},{24,16},{28,20},{1,9},{5... | collective-permute-start | bytes 301064 | tf_op jit(solution)/shard_map/ppermute | solution.py:53
  49.5 8.0 %collective-permute-start.12 = (f16[392,128]{1,0:T(8,128)(2,1)S(1)}, f16[392,128]{1,0:T(8,128)(2,1)S(1)}, u32[]{:S(2)}, u32[]{:S(2)}) collective-permute-start(f16[392,128]{1,0:T(8,128)(2,1)S(1)} %pad_maximum_fusion.4), channel_id=1, source_target_pairs={{0,16},{4,20},{8,24},{12,28},{16,0},{20,4},{24,8},{28,12},{1,17},{... | collective-permute-start | bytes 301064 | tf_op jit(solution)/shard_map/ppermute | solution.py:53
  51.2 6.4 %collective-permute-start.13 = (f16[392,128]{1,0:T(8,128)(2,1)S(1)}, f16[392,128]{1,0:T(8,128)(2,1)S(1)}, u32[]{:S(2)}, u32[]{:S(2)}) collective-permute-start(f16[392,128]{1,0:T(8,128)(2,1)S(1)} %pad_maximum_fusion.5), channel_id=1, source_target_pairs={{0,24},{4,28},{8,16},{12,20},{16,8},{20,12},{24,0},{28,4},{1,25},{... | collective-permute-start | bytes 301064 | tf_op jit(solution)/shard_map/ppermute | solution.py:53
  53.1 8.0 %collective-permute-start.17 = (f16[192,128]{1,0:T(8,128)(2,1)S(1)}, f16[192,128]{1,0:T(8,128)(2,1)S(1)}, u32[]{:S(2)}, u32[]{:S(2)}) collective-permute-start(f16[192,128]{1,0:T(8,128)(2,1)S(1)} %get-tuple-element.78), channel_id=1, source_target_pairs={{0,1},{1,0},{2,3},{3,2},{4,5},{5,4},{6,7},{7,6},{8,9},{9,8},{10,11... | collective-permute-start | bytes 147464 | tf_op jit(solution)/shard_map/ppermute | solution.py:53
  53.2 9.3 %collective-permute-start.18 = (f16[192,128]{1,0:T(8,128)(2,1)S(1)}, f16[192,128]{1,0:T(8,128)(2,1)S(1)}, u32[]{:S(2)}, u32[]{:S(2)}) collective-permute-start(f16[192,128]{1,0:T(8,128)(2,1)S(1)} %get-tuple-element.78), channel_id=1, source_target_pairs={{0,2},{1,3},{2,0},{3,1},{4,6},{5,7},{6,4},{7,5},{8,10},{9,11},{10,... | collective-permute-start | bytes 147464 | tf_op jit(solution)/shard_map/ppermute | solution.py:53
  56.2 6.5 %collective-permute-start.19 = (f16[192,128]{1,0:T(8,128)(2,1)S(1)}, f16[192,128]{1,0:T(8,128)(2,1)S(1)}, u32[]{:S(2)}, u32[]{:S(2)}) collective-permute-start(f16[192,128]{1,0:T(8,128)(2,1)S(1)} %get-tuple-element.78), channel_id=1, source_target_pairs={{0,3},{1,2},{2,1},{3,0},{4,7},{5,6},{6,5},{7,4},{8,11},{9,10},{10,... | collective-permute-start | bytes 147464 | tf_op jit(solution)/shard_map/ppermute | solution.py:53
  57.9 8.4 %collective-permute-start.14 = (f16[392,128]{1,0:T(8,128)(2,1)S(1)}, f16[392,128]{1,0:T(8,128)(2,1)S(1)}, u32[]{:S(2)}, u32[]{:S(2)}) collective-permute-start(f16[392,128]{1,0:T(8,128)(2,1)S(1)} %get-tuple-element.72), channel_id=1, source_target_pairs={{0,1},{1,0},{2,3},{3,2},{4,5},{5,4},{6,7},{7,6},{8,9},{9,8},{10,11... | collective-permute-start | bytes 301064 | tf_op jit(solution)/shard_map/ppermute | solution.py:53
  58.0 10.5 %collective-permute-start.15 = (f16[392,128]{1,0:T(8,128)(2,1)S(1)}, f16[392,128]{1,0:T(8,128)(2,1)S(1)}, u32[]{:S(2)}, u32[]{:S(2)}) collective-permute-start(f16[392,128]{1,0:T(8,128)(2,1)S(1)} %get-tuple-element.72), channel_id=1, source_target_pairs={{0,2},{1,3},{2,0},{3,1},{4,6},{5,7},{6,4},{7,5},{8,10},{9,11},{10,... | collective-permute-start | bytes 301064 | tf_op jit(solution)/shard_map/ppermute | solution.py:53
  61.1 7.4 %collective-permute-start.16 = (f16[392,128]{1,0:T(8,128)(2,1)S(1)}, f16[392,128]{1,0:T(8,128)(2,1)S(1)}, u32[]{:S(2)}, u32[]{:S(2)}) collective-permute-start(f16[392,128]{1,0:T(8,128)(2,1)S(1)} %get-tuple-element.72), channel_id=1, source_target_pairs={{0,3},{1,2},{2,1},{3,0},{4,7},{5,6},{6,5},{7,4},{8,11},{9,10},{10,... | collective-permute-start | bytes 301064 | tf_op jit(solution)/shard_map/ppermute | solution.py:53
  62.8 7.0 %collective-permute-start.20 = (f16[4,192,128]{2,1,0:T(8,128)(2,1)S(1)}, f16[4,192,128]{2,1,0:T(8,128)(2,1)S(1)}, u32[]{:S(2)}, u32[]{:S(2)}) collective-permute-start(f16[4,192,128]{2,1,0:T(8,128)(2,1)S(1)} %pad_maximum_fusion.2), channel_id=1, source_target_pairs={{0,8},{4,12},{8,0},{12,4},{16,24},{20,28},{24,16},{28,20},{1,9},{5... | collective-permute-start | bytes 589832 | tf_op jit(solution)/shard_map/ppermute | solution.py:53
  64.8 8.8 %collective-permute-start.21 = (f16[4,192,128]{2,1,0:T(8,128)(2,1)S(1)}, f16[4,192,128]{2,1,0:T(8,128)(2,1)S(1)}, u32[]{:S(2)}, u32[]{:S(2)}) collective-permute-start(f16[4,192,128]{2,1,0:T(8,128)(2,1)S(1)} %pad_maximum_fusion.2), channel_id=1, source_target_pairs={{0,16},{4,20},{8,24},{12,28},{16,0},{20,4},{24,8},{28,12},{1,17},{... | collective-permute-start | bytes 589832 | tf_op jit(solution)/shard_map/ppermute | solution.py:53
  66.3 7.3 %collective-permute-start.22 = (f16[4,192,128]{2,1,0:T(8,128)(2,1)S(1)}, f16[4,192,128]{2,1,0:T(8,128)(2,1)S(1)}, u32[]{:S(2)}, u32[]{:S(2)}) collective-permute-start(f16[4,192,128]{2,1,0:T(8,128)(2,1)S(1)} %pad_maximum_fusion.2), channel_id=1, source_target_pairs={{0,24},{4,28},{8,16},{12,20},{16,8},{20,12},{24,0},{28,4},{1,25},{... | collective-permute-start | bytes 589832 | tf_op jit(solution)/shard_map/ppermute | solution.py:53
  73.6 4.6 %collective-permute-start.23 = (f16[392,128]{1,0:T(8,128)(2,1)S(1)}, f16[392,128]{1,0:T(8,128)(2,1)S(1)}, u32[]{:S(2)}, u32[]{:S(2)}) collective-permute-start(f16[392,128]{1,0:T(8,128)(2,1)S(1)} %pad_maximum_fusion.7), channel_id=1, source_target_pairs={{0,8},{4,12},{8,0},{12,4},{16,24},{20,28},{24,16},{28,20},{1,9},{5... | collective-permute-start | bytes 301064 | tf_op jit(solution)/shard_map/ppermute | solution.py:53
  75.0 4.6 %collective-permute-start.24 = (f16[392,128]{1,0:T(8,128)(2,1)S(1)}, f16[392,128]{1,0:T(8,128)(2,1)S(1)}, u32[]{:S(2)}, u32[]{:S(2)}) collective-permute-start(f16[392,128]{1,0:T(8,128)(2,1)S(1)} %pad_maximum_fusion.7), channel_id=1, source_target_pairs={{0,16},{4,20},{8,24},{12,28},{16,0},{20,4},{24,8},{28,12},{1,17},{... | collective-permute-start | bytes 301064 | tf_op jit(solution)/shard_map/ppermute | solution.py:53
  75.2 5.5 %collective-permute-start.25 = (f16[392,128]{1,0:T(8,128)(2,1)S(1)}, f16[392,128]{1,0:T(8,128)(2,1)S(1)}, u32[]{:S(2)}, u32[]{:S(2)}) collective-permute-start(f16[392,128]{1,0:T(8,128)(2,1)S(1)} %pad_maximum_fusion.7), channel_id=1, source_target_pairs={{0,24},{4,28},{8,16},{12,20},{16,8},{20,12},{24,0},{28,4},{1,25},{... | collective-permute-start | bytes 301064 | tf_op jit(solution)/shard_map/ppermute | solution.py:53
  77.1 4.0 %collective-permute-start.27 = (f16[4,192,128]{2,1,0:T(8,128)(2,1)S(1)}, f16[4,192,128]{2,1,0:T(8,128)(2,1)S(1)}, u32[]{:S(2)}, u32[]{:S(2)}) collective-permute-start(f16[4,192,128]{2,1,0:T(8,128)(2,1)S(1)} %pad_maximum_fusion.2), channel_id=1, source_target_pairs={{0,4},{4,0},{8,12},{12,8},{16,20},{20,16},{24,28},{28,24},{1,5},{5... | collective-permute-start | bytes 589832 | tf_op jit(solution)/shard_map/ppermute | solution.py:53
  77.2 3.9 %collective-permute-start.28 = (f16[4,192,128]{2,1,0:T(8,128)(2,1)S(1)}, f16[4,192,128]{2,1,0:T(8,128)(2,1)S(1)}, u32[]{:S(2)}, u32[]{:S(2)}) collective-permute-start(f16[4,192,128]{2,1,0:T(8,128)(2,1)S(1)} %collective-permute-done.20), channel_id=1, source_target_pairs={{0,4},{4,0},{8,12},{12,8},{16,20},{20,16},{24,28},{28,24},{1,5},{5... | collective-permute-start | bytes 589832 | tf_op jit(solution)/shard_map/ppermute | solution.py:53
  78.2 2.9 %collective-permute-start.29 = (f16[4,192,128]{2,1,0:T(8,128)(2,1)S(1)}, f16[4,192,128]{2,1,0:T(8,128)(2,1)S(1)}, u32[]{:S(2)}, u32[]{:S(2)}) collective-permute-start(f16[4,192,128]{2,1,0:T(8,128)(2,1)S(1)} %collective-permute-done.21), channel_id=1, source_target_pairs={{0,4},{4,0},{8,12},{12,8},{16,20},{20,16},{24,28},{28,24},{1,5},{5... | collective-permute-start | bytes 589832 | tf_op jit(solution)/shard_map/ppermute | solution.py:53
  79.6 1.6 %collective-permute-start.30 = (f16[4,192,128]{2,1,0:T(8,128)(2,1)S(1)}, f16[4,192,128]{2,1,0:T(8,128)(2,1)S(1)}, u32[]{:S(2)}, u32[]{:S(2)}) collective-permute-start(f16[4,192,128]{2,1,0:T(8,128)(2,1)S(1)} %collective-permute-done.22), channel_id=1, source_target_pairs={{0,4},{4,0},{8,12},{12,8},{16,20},{20,16},{24,28},{28,24},{1,5},{5... | collective-permute-start | bytes 589832 | tf_op jit(solution)/shard_map/ppermute | solution.py:53
  80.9 1.9 %collective-permute-start.26 = (f16[4,392,128]{2,1,0:T(8,128)(2,1)S(1)}, f16[4,392,128]{2,1,0:T(8,128)(2,1)S(1)}, u32[]{:S(2)}, u32[]{:S(2)}) collective-permute-start(f16[4,392,128]{2,1,0:T(8,128)(2,1)S(1)} %pad_maximum_fusion.1), channel_id=1, source_target_pairs={{0,4},{4,0},{8,12},{12,8},{16,20},{20,16},{24,28},{28,24},{1,5},{5... | collective-permute-start | bytes 1204232 | tf_op jit(solution)/shard_map/ppermute | solution.py:53

commit v7 on v6

--- a/solution.py
+++ b/solution.py
@@ -282,16 +282,17 @@
     def place(k, carry):
         other, offset = k // (devices // 2), lax.rem(k, devices // 2)
         owner = 2 * lax.bitwise_xor(chip, offset) + lax.bitwise_xor(core, other)
+        power = cross[k, share * LANES :, :]
         for j, inner in enumerate(spans(share, LANES)):
             at = 2 * (owner * share + j)
             row = pl.ds(pl.multiple_of(table[at] * LANES, LANES), LANES)
             column = pl.ds(pl.multiple_of(table[at + 1] * LANES, LANES), LANES)
-            tile = cross[k, inner, :] * factor
+            tile = unscale(cross[k, inner, :], power) * factor
             pair[0][row, column], pair[1][row, column] = split(tile)
             pair[0][column, row], pair[1][column, row] = split(tile.T)
         return carry
 
-    lax.fori_loop(0, devices, place, 0)
+    lax.fori_loop(0, devices, place, 0, unroll=True)
     for group in range(n_batch):
         for at, (i, j) in zip(spans(len(own_tiles(per_basis)), LANES), own_tiles(per_basis)):
             rows, columns = (slice((group * per_basis + k) * LANES, (group * per_basis + k + 1) * LANES) for k in (i, j))
@@ -319,7 +320,7 @@
             target[0, :, at], target[1, :, at] = split(after)
             return carry
 
-        lax.fori_loop(0, columns // WIDE, chunk, 0)
+        lax.fori_loop(0, columns // WIDE, chunk, 0, unroll=True)
 
     def turn_of(step):
         return lax.rem(step + REPEAT - 1, REPEAT)
@@ -463,7 +464,7 @@
 
     cross = spread_copy(total, "rows", other_chips)
     cross = jnp.concatenate([cross, swap(cross, "rows", 1)])
-    cross = jax.vmap(decode)(cross)
+    cross = cross.astype(f32)
     (modes,) = call(
         solve_kernel,
         [((sub_rows, size), bf16)],

time: 112 us -> 111 us (level)
  no operation moved by 1% of the time
where the time goes in v7:
time: 111 us
  waiting for transfers between devices  37.1 us (33%)
  Pallas kernels  34.1 us (31%)
  starting transfers between devices  33.7 us (30%)
  other arithmetic  2.71 us (2%)
  local copies, waits for them, and re-layouts  2.52 us (2%)
    ppermute x31, waiting for transfers between devices, swap(): return lax.ppermute(value, axis, [(i, i ^ offset) for i in range(size)])  37.1 us
    pallas_call x4, Pallas kernels, call(): pl.pallas_call(body, out_shape=[jax.ShapeDtypeStruct(shape, dtype) for sh...  34.1 us
    ppermute x31, starting transfers between devices, swap(): return lax.ppermute(value, axis, [(i, i ^ offset) for i in range(size)])  33.7 us
  transfers between devices with their start and end apart: 31, of which 13 were waited for; matrix products, arithmetic and copies ran while one was open for 2% of the time, Pallas kernels for 2%

profile of v7, /device:TPU:0, one launch (start us, length us, event | category | flops | bytes accessed | tf_op | source)
XLA Modules:
  0.0 110.7 jit_solution(11177873044072818636)
XLA Ops:
  0.0 1.6 %constant_dynamic-slice_fusion = (bf16[768,256]{1,0:T(8,128)(2,1)S(1)}, bf16[768,256]{1,0:T(8,128)(2,1)S(1)}, bf16[768,256]{1,0:T(8,128)(2,1)S(1)}, bf16[768,256]{1,0:T(8,128)(2,1)S(1)}) fusion(bf16[3072,256]{1,0:T(8,128)(2,1)} %refs_0_.1, s32[]{:T(128)S(6)} %select_n.28, s32[]{:T(128)S(6)} %select_n.26, s32[]{:T(128)S(6)} %select_n.25, s32[]{:T(128)S(6)} %select_n.27), kind=kLoop, calls=%fused_computation.99 | loop fusion | bytes 3145744 | tf_op jit(solution)/shard_map/dynamic_slice | solution.py:422
  1.6 0.5 collective-permute-start
  2.1 4.7 %collective-permute-start.7 = (bf16[768,256]{1,0:T(8,128)(2,1)S(1)}, bf16[768,256]{1,0:T(8,128)(2,1)S(1)}, u32[]{:S(2)}, u32[]{:S(2)}) collective-permute-start(bf16[768,256]{1,0:T(8,128)(2,1)S(1)} %get-tuple-element.43), channel_id=1, source_target_pairs={{0,3},{1,2},{2,1},{3,0},{4,7},{5,6},{6,5},{7,4},{8,11},{9,10},{10,... | collective-permute-start | bytes 1179656 | tf_op jit(solution)/shard_map/ppermute | solution.py:53
  6.8 0.6 collective-permute-start.6
  7.4 0.0 collective-permute-done.refs_1_.refs_8_
  7.4 0.8 shard_map.37
  8.2 0.1 collective-permute-start.1
  8.3 1.4 %collective-permute-done.1 = f32[384,128]{1,0:T(8,128)S(1)} collective-permute-done((f32[384,128]{1,0:T(8,128)S(1)}, f32[384,128]{1,0:T(8,128)S(1)}, u32[]{:S(2)}, u32[]{:S(2)}) %collective-permute-start.1) | collective-permute-done | bytes 196640 | tf_op jit(solution)/shard_map/ppermute | solution.py:53
  9.8 1.7 %collective-permute-start.2 = (f32[384,128]{1,0:T(8,128)S(1)}, f32[384,128]{1,0:T(8,128)S(1)}, u32[]{:S(2)}, u32[]{:S(2)}) collective-permute-start(f32[384,128]{1,0:T(8,128)S(1)} %add.73), channel_id=1, source_target_pairs={{0,8},{4,12},{8,0},{12,4},{16,24},{20,28},{24,16},{28,20},{1,9},{5... | collective-permute-start | bytes 589832 | tf_op jit(solution)/shard_map/ppermute | solution.py:53
  11.5 1.5 %collective-permute-start.3 = (f32[384,128]{1,0:T(8,128)S(1)}, f32[384,128]{1,0:T(8,128)}, u32[]{:S(2)}, u32[]{:S(2)}) collective-permute-start(f32[384,128]{1,0:T(8,128)S(1)} %add.73), channel_id=1, source_target_pairs={{0,16},{4,20},{8,24},{12,28},{16,0},{20,4},{24,8},{28,12},{1,17},{... | collective-permute-start | bytes 589832 | tf_op jit(solution)/shard_map/ppermute | solution.py:53
  13.0 3.8 %collective-permute-done.7.refs_7_ = bf16[768,256]{1,0:T(8,128)(2,1)S(1)} collective-permute-done((bf16[768,256]{1,0:T(8,128)(2,1)S(1)}, bf16[768,256]{1,0:T(8,128)(2,1)S(1)}, u32[]{:S(2)}, u32[]{:S(2)}) %collective-permute-start.7) | collective-permute-done | bytes 393248 | tf_op jit(solution)/shard_map/ppermute | solution.py:53
  16.8 2.6 %collective-permute-start.4 = (f32[384,128]{1,0:T(8,128)S(1)}, f32[384,128]{1,0:T(8,128)}, u32[]{:S(2)}, u32[]{:S(2)}) collective-permute-start(f32[384,128]{1,0:T(8,128)S(1)} %add.73), channel_id=1, source_target_pairs={{0,24},{4,28},{8,16},{12,20},{16,8},{20,12},{24,0},{28,4},{1,25},{... | collective-permute-start | bytes 589832 | tf_op jit(solution)/shard_map/ppermute | solution.py:53
  19.4 6.6 %collective-permute-done.5.refs_5_ = bf16[768,256]{1,0:T(8,128)(2,1)S(1)} collective-permute-done((bf16[768,256]{1,0:T(8,128)(2,1)S(1)}, bf16[768,256]{1,0:T(8,128)(2,1)S(1)}, u32[]{:S(2)}, u32[]{:S(2)}) %collective-permute-start.5) | collective-permute-done | bytes 393248 | tf_op jit(solution)/shard_map/ppermute | solution.py:53
  26.0 0.0 collective-permute-start.10
  26.1 14.9 %collective-permute-done.6.refs_6_ = bf16[768,256]{1,0:T(8,128)(2,1)S(1)} collective-permute-done((bf16[768,256]{1,0:T(8,128)(2,1)S(1)}, bf16[768,256]{1,0:T(8,128)(2,1)S(1)}, u32[]{:S(2)}, u32[]{:S(2)}) %collective-permute-start.6) | collective-permute-done | bytes 393248 | tf_op jit(solution)/shard_map/ppermute | solution.py:53
  40.9 0.0 collective-permute-start.8
  40.9 0.0 collective-permute-done.2
  40.9 0.7 copy-done.3
  41.6 0.5 collective-permute-start.9
  42.1 0.1 pad_add_fusion.refs_0_
  42.2 0.0 collective-permute-done.3
  42.2 0.0 collective-permute-done.4
  42.2 1.2 %add_add_fusion.refs_3_ = f32[384,128]{1,0:T(8,128)S(1)} fusion(f32[384,128]{1,0:T(8,128)} %collective-permute-done.4, f32[384,128]{1,0:T(8,128)} %collective-permute-done.3, f32[384,128]{1,0:T(8,128)S(1)} %add.73, f32[384,128]{1,0:T(8,128)} %copy-done.3), kind=kLoop, calls=%fused_computation.28 | loop fusion | flops 147456 | bytes 983040 | tf_op jit(solution)/shard_map/add | solution.py:432
  43.4 0.0 collective-permute-done.10.refs_11_
  43.4 0.0 collective-permute-done.8.refs_9_
  43.4 0.2 collective-permute-done.9.refs_10_
  43.6 4.1 %shard_map.38 = (bf16[768,1024]{1,0:T(8,128)(2,1)S(1)}, f32[192,128]{1,0:T(8,128)S(1)}, f32[392,128]{1,0:T(8,128)S(1)}, f32[392,128]{1,0:T(8,128)S(1)}, f32[392,128]{1,0:T(8,128)S(1)}, /*index=5*/f32[392,128]{1,0:T(8,128)S(1)}) custom-call(s32[3]{0:T(128)S(1)} %pad_add_fusion.refs_0_, s32[48]{0:T(128)S(1)} %copy-done.2, f32[256,512]{1,0:T(8,128)S(1)} %copy-done.1, ...), custom_call_target="tpu_custom_call" | custom-call | flops 603979776 | bytes 6291456 | tf_op jit(solution)/shard_map/pallas_call | solution.py:410
  47.8 1.6 %collective-permute-start.11 = (f16[392,128]{1,0:T(8,128)(2,1)S(1)}, f16[392,128]{1,0:T(8,128)(2,1)S(1)}, u32[]{:S(2)}, u32[]{:S(2)}) collective-permute-start(f16[392,128]{1,0:T(8,128)(2,1)S(1)} %pad_maximum_fusion.2), channel_id=1, source_target_pairs={{0,8},{4,12},{8,0},{12,4},{16,24},{20,28},{24,16},{28,20},{1,9},{5... | collective-permute-start | bytes 301064 | tf_op jit(solution)/shard_map/ppermute | solution.py:53
  49.5 1.6 %collective-permute-start.12 = (f16[392,128]{1,0:T(8,128)(2,1)S(1)}, f16[392,128]{1,0:T(8,128)(2,1)S(1)}, u32[]{:S(2)}, u32[]{:S(2)}) collective-permute-start(f16[392,128]{1,0:T(8,128)(2,1)S(1)} %pad_maximum_fusion.3), channel_id=1, source_target_pairs={{0,16},{4,20},{8,24},{12,28},{16,0},{20,4},{24,8},{28,12},{1,17},{... | collective-permute-start | bytes 301064 | tf_op jit(solution)/shard_map/ppermute | solution.py:53
  51.2 0.5 collective-permute-start.13
  51.8 1.2 %collective-permute-done.11 = f16[392,128]{1,0:T(8,128)(2,1)S(1)} collective-permute-done((f16[392,128]{1,0:T(8,128)(2,1)S(1)}, f16[392,128]{1,0:T(8,128)(2,1)S(1)}, u32[]{:S(2)}, u32[]{:S(2)}) %collective-permute-start.11) | collective-permute-done | bytes 100384 | tf_op jit(solution)/shard_map/ppermute | solution.py:53
  53.1 0.1 collective-permute-start.17
  53.2 3.1 %collective-permute-start.18 = (f16[192,128]{1,0:T(8,128)(2,1)S(1)}, f16[192,128]{1,0:T(8,128)(2,1)S(1)}, u32[]{:S(2)}, u32[]{:S(2)}) collective-permute-start(f16[192,128]{1,0:T(8,128)(2,1)S(1)} %get-tuple-element.76), channel_id=1, source_target_pairs={{0,2},{1,3},{2,0},{3,1},{4,6},{5,7},{6,4},{7,5},{8,10},{9,11},{10,... | collective-permute-start | bytes 147464 | tf_op jit(solution)/shard_map/ppermute | solution.py:53
  56.2 1.3 %collective-permute-start.19 = (f16[192,128]{1,0:T(8,128)(2,1)S(1)}, f16[192,128]{1,0:T(8,128)(2,1)S(1)}, u32[]{:S(2)}, u32[]{:S(2)}) collective-permute-start(f16[192,128]{1,0:T(8,128)(2,1)S(1)} %get-tuple-element.76), channel_id=1, source_target_pairs={{0,3},{1,2},{2,1},{3,0},{4,7},{5,6},{6,5},{7,4},{8,11},{9,10},{10,... | collective-permute-start | bytes 147464 | tf_op jit(solution)/shard_map/ppermute | solution.py:53
  57.6 0.0 collective-permute-done.12
  57.6 0.0 collective-permute-done.13
  57.8 0.1 fusion.1
  57.9 0.1 collective-permute-start.14
  58.0 3.1 %collective-permute-start.15 = (f16[392,128]{1,0:T(8,128)(2,1)S(1)}, f16[392,128]{1,0:T(8,128)(2,1)S(1)}, u32[]{:S(2)}, u32[]{:S(2)}) collective-permute-start(f16[392,128]{1,0:T(8,128)(2,1)S(1)} %get-tuple-element.70), channel_id=1, source_target_pairs={{0,2},{1,3},{2,0},{3,1},{4,6},{5,7},{6,4},{7,5},{8,10},{9,11},{10,... | collective-permute-start | bytes 301064 | tf_op jit(solution)/shard_map/ppermute | solution.py:53
  61.1 1.4 %collective-permute-start.16 = (f16[392,128]{1,0:T(8,128)(2,1)S(1)}, f16[392,128]{1,0:T(8,128)(2,1)S(1)}, u32[]{:S(2)}, u32[]{:S(2)}) collective-permute-start(f16[392,128]{1,0:T(8,128)(2,1)S(1)} %get-tuple-element.70), channel_id=1, source_target_pairs={{0,3},{1,2},{2,1},{3,0},{4,7},{5,6},{6,5},{7,4},{8,11},{9,10},{10,... | collective-permute-start | bytes 301064 | tf_op jit(solution)/shard_map/ppermute | solution.py:53
  62.5 0.0 collective-permute-done.18
  62.5 0.3 collective-permute-done.19
  62.8 0.1 pad_maximum_fusion.1
  62.8 2.0 %collective-permute-start.20 = (f16[4,192,128]{2,1,0:T(8,128)(2,1)S(1)}, f16[4,192,128]{2,1,0:T(8,128)(2,1)S(1)}, u32[]{:S(2)}, u32[]{:S(2)}) collective-permute-start(f16[4,192,128]{2,1,0:T(8,128)(2,1)S(1)} %pad_maximum_fusion.1), channel_id=1, source_target_pairs={{0,8},{4,12},{8,0},{12,4},{16,24},{20,28},{24,16},{28,20},{1,9},{5... | collective-permute-start | bytes 589832 | tf_op jit(solution)/shard_map/ppermute | solution.py:53
  64.8 1.5 %collective-permute-start.21 = (f16[4,192,128]{2,1,0:T(8,128)(2,1)S(1)}, f16[4,192,128]{2,1,0:T(8,128)(2,1)S(1)}, u32[]{:S(2)}, u32[]{:S(2)}) collective-permute-start(f16[4,192,128]{2,1,0:T(8,128)(2,1)S(1)} %pad_maximum_fusion.1), channel_id=1, source_target_pairs={{0,16},{4,20},{8,24},{12,28},{16,0},{20,4},{24,8},{28,12},{1,17},{... | collective-permute-start | bytes 589832 | tf_op jit(solution)/shard_map/ppermute | solution.py:53
  66.3 1.1 collective-permute-start.22
  67.5 1.0 collective-permute-done.15
  68.8 1.0 collective-permute-done.20
  69.8 3.8 %collective-permute-done.21 = f16[4,192,128]{2,1,0:T(8,128)(2,1)S(1)} collective-permute-done((f16[4,192,128]{2,1,0:T(8,128)(2,1)S(1)}, f16[4,192,128]{2,1,0:T(8,128)(2,1)S(1)}, u32[]{:S(2)}, u32[]{:S(2)}) %collective-permute-start.21) | collective-permute-done | bytes 196640 | tf_op jit(solution)/shard_map/ppermute | solution.py:53
  73.6 1.4 %collective-permute-start.23 = (f16[392,128]{1,0:T(8,128)(2,1)S(1)}, f16[392,128]{1,0:T(8,128)(2,1)S(1)}, u32[]{:S(2)}, u32[]{:S(2)}) collective-permute-start(f16[392,128]{1,0:T(8,128)(2,1)S(1)} %pad_maximum_fusion.6), channel_id=1, source_target_pairs={{0,8},{4,12},{8,0},{12,4},{16,24},{20,28},{24,16},{28,20},{1,9},{5... | collective-permute-start | bytes 301064 | tf_op jit(solution)/shard_map/ppermute | solution.py:53
  75.0 0.2 collective-permute-start.24
  75.2 1.9 %collective-permute-start.25 = (f16[392,128]{1,0:T(8,128)(2,1)S(1)}, f16[392,128]{1,0:T(8,128)(2,1)S(1)}, u32[]{:S(2)}, u32[]{:S(2)}) collective-permute-start(f16[392,128]{1,0:T(8,128)(2,1)S(1)} %pad_maximum_fusion.6), channel_id=1, source_target_pairs={{0,24},{4,28},{8,16},{12,20},{16,8},{20,12},{24,0},{28,4},{1,25},{... | collective-permute-start | bytes 301064 | tf_op jit(solution)/shard_map/ppermute | solution.py:53
  77.1 0.1 collective-permute-start.27
  77.2 0.6 collective-permute-start.28
  77.9 0.3 collective-permute-done.23
  78.2 1.4 %collective-permute-done.24 = f16[392,128]{1,0:T(8,128)(2,1)S(1)} collective-permute-done((f16[392,128]{1,0:T(8,128)(2,1)S(1)}, f16[392,128]{1,0:T(8,128)(2,1)S(1)}, u32[]{:S(2)}, u32[]{:S(2)}) %collective-permute-start.24) | collective-permute-done | bytes 100384 | tf_op jit(solution)/shard_map/ppermute | solution.py:53
  79.6 1.1 %collective-permute-done.25 = f16[392,128]{1,0:T(8,128)(2,1)S(1)} collective-permute-done((f16[392,128]{1,0:T(8,128)(2,1)S(1)}, f16[392,128]{1,0:T(8,128)(2,1)S(1)}, u32[]{:S(2)}, u32[]{:S(2)}) %collective-permute-start.25) | collective-permute-done | bytes 100384 | tf_op jit(solution)/shard_map/ppermute | solution.py:53
  80.7 0.1 pad_maximum_fusion
  80.9 0.1 collective-permute-start.26
  81.2 0.0 collective-permute-done.29
  81.3 1.5 %shard_map.39 = (bf16[512,1024]{1,0:T(8,128)(2,1)S(1)}, bf16[512,1024]{1,0:T(8,128)(2,1)S(1)}, f32[4,384,128]{2,1,0:T(8,128)S(1)}) custom-call(s32[3]{0:T(128)S(1)} %pad_add_fusion.refs_0_, f32[4,192,128]{2,1,0:T(8,128)S(1)} %convert_element_type.68.refs_1_, f32[4,192,128]{2,1,0:T(8,128)S(1)} %convert_element_type.69.refs_2_, ...), custom_call_target="tpu_custom_call" | custom-call | bytes 8388608 | tf_op jit(solution)/shard_map/pallas_call | solution.py:410
  82.8 0.1 constant_dynamic-update-slice_fusion
  82.9 0.1 convert_element_type.67.refs_2_
  83.0 27.6 %shard_map.40 = bf16[768,512]{1,0:T(8,128)(2,1)} custom-call(s32[3]{0:T(128)S(1)} %pad_add_fusion.refs_0_, s32[48]{0:T(128)S(1)} %copy-done.2, f32[8,392,128]{2,1,0:T(8,128)S(1)} %convert_element_type.67.refs_2_, f32[4,384,128]{2,1,0:T(8,128)S(1)} %get-tuple-element.33.refs_3_, bf16[512,1024]{1,0:T(8,128)(2,1)S(1)} %get-tuple-element.34.refs_4_, ...), custom_call_target="tpu_custom_call" | custom-call | flops 10000000000 | bytes 10485760 | tf_op jit(solution)/shard_map/pallas_call | solution.py:410
  (77 shorter events, 1.3 us)
Async XLA Ops:
  0.0 7.4 %copy-start = (bf16[3072,256]{1,0:T(8,128)(2,1)S(1)}, bf16[3072,256]{1,0:T(8,128)(2,1)}, u32[]{:S(2)}) copy-start(bf16[3072,256]{1,0:T(8,128)(2,1)} %refs_0_.1) | copy-start | bytes 4718596
  1.6 5.8 %collective-permute-start = (bf16[768,256]{1,0:T(8,128)(2,1)S(1)}, bf16[768,256]{1,0:T(8,128)(2,1)S(1)}, u32[]{:S(2)}, u32[]{:S(2)}) collective-permute-start(bf16[768,256]{1,0:T(8,128)(2,1)S(1)} %get-tuple-element.45.refs_4_), channel_id=1, source_target_pairs={{0,4},{4,0},{8,12},{12,8},{16,20},{20,16},{24,28},{28,24},{1,5},{5... | collective-permute-start | bytes 1179656 | tf_op jit(solution)/shard_map/ppermute | solution.py:53
  2.1 14.7 %collective-permute-start.7 = (bf16[768,256]{1,0:T(8,128)(2,1)S(1)}, bf16[768,256]{1,0:T(8,128)(2,1)S(1)}, u32[]{:S(2)}, u32[]{:S(2)}) collective-permute-start(bf16[768,256]{1,0:T(8,128)(2,1)S(1)} %get-tuple-element.43), channel_id=1, source_target_pairs={{0,3},{1,2},{2,1},{3,0},{4,7},{5,6},{6,5},{7,4},{8,11},{9,10},{10,... | collective-permute-start | bytes 1179656 | tf_op jit(solution)/shard_map/ppermute | solution.py:53
  6.8 19.3 %collective-permute-start.5 = (bf16[768,256]{1,0:T(8,128)(2,1)S(1)}, bf16[768,256]{1,0:T(8,128)(2,1)S(1)}, u32[]{:S(2)}, u32[]{:S(2)}) collective-permute-start(bf16[768,256]{1,0:T(8,128)(2,1)S(1)} %get-tuple-element.44), channel_id=1, source_target_pairs={{0,1},{1,0},{2,3},{3,2},{4,5},{5,4},{6,7},{7,6},{8,9},{9,8},{10,11... | collective-permute-start | bytes 1179656 | tf_op jit(solution)/shard_map/ppermute | solution.py:53
  6.8 36.8 %copy-start.1 = (f32[256,512]{1,0:T(8,128)S(1)}, f32[256,512]{1,0:T(8,128)}, u32[]{:S(2)}) copy-start(f32[256,512]{1,0:T(8,128)} %refs_2_.1) | copy-start | bytes 1572868
  6.8 36.8 %copy-start.2 = (s32[48]{0:T(128)S(1)}, s32[48]{0:T(128)}, u32[]{:S(2)}) copy-start(s32[48]{0:T(128)} %constant.55.clone.refs_1_) | copy-start | bytes 580
  6.8 34.1 %collective-permute-start.6 = (bf16[768,256]{1,0:T(8,128)(2,1)S(1)}, bf16[768,256]{1,0:T(8,128)(2,1)S(1)}, u32[]{:S(2)}, u32[]{:S(2)}) collective-permute-start(bf16[768,256]{1,0:T(8,128)(2,1)S(1)} %get-tuple-element.46), channel_id=1, source_target_pairs={{0,2},{1,3},{2,0},{3,1},{4,6},{5,7},{6,4},{7,5},{8,10},{9,11},{10,... | collective-permute-start | bytes 1179656 | tf_op jit(solution)/shard_map/ppermute | solution.py:53
  8.2 1.5 %collective-permute-start.1 = (f32[384,128]{1,0:T(8,128)S(1)}, f32[384,128]{1,0:T(8,128)S(1)}, u32[]{:S(2)}, u32[]{:S(2)}) collective-permute-start(f32[384,128]{1,0:T(8,128)S(1)} %shard_map.37), channel_id=1, source_target_pairs={{0,4},{4,0},{8,12},{12,8},{16,20},{20,16},{24,28},{28,24},{1,5},{5... | collective-permute-start | bytes 589832 | tf_op jit(solution)/shard_map/ppermute | solution.py:53
  9.8 31.2 %collective-permute-start.2 = (f32[384,128]{1,0:T(8,128)S(1)}, f32[384,128]{1,0:T(8,128)S(1)}, u32[]{:S(2)}, u32[]{:S(2)}) collective-permute-start(f32[384,128]{1,0:T(8,128)S(1)} %add.73), channel_id=1, source_target_pairs={{0,8},{4,12},{8,0},{12,4},{16,24},{20,28},{24,16},{28,20},{1,9},{5... | collective-permute-start | bytes 589832 | tf_op jit(solution)/shard_map/ppermute | solution.py:53
  11.5 30.7 %collective-permute-start.3 = (f32[384,128]{1,0:T(8,128)S(1)}, f32[384,128]{1,0:T(8,128)}, u32[]{:S(2)}, u32[]{:S(2)}) collective-permute-start(f32[384,128]{1,0:T(8,128)S(1)} %add.73), channel_id=1, source_target_pairs={{0,16},{4,20},{8,24},{12,28},{16,0},{20,4},{24,8},{28,12},{1,17},{... | collective-permute-start | bytes 589832 | tf_op jit(solution)/shard_map/ppermute | solution.py:53
  16.8 25.4 %collective-permute-start.4 = (f32[384,128]{1,0:T(8,128)S(1)}, f32[384,128]{1,0:T(8,128)}, u32[]{:S(2)}, u32[]{:S(2)}) collective-permute-start(f32[384,128]{1,0:T(8,128)S(1)} %add.73), channel_id=1, source_target_pairs={{0,24},{4,28},{8,16},{12,20},{16,8},{20,12},{24,0},{28,4},{1,25},{... | collective-permute-start | bytes 589832 | tf_op jit(solution)/shard_map/ppermute | solution.py:53
  26.0 17.3 %collective-permute-start.10 = (bf16[768,256]{1,0:T(8,128)(2,1)S(1)}, bf16[768,256]{1,0:T(8,128)(2,1)S(1)}, u32[]{:S(2)}, u32[]{:S(2)}) collective-permute-start(bf16[768,256]{1,0:T(8,128)(2,1)S(1)} %collective-permute-done.7.refs_7_), channel_id=1, source_target_pairs={{0,4},{4,0},{8,12},{12,8},{16,20},{20,16},{24,28},{28,24},{1,5},{5... | collective-permute-start | bytes 1179656 | tf_op jit(solution)/shard_map/ppermute | solution.py:53
  40.9 2.5 %collective-permute-start.8 = (bf16[768,256]{1,0:T(8,128)(2,1)S(1)}, bf16[768,256]{1,0:T(8,128)(2,1)S(1)}, u32[]{:S(2)}, u32[]{:S(2)}) collective-permute-start(bf16[768,256]{1,0:T(8,128)(2,1)S(1)} %collective-permute-done.5.refs_5_), channel_id=1, source_target_pairs={{0,4},{4,0},{8,12},{12,8},{16,20},{20,16},{24,28},{28,24},{1,5},{5... | collective-permute-start | bytes 1179656 | tf_op jit(solution)/shard_map/ppermute | solution.py:53
  40.9 0.7 copy-start.3
  41.6 2.0 %collective-permute-start.9 = (bf16[768,256]{1,0:T(8,128)(2,1)S(1)}, bf16[768,256]{1,0:T(8,128)(2,1)}, u32[]{:S(2)}, u32[]{:S(2)}) collective-permute-start(bf16[768,256]{1,0:T(8,128)(2,1)S(1)} %collective-permute-done.6.refs_6_), channel_id=1, source_target_pairs={{0,4},{4,0},{8,12},{12,8},{16,20},{20,16},{24,28},{28,24},{1,5},{5... | collective-permute-start | bytes 1179656 | tf_op jit(solution)/shard_map/ppermute | solution.py:53
  47.8 5.2 %collective-permute-start.11 = (f16[392,128]{1,0:T(8,128)(2,1)S(1)}, f16[392,128]{1,0:T(8,128)(2,1)S(1)}, u32[]{:S(2)}, u32[]{:S(2)}) collective-permute-start(f16[392,128]{1,0:T(8,128)(2,1)S(1)} %pad_maximum_fusion.2), channel_id=1, source_target_pairs={{0,8},{4,12},{8,0},{12,4},{16,24},{20,28},{24,16},{28,20},{1,9},{5... | collective-permute-start | bytes 301064 | tf_op jit(solution)/shard_map/ppermute | solution.py:53
  49.5 8.0 %collective-permute-start.12 = (f16[392,128]{1,0:T(8,128)(2,1)S(1)}, f16[392,128]{1,0:T(8,128)(2,1)S(1)}, u32[]{:S(2)}, u32[]{:S(2)}) collective-permute-start(f16[392,128]{1,0:T(8,128)(2,1)S(1)} %pad_maximum_fusion.3), channel_id=1, source_target_pairs={{0,16},{4,20},{8,24},{12,28},{16,0},{20,4},{24,8},{28,12},{1,17},{... | collective-permute-start | bytes 301064 | tf_op jit(solution)/shard_map/ppermute | solution.py:53
  51.2 6.4 %collective-permute-start.13 = (f16[392,128]{1,0:T(8,128)(2,1)S(1)}, f16[392,128]{1,0:T(8,128)(2,1)S(1)}, u32[]{:S(2)}, u32[]{:S(2)}) collective-permute-start(f16[392,128]{1,0:T(8,128)(2,1)S(1)} %pad_maximum_fusion.4), channel_id=1, source_target_pairs={{0,24},{4,28},{8,16},{12,20},{16,8},{20,12},{24,0},{28,4},{1,25},{... | collective-permute-start | bytes 301064 | tf_op jit(solution)/shard_map/ppermute | solution.py:53
  53.1 8.0 %collective-permute-start.17 = (f16[192,128]{1,0:T(8,128)(2,1)S(1)}, f16[192,128]{1,0:T(8,128)(2,1)S(1)}, u32[]{:S(2)}, u32[]{:S(2)}) collective-permute-start(f16[192,128]{1,0:T(8,128)(2,1)S(1)} %get-tuple-element.76), channel_id=1, source_target_pairs={{0,1},{1,0},{2,3},{3,2},{4,5},{5,4},{6,7},{7,6},{8,9},{9,8},{10,11... | collective-permute-start | bytes 147464 | tf_op jit(solution)/shard_map/ppermute | solution.py:53
  53.2 9.3 %collective-permute-start.18 = (f16[192,128]{1,0:T(8,128)(2,1)S(1)}, f16[192,128]{1,0:T(8,128)(2,1)S(1)}, u32[]{:S(2)}, u32[]{:S(2)}) collective-permute-start(f16[192,128]{1,0:T(8,128)(2,1)S(1)} %get-tuple-element.76), channel_id=1, source_target_pairs={{0,2},{1,3},{2,0},{3,1},{4,6},{5,7},{6,4},{7,5},{8,10},{9,11},{10,... | collective-permute-start | bytes 147464 | tf_op jit(solution)/shard_map/ppermute | solution.py:53
  56.2 6.5 %collective-permute-start.19 = (f16[192,128]{1,0:T(8,128)(2,1)S(1)}, f16[192,128]{1,0:T(8,128)(2,1)S(1)}, u32[]{:S(2)}, u32[]{:S(2)}) collective-permute-start(f16[192,128]{1,0:T(8,128)(2,1)S(1)} %get-tuple-element.76), channel_id=1, source_target_pairs={{0,3},{1,2},{2,1},{3,0},{4,7},{5,6},{6,5},{7,4},{8,11},{9,10},{10,... | collective-permute-start | bytes 147464 | tf_op jit(solution)/shard_map/ppermute | solution.py:53
  57.9 8.4 %collective-permute-start.14 = (f16[392,128]{1,0:T(8,128)(2,1)S(1)}, f16[392,128]{1,0:T(8,128)(2,1)S(1)}, u32[]{:S(2)}, u32[]{:S(2)}) collective-permute-start(f16[392,128]{1,0:T(8,128)(2,1)S(1)} %get-tuple-element.70), channel_id=1, source_target_pairs={{0,1},{1,0},{2,3},{3,2},{4,5},{5,4},{6,7},{7,6},{8,9},{9,8},{10,11... | collective-permute-start | bytes 301064 | tf_op jit(solution)/shard_map/ppermute | solution.py:53
  58.0 10.5 %collective-permute-start.15 = (f16[392,128]{1,0:T(8,128)(2,1)S(1)}, f16[392,128]{1,0:T(8,128)(2,1)S(1)}, u32[]{:S(2)}, u32[]{:S(2)}) collective-permute-start(f16[392,128]{1,0:T(8,128)(2,1)S(1)} %get-tuple-element.70), channel_id=1, source_target_pairs={{0,2},{1,3},{2,0},{3,1},{4,6},{5,7},{6,4},{7,5},{8,10},{9,11},{10,... | collective-permute-start | bytes 301064 | tf_op jit(solution)/shard_map/ppermute | solution.py:53
  61.1 7.4 %collective-permute-start.16 = (f16[392,128]{1,0:T(8,128)(2,1)S(1)}, f16[392,128]{1,0:T(8,128)(2,1)S(1)}, u32[]{:S(2)}, u32[]{:S(2)}) collective-permute-start(f16[392,128]{1,0:T(8,128)(2,1)S(1)} %get-tuple-element.70), channel_id=1, source_target_pairs={{0,3},{1,2},{2,1},{3,0},{4,7},{5,6},{6,5},{7,4},{8,11},{9,10},{10,... | collective-permute-start | bytes 301064 | tf_op jit(solution)/shard_map/ppermute | solution.py:53
  62.8 7.0 %collective-permute-start.20 = (f16[4,192,128]{2,1,0:T(8,128)(2,1)S(1)}, f16[4,192,128]{2,1,0:T(8,128)(2,1)S(1)}, u32[]{:S(2)}, u32[]{:S(2)}) collective-permute-start(f16[4,192,128]{2,1,0:T(8,128)(2,1)S(1)} %pad_maximum_fusion.1), channel_id=1, source_target_pairs={{0,8},{4,12},{8,0},{12,4},{16,24},{20,28},{24,16},{28,20},{1,9},{5... | collective-permute-start | bytes 589832 | tf_op jit(solution)/shard_map/ppermute | solution.py:53
  64.8 8.8 %collective-permute-start.21 = (f16[4,192,128]{2,1,0:T(8,128)(2,1)S(1)}, f16[4,192,128]{2,1,0:T(8,128)(2,1)S(1)}, u32[]{:S(2)}, u32[]{:S(2)}) collective-permute-start(f16[4,192,128]{2,1,0:T(8,128)(2,1)S(1)} %pad_maximum_fusion.1), channel_id=1, source_target_pairs={{0,16},{4,20},{8,24},{12,28},{16,0},{20,4},{24,8},{28,12},{1,17},{... | collective-permute-start | bytes 589832 | tf_op jit(solution)/shard_map/ppermute | solution.py:53
  66.3 7.3 %collective-permute-start.22 = (f16[4,192,128]{2,1,0:T(8,128)(2,1)S(1)}, f16[4,192,128]{2,1,0:T(8,128)(2,1)S(1)}, u32[]{:S(2)}, u32[]{:S(2)}) collective-permute-start(f16[4,192,128]{2,1,0:T(8,128)(2,1)S(1)} %pad_maximum_fusion.1), channel_id=1, source_target_pairs={{0,24},{4,28},{8,16},{12,20},{16,8},{20,12},{24,0},{28,4},{1,25},{... | collective-permute-start | bytes 589832 | tf_op jit(solution)/shard_map/ppermute | solution.py:53
  73.6 4.6 %collective-permute-start.23 = (f16[392,128]{1,0:T(8,128)(2,1)S(1)}, f16[392,128]{1,0:T(8,128)(2,1)S(1)}, u32[]{:S(2)}, u32[]{:S(2)}) collective-permute-start(f16[392,128]{1,0:T(8,128)(2,1)S(1)} %pad_maximum_fusion.6), channel_id=1, source_target_pairs={{0,8},{4,12},{8,0},{12,4},{16,24},{20,28},{24,16},{28,20},{1,9},{5... | collective-permute-start | bytes 301064 | tf_op jit(solution)/shard_map/ppermute | solution.py:53
  75.0 4.6 %collective-permute-start.24 = (f16[392,128]{1,0:T(8,128)(2,1)S(1)}, f16[392,128]{1,0:T(8,128)(2,1)S(1)}, u32[]{:S(2)}, u32[]{:S(2)}) collective-permute-start(f16[392,128]{1,0:T(8,128)(2,1)S(1)} %pad_maximum_fusion.6), channel_id=1, source_target_pairs={{0,16},{4,20},{8,24},{12,28},{16,0},{20,4},{24,8},{28,12},{1,17},{... | collective-permute-start | bytes 301064 | tf_op jit(solution)/shard_map/ppermute | solution.py:53
  75.2 5.5 %collective-permute-start.25 = (f16[392,128]{1,0:T(8,128)(2,1)S(1)}, f16[392,128]{1,0:T(8,128)(2,1)S(1)}, u32[]{:S(2)}, u32[]{:S(2)}) collective-permute-start(f16[392,128]{1,0:T(8,128)(2,1)S(1)} %pad_maximum_fusion.6), channel_id=1, source_target_pairs={{0,24},{4,28},{8,16},{12,20},{16,8},{20,12},{24,0},{28,4},{1,25},{... | collective-permute-start | bytes 301064 | tf_op jit(solution)/shard_map/ppermute | solution.py:53
  77.1 4.0 %collective-permute-start.27 = (f16[4,192,128]{2,1,0:T(8,128)(2,1)S(1)}, f16[4,192,128]{2,1,0:T(8,128)(2,1)S(1)}, u32[]{:S(2)}, u32[]{:S(2)}) collective-permute-start(f16[4,192,128]{2,1,0:T(8,128)(2,1)S(1)} %pad_maximum_fusion.1), channel_id=1, source_target_pairs={{0,4},{4,0},{8,12},{12,8},{16,20},{20,16},{24,28},{28,24},{1,5},{5... | collective-permute-start | bytes 589832 | tf_op jit(solution)/shard_map/ppermute | solution.py:53
  77.2 3.9 %collective-permute-start.28 = (f16[4,192,128]{2,1,0:T(8,128)(2,1)S(1)}, f16[4,192,128]{2,1,0:T(8,128)(2,1)S(1)}, u32[]{:S(2)}, u32[]{:S(2)}) collective-permute-start(f16[4,192,128]{2,1,0:T(8,128)(2,1)S(1)} %collective-permute-done.20), channel_id=1, source_target_pairs={{0,4},{4,0},{8,12},{12,8},{16,20},{20,16},{24,28},{28,24},{1,5},{5... | collective-permute-start | bytes 589832 | tf_op jit(solution)/shard_map/ppermute | solution.py:53
  78.2 2.9 %collective-permute-start.29 = (f16[4,192,128]{2,1,0:T(8,128)(2,1)S(1)}, f16[4,192,128]{2,1,0:T(8,128)(2,1)S(1)}, u32[]{:S(2)}, u32[]{:S(2)}) collective-permute-start(f16[4,192,128]{2,1,0:T(8,128)(2,1)S(1)} %collective-permute-done.21), channel_id=1, source_target_pairs={{0,4},{4,0},{8,12},{12,8},{16,20},{20,16},{24,28},{28,24},{1,5},{5... | collective-permute-start | bytes 589832 | tf_op jit(solution)/shard_map/ppermute | solution.py:53
  79.6 1.6 %collective-permute-start.30 = (f16[4,192,128]{2,1,0:T(8,128)(2,1)S(1)}, f16[4,192,128]{2,1,0:T(8,128)(2,1)S(1)}, u32[]{:S(2)}, u32[]{:S(2)}) collective-permute-start(f16[4,192,128]{2,1,0:T(8,128)(2,1)S(1)} %collective-permute-done.22), channel_id=1, source_target_pairs={{0,4},{4,0},{8,12},{12,8},{16,20},{20,16},{24,28},{28,24},{1,5},{5... | collective-permute-start | bytes 589832 | tf_op jit(solution)/shard_map/ppermute | solution.py:53
  80.9 1.9 %collective-permute-start.26 = (f16[4,392,128]{2,1,0:T(8,128)(2,1)S(1)}, f16[4,392,128]{2,1,0:T(8,128)(2,1)S(1)}, u32[]{:S(2)}, u32[]{:S(2)}) collective-permute-start(f16[4,392,128]{2,1,0:T(8,128)(2,1)S(1)} %pad_maximum_fusion), channel_id=1, source_target_pairs={{0,4},{4,0},{8,12},{12,8},{16,20},{20,16},{24,28},{28,24},{1,5},{5... | collective-permute-start | bytes 1204232 | tf_op jit(solution)/shard_map/ppermute | solution.py:53
